TPU v7x, 32 devices: a whole 2x2x4 slice. The times are simulated.
32 devices in a mesh: patch: 4 (over z), mode: 8 (over y, x, core).
Axes of the slice: x: 2, y: 2, z: 4, core: 2. Of those that a mesh axis runs over, the one named last changes fastest.
Arguments:
- sky_map: bfloat16 [32, 8192, 64], P('patch', 'mode'), may hold values from -6 to 6
- pixel_mask: int32 [32, 8192], P('patch', 'mode'), may hold values 0 or 1
- noise_factor: float32 [32, 8, 64, 64], P('patch', 'mode'), as said below
- cycle_legendre: float32 [32, 6144, 4], P('patch', 'mode'), may hold values from -6 to 6
- band_power: float32 [6144, 4], P('mode', 'patch'), may hold values from 0.1 to 10
- channel_cov: float32 [64, 64], replicated
- test_matrix: bfloat16 [4, 6144, 2, 512], P('patch', 'mode'), may hold values from -6 to 6
Outputs:
- sketch: float32 [64, 512], P(None, ('patch', 'mode'))
Inputs may be any that keep to these rules, and one draw needn't show every extreme that they name: `noise_factor`: each noise factor is lower triangular with a positive diagonal.
All inputs are finite; a program needn't handle non-finite values. No bound on the sum of `pixel_mask` on one device may be relied on, other than what follows from the above.
Results may differ from a plain program's by a relative error of at most 0.017.
Values may be sent and summed in bfloat16 or wider, within the bound.
No kernel may reach another device: no remote copies, remote signals or barrier semaphores. Data moves between devices by JAX's collectives and lax.ppermute only.
A program may use at most 64 MiB of HBM per device.

v0:
```python
import functools
import math

import jax
import jax.numpy as jnp
import ml_dtypes
import numpy as np
from jax import lax
from jax.experimental import pallas as pl
from jax.experimental.pallas import tpu as pltpu
from jax.sharding import PartitionSpec as P

LANES = 128
MIB = 1 << 20
SUBLANES = 8
PAIR = 2


def rotate(value, step, points):
    re, im = value
    step %= points
    if step == 0:
        return re, im
    if 2 * step == points:
        return -re, -im
    if 4 * step == points:
        return im, -re
    if 8 * step == points:
        return (re + im) * math.sqrt(0.5), (im - re) * math.sqrt(0.5)
    if 8 * step == 3 * points:
        return (im - re) * math.sqrt(0.5), (re + im) * -math.sqrt(0.5)
    c, s = math.cos(2 * math.pi * step / points), math.sin(2 * math.pi * step / points)
    return re * c + im * s, im * c - re * s


def dft(values):
    n = len(values)
    if n == 1:
        return values
    half = n // 2
    even, odd = dft(values[0::2]), dft(values[1::2])
    out = [None] * n
    for b in range(half):
        re, im = rotate(odd[b], b, n)
        out[b] = even[b][0] + re, even[b][1] + im
        out[b + half] = even[b][0] - re, even[b][1] - im
    return out


def whiten_kernel(order, me_ref, sky_hbm, mask_hbm, factor_hbm, leg_hbm, sort_hbm, *refs):
    sky, mask, factor, leg, sort, white, stage, sems = refs[-8:]
    outs = refs[:-8]
    cycles, chans, pixels = sky.shape
    groups = len(outs)
    width = chans // groups
    group = max(1, SUBLANES // width)
    tall = group * width
    split = pixels // LANES
    sources, targets = (factor_hbm, sky_hbm, mask_hbm, leg_hbm, sort_hbm), (factor, sky, mask, leg, sort)
    copies = [pltpu.make_async_copy(a, b, sems.at[n]) for n, (a, b) in enumerate(zip(sources, targets))]
    for copy in copies:
        copy.start()
    copies[0].wait()
    row_of = lax.broadcasted_iota(jnp.int32, (tall, group * chans), 0) // width
    lane_of = lax.broadcasted_iota(jnp.int32, (tall, group * chans), 1) // chans
    lefts = []
    for pack in range(cycles // group):
        rows = []
        for e in range(groups):
            tile = [factor[pack * group + g, e * width : (e + 1) * width, :] for g in range(group)]
            tile = jnp.concatenate(tile, axis=0)
            rows.append(jnp.where(row_of == lane_of, jnp.concatenate([tile] * group, axis=1), 0.0))
        rows = jnp.concatenate(rows, axis=0)
        high = rows.astype(jnp.bfloat16)
        low = (rows - high.astype(jnp.float32)).astype(jnp.bfloat16)
        lefts.append((high, low))
    for copy in copies[1:3]:
        copy.wait()
    cycle_of = lax.broadcasted_iota(jnp.int32, (tall, pixels), 0) // width
    for pack in range(cycles // group):
        data = jnp.concatenate([sky[pack * group + g] for g in range(group)], axis=0)
        value = jnp.dot(lefts[pack][0], data, preferred_element_type=jnp.float32)
        value += jnp.dot(lefts[pack][1], data, preferred_element_type=jnp.float32)
        keep = jnp.broadcast_to(mask[pack * group : pack * group + 1, :], (tall, pixels))
        for g in range(1, group):
            keep = jnp.where(cycle_of < g, keep, mask[pack * group + g : pack * group + g + 1, :])
        keep = keep.astype(jnp.float32)
        for e in range(groups):
            place = (e * (cycles // group) + pack) * tall
            white[place : place + tall, :] = (value[e * tall : (e + 1) * tall] * keep).astype(jnp.bfloat16)
    copies[3].wait()
    count = cycles * width
    rows = jnp.concatenate([leg[r] for r in range(cycles)], axis=0).astype(jnp.bfloat16)
    high = rows.shape[0]
    for n in range(rows.shape[1] // LANES):
        for e in range(groups):
            place = split * count + n * high
            stage[e, place : place + high, :] = rows[:, n * LANES : (n + 1) * LANES]
    copies[4].wait()
    for pair in range(split // 2):
        wide = slice(pair * 2 * LANES, (pair + 1) * 2 * LANES)
        value = jnp.dot(white[...], sort[:, wide], preferred_element_type=jnp.float32).astype(jnp.bfloat16)
        for side in range(2):
            s = pair * 2 + side
            for e in range(groups):
                stage[e, s * count : (s + 1) * count, :] = value[
                    e * count : (e + 1) * count, side * LANES : (side + 1) * LANES
                ]
    me = me_ref[0]
    sends = [
        pltpu.make_async_copy(stage.at[jnp.bitwise_xor(me, n)], outs[slot], sems.at[5 + slot])
        for slot, n in enumerate(order)
    ]
    for send in sends:
        send.start()
    for send in sends:
        send.wait()


def modes_kernel(order, cycles, width, offsets, me_ref, twiddle_ref, table_hbm, *refs):
    slots = refs[: len(order)]
    out_ref, table, left, leg, prod_a, prod_b, x_ref, table_sems = refs[len(order) :]
    tiles = table.shape[0]
    split = twiddle_ref.shape[1]
    tall = x_ref.shape[3]
    group = tall // width
    modes = out_ref.shape[3]
    sources = len(order) // PAIR
    blocks = sources * modes // (tiles * LANES)
    per = modes // LANES
    count = cycles // PAIR * width
    high = cycles // PAIR * offsets
    me = me_ref[0]

    def copy(tile):
        return pltpu.make_async_copy(table_hbm.at[tile], table.at[tile], table_sems.at[tile])

    for tile in range(tiles):
        copy(tile).start()
    for slot, n in enumerate(order):
        q = jnp.bitwise_xor(me, n) % sources
        lanes = pl.ds(pl.multiple_of(q * LANES, LANES), LANES)
        for s in range(split):
            place = (s * PAIR + n // sources) * count
            left[place : place + count, lanes] = slots[slot][s * count : (s + 1) * count, :]
        for j in range(per):
            lanes = pl.ds(pl.multiple_of((q * per + j) * LANES, LANES), LANES)
            place = split * count + j * high
            rows = slots[slot][place : place + high, :].astype(jnp.float32)
            leg[n // sources * high : (n // sources + 1) * high, lanes] = rows

    def product(tile, prod):
        prod[...] = jnp.dot(left[...], table[tile], preferred_element_type=jnp.float32)

    def use(tile, prod):
        lanes = pl.ds(pl.multiple_of(tile * LANES, LANES), LANES)
        cosine, sine = twiddle_ref[0, :, lanes], twiddle_ref[1, :, lanes]
        cycle_of = lax.broadcasted_iota(jnp.int32, (tall, LANES), 0) // width
        for pack in range(cycles // group):
            values = []
            for s in range(split):
                place = (s * cycles + pack * group) * width
                re = prod[place : place + tall, :LANES]
                im = prod[place : place + tall, LANES:]
                if s == 0:
                    values.append((re, -im))
                else:
                    c, d = cosine[s : s + 1, :], sine[s : s + 1, :]
                    values.append((re * c - im * d, -(re * d) - im * c))
            parts = dft(values)
            for b in range(blocks):
                x_ref[b, 0, pack] = parts[b][0]
                x_ref[b, 1, pack] = parts[b][1]
        for b in range(blocks):
            mode_tile = b * tiles + tile
            d, n = mode_tile // per, mode_tile % per
            mode = pl.ds(pl.multiple_of(mode_tile * LANES, LANES), LANES)
            for k in range(offsets):
                total = [None, None]
                for pack in range(cycles // group):
                    row = None
                    for g in range(group):
                        r = pack * group + g
                        next_row = leg[r * offsets + k : r * offsets + k + 1, mode]
                        if g == 0:
                            row = jnp.broadcast_to(next_row, (tall, LANES))
                        else:
                            row = jnp.where(cycle_of < g, row, next_row)
                    for t in range(2):
                        term = row * x_ref[b, t, pack]
                        total[t] = term if pack == 0 else total[t] + term
                step = tall // 2
                while step >= width:
                    total = [value + pltpu.roll(value, step, 0) for value in total]
                    step //= 2
                if group == 1:
                    both = jnp.concatenate(total, axis=0)
                else:
                    both = jnp.where(cycle_of < 1, total[0], total[1])[: 2 * width]
                place = pl.ds(pl.multiple_of(n * LANES, LANES), LANES)
                out_ref[k, d, :, place] = both.astype(jnp.bfloat16)

    copy(0).wait()
    product(0, prod_a)

    @pl.loop(0, tiles // 2)
    def _(step):
        copy(2 * step + 1).wait()

        @pl.when(2 * step + 2 < tiles)
        def _():
            copy(2 * step + 2).wait()

        product(2 * step + 1, prod_b)
        use(2 * step, prod_a)
        product(jnp.minimum(2 * step + 2, tiles - 1), prod_a)
        use(2 * step + 1, prod_b)


def sketch_kernel(alm_ref, band_ref, cov_ref, test_ref, out_ref, left_ref):
    patches, groups, rows, lanes = alm_ref.shape
    chans = cov_ref.shape[0]
    width = rows // 2
    for low in range(PAIR):
        for g in range(groups):
            part = alm_ref[low, g].astype(jnp.float32)
            for p in range(low + PAIR, patches, PAIR):
                part += alm_ref[p, g].astype(jnp.float32)
            part = part * band_ref[...]
            place = (low * groups + g) * width
            for t in range(2):
                left_ref[t, place : place + width, :] = part[t * width : (t + 1) * width]
    sketch = None
    for t in range(2):
        term = lax.dot_general(
            test_ref[t],
            left_ref[t].astype(jnp.bfloat16),
            (((0,), (1,)), ((), ())),
            preferred_element_type=jnp.float32,
        )
        sketch = term if t == 0 else sketch + term
    mixed = lax.dot_general(
        sketch,
        cov_ref[...],
        (((1,), (1,)), ((), ())),
        precision=lax.Precision.HIGHEST,
        preferred_element_type=jnp.float32,
    )
    if out_ref.ndim == 2:
        out_ref[...] = mixed
    else:
        owners, block, _ = out_ref.shape
        fold = out_ref.shape[2] // chans
        mixed = mixed.reshape(owners, fold, block, chans)
        out_ref[...] = jnp.concatenate([mixed[:, n] for n in range(fold)], axis=-1)


def total_kernel(part_ref, out_ref):
    block, chans = part_ref.shape[1], out_ref.shape[1]
    total = jnp.sum(part_ref[...], axis=0)
    for n in range(part_ref.shape[2] // chans):
        out_ref[n * block : (n + 1) * block, :] = total[:, n * chans : (n + 1) * chans]


def call(kernel, shape, scratch, mib, spaces, *operands, out_space=pltpu.VMEM, cost=(0, 0)):
    return pl.pallas_call(
        kernel,
        out_shape=shape,
        in_specs=[pl.BlockSpec(memory_space=space) for space in spaces],
        out_specs=jax.tree.map(lambda _: pl.BlockSpec(memory_space=out_space), shape),
        scratch_shapes=scratch,
        compiler_params=pltpu.CompilerParams(vmem_limit_bytes=mib * MIB),
        cost_estimate=pl.CostEstimate(flops=cost[0], bytes_accessed=cost[1], transcendentals=0),
    )(*operands)


def transform_tables(split, cycle):
    half = cycle // split
    step = np.arange(split)[:, None] * np.arange(half)[None, :] % cycle
    angle = step * (2.0 * math.pi / cycle)
    twiddle = np.stack([np.cos(angle), np.sin(angle)]).astype(np.float32)
    step = np.arange(half)[:, None] * np.arange(half)[None, :] % half
    angle = (step * (2.0 * math.pi / half)).reshape(half, half // LANES, LANES)
    table = np.transpose(np.concatenate([np.cos(angle), np.sin(angle)], axis=2), (1, 0, 2))
    return twiddle, table.astype(ml_dtypes.bfloat16)


def sorting(pixels, split):
    place = np.arange(pixels) % split * (pixels // split) + np.arange(pixels) // split
    return (place[:, None] == np.arange(pixels)[None, :]).astype(ml_dtypes.bfloat16)


def local(sky_map, pixel_mask, noise_factor, cycle_legendre, band_power, channel_cov, test_matrix):
    cycles, pixels, chans = sky_map.shape
    modes, _ = band_power.shape
    offsets = cycle_legendre.shape[2]
    columns = test_matrix.shape[3]
    mode_count, patches = lax.axis_size("mode"), lax.axis_size("patch")
    groups = PAIR * mode_count
    width = chans // groups
    group = max(1, SUBLANES // width)
    split = pixels // LANES
    rows = split * cycles * width
    legs = cycles * offsets * (modes // LANES)
    tiles = mode_count
    blocks = modes * mode_count // (tiles * LANES)
    everyone = ("patch", "mode")
    hbm, vmem, bf16, f32, shape = pl.ANY, pltpu.VMEM, jnp.bfloat16, jnp.float32, jax.ShapeDtypeStruct

    place = lax.axis_index("patch") % PAIR * mode_count + lax.axis_index("mode")
    me = place.astype(jnp.int32).reshape(1)

    def partner(place, n):
        return (place // groups) * groups + (place % groups ^ n)

    def swap(value, n):
        pairs = [(i, partner(i, n)) for i in range(patches * mode_count)]
        return lax.ppermute(value, everyone, pairs)

    twiddle, table = transform_tables(split, pixels * mode_count)
    order = sorted(range(groups), key=lambda n: (-(n >> 1).bit_count(), n % 2 - (n < 2), -n))

    messages = call(
        functools.partial(whiten_kernel, order),
        [shape((rows + legs, LANES), bf16)] * groups,
        [
            vmem((cycles, chans, pixels), bf16),
            vmem((cycles, pixels), jnp.int32),
            vmem((cycles, chans, chans), f32),
            vmem((cycles, offsets, modes), f32),
            vmem((pixels, pixels), bf16),
            vmem((cycles * chans, pixels), bf16),
            vmem((groups, rows + legs, LANES), bf16),
            pltpu.SemaphoreType.DMA((5 + groups,)),
        ],
        56,
        [pltpu.SMEM] + [hbm] * 5,
        me,
        jnp.transpose(sky_map, (0, 2, 1)),
        pixel_mask,
        noise_factor[:, 0],
        jnp.transpose(cycle_legendre, (0, 2, 1)),
        jnp.asarray(sorting(pixels, split)),
        out_space=hbm,
        cost=(2 * cycles * chans * pixels * (pixels + 4 * chans), 8 * MIB),
    )
    slots = [messages[slot] if n == 0 else swap(messages[slot], n) for slot, n in enumerate(order)]

    alm = call(
        functools.partial(modes_kernel, order, PAIR * cycles, width, offsets),
        shape((offsets, mode_count, 2 * width, modes), bf16),
        [
            vmem((tiles, tiles * LANES, 2 * LANES), bf16),
            vmem((PAIR * rows, tiles * LANES), bf16),
            vmem((PAIR * cycles * offsets, mode_count * modes), f32),
            vmem((PAIR * rows, 2 * LANES), f32),
            vmem((PAIR * rows, 2 * LANES), f32),
            vmem((blocks, 2, PAIR * cycles // group, group * width, LANES), f32),
            pltpu.SemaphoreType.DMA((tiles,)),
        ],
        40,
        [pltpu.SMEM, vmem, hbm] + [vmem] * groups,
        me,
        jnp.asarray(twiddle),
        jnp.asarray(table),
        *slots,
        cost=(4 * PAIR * rows * (tiles * LANES) ** 2, 8 * MIB),
    )
    alm = alm.reshape(patches * mode_count, 2 * width, modes)
    alm = lax.all_to_all(alm, everyone, 0, 0, tiled=True)
    alm = alm.reshape(patches, mode_count, 2 * width, modes)

    share = columns // (patches * mode_count)
    fold = LANES // chans
    packed = share % (8 * fold) == 0
    part = call(
        sketch_kernel,
        shape((patches * mode_count, share // fold, LANES) if packed else (columns, chans), f32),
        [vmem((2, chans, modes), f32)],
        24,
        [vmem] * 4,
        alm,
        jnp.transpose(band_power),
        channel_cov,
        jnp.transpose(test_matrix[0], (1, 0, 2)),
    )
    if not packed:
        part = part.reshape(patches * mode_count, share, chans)
    part = lax.all_to_all(part, everyone, 0, 0, tiled=True)
    return jnp.transpose(call(total_kernel, shape((share, chans), f32), [], 16, [vmem], part))


def solution(mesh):
    return jax.shard_map(
        local,
        mesh=mesh,
        in_specs=(
            P("patch", "mode", None),
            P("patch", "mode"),
            P("patch", "mode", None, None),
            P("patch", "mode", None),
            P("mode", "patch"),
            P(),
            P("patch", "mode", None, None),
        ),
        out_specs=P(None, ("patch", "mode")),
        check_vma=False,
    )
```

profile of v0, /device:TPU:0, one launch (start us, length us, event | category | flops | bytes accessed | tf_op | source)
XLA Modules:
  0.0 75.5 jit_solution(400683505974297451)
XLA Ops:
  0.0 0.0 copy-start.2
  0.0 0.0 copy-start.3
  0.0 4.9 %shard_map.100 = (bf16[448,128]{1,0:T(8,128)(2,1)}, bf16[448,128]{1,0:T(8,128)(2,1)}, bf16[448,128]{1,0:T(8,128)(2,1)}, bf16[448,128]{1,0:T(8,128)(2,1)}, bf16[4...) custom-call(s32[1]{0:T(128)} %bitcast.me_ref, ...), custom_call_target="tpu_custom_call" | custom-call | flops 1342177280 | bytes 8388608 | tf_op jit(solution)/shard_map/pallas_call | solution.py:266
  5.0 5.0 %collective-permute-start = (bf16[448,128]{1,0:T(8,128)(2,1)}, bf16[448,128]{1,0:T(8,128)(2,1)S(1)}, u32[]{:S(2)}, u32[]{:S(2)}) collective-permute-start(bf16[448,128]{1,0:T(8,128)(2,1)} %get-tuple-element.21), channel_id=1, source_target_pairs={{0,14},{1,15},{2,12},{3,13},{4,10},{5,11},{6,8},{7,9},{8,6},{9,7},... | collective-permute-start | bytes 344072 | tf_op jit(solution)/shard_map/ppermute | solution.py:318
  9.9 0.0 collective-permute-start.1
  9.9 1.0 %collective-permute-start.10 = (bf16[448,128]{1,0:T(8,128)(2,1)}, bf16[448,128]{1,0:T(8,128)(2,1)S(1)}, u32[]{:S(2)}, u32[]{:S(2)}) collective-permute-start(bf16[448,128]{1,0:T(8,128)(2,1)} %get-tuple-element.31), channel_id=1, source_target_pairs={{0,2},{1,3},{2,0},{3,1},{4,6},{5,7},{6,4},{7,5},{8,10},{9,11},{10,... | collective-permute-start | bytes 344072 | tf_op jit(solution)/shard_map/ppermute | solution.py:318
  10.9 1.9 %collective-permute-start.11 = (bf16[448,128]{1,0:T(8,128)(2,1)}, bf16[448,128]{1,0:T(8,128)(2,1)S(1)}, u32[]{:S(2)}, u32[]{:S(2)}) collective-permute-start(bf16[448,128]{1,0:T(8,128)(2,1)} %get-tuple-element.32), channel_id=1, source_target_pairs={{0,9},{1,8},{2,11},{3,10},{4,13},{5,12},{6,15},{7,14},{8,1},{9,0},... | collective-permute-start | bytes 344072 | tf_op jit(solution)/shard_map/ppermute | solution.py:318
  12.8 1.0 %collective-permute-start.12 = (bf16[448,128]{1,0:T(8,128)(2,1)}, bf16[448,128]{1,0:T(8,128)(2,1)S(1)}, u32[]{:S(2)}, u32[]{:S(2)}) collective-permute-start(bf16[448,128]{1,0:T(8,128)(2,1)} %get-tuple-element.33), channel_id=1, source_target_pairs={{0,5},{1,4},{2,7},{3,6},{4,1},{5,0},{6,3},{7,2},{8,13},{9,12},{10,... | collective-permute-start | bytes 344072 | tf_op jit(solution)/shard_map/ppermute | solution.py:318
  13.8 0.0 collective-permute-done.refs_0_
  13.8 0.8 %collective-permute-start.13 = (bf16[448,128]{1,0:T(8,128)(2,1)}, bf16[448,128]{1,0:T(8,128)(2,1)S(1)}, u32[]{:S(2)}, u32[]{:S(2)}) collective-permute-start(bf16[448,128]{1,0:T(8,128)(2,1)} %get-tuple-element.34), channel_id=1, source_target_pairs={{0,3},{1,2},{2,1},{3,0},{4,7},{5,6},{6,5},{7,4},{8,11},{9,10},{10,... | collective-permute-start | bytes 344072 | tf_op jit(solution)/shard_map/ppermute | solution.py:318
  14.6 2.8 %collective-permute-done.1.refs_1_ = bf16[448,128]{1,0:T(8,128)(2,1)S(1)} collective-permute-done((bf16[448,128]{1,0:T(8,128)(2,1)}, bf16[448,128]{1,0:T(8,128)(2,1)S(1)}, u32[]{:S(2)}, u32[]{:S(2)}) %collective-permute-start.1) | collective-permute-done | bytes 114720 | tf_op jit(solution)/shard_map/ppermute | solution.py:318
  17.4 0.0 collective-permute-start.14
  17.4 1.2 %collective-permute-done.10.refs_10_ = bf16[448,128]{1,0:T(8,128)(2,1)S(1)} collective-permute-done((bf16[448,128]{1,0:T(8,128)(2,1)}, bf16[448,128]{1,0:T(8,128)(2,1)S(1)}, u32[]{:S(2)}, u32[]{:S(2)}) %collective-permute-start.10) | collective-permute-done | bytes 114720 | tf_op jit(solution)/shard_map/ppermute | solution.py:318
  18.6 1.4 %collective-permute-start.2 = (bf16[448,128]{1,0:T(8,128)(2,1)}, bf16[448,128]{1,0:T(8,128)(2,1)S(1)}, u32[]{:S(2)}, u32[]{:S(2)}) collective-permute-start(bf16[448,128]{1,0:T(8,128)(2,1)} %get-tuple-element.23), channel_id=1, source_target_pairs={{0,12},{1,13},{2,14},{3,15},{4,8},{5,9},{6,10},{7,11},{8,4},{9,5},... | collective-permute-start | bytes 344072 | tf_op jit(solution)/shard_map/ppermute | solution.py:318
  20.0 0.0 collective-permute-done.11.refs_11_
  20.0 1.6 %collective-permute-start.3 = (bf16[448,128]{1,0:T(8,128)(2,1)}, bf16[448,128]{1,0:T(8,128)(2,1)S(1)}, u32[]{:S(2)}, u32[]{:S(2)}) collective-permute-start(bf16[448,128]{1,0:T(8,128)(2,1)} %get-tuple-element.24), channel_id=1, source_target_pairs={{0,10},{1,11},{2,8},{3,9},{4,14},{5,15},{6,12},{7,13},{8,2},{9,3},... | collective-permute-start | bytes 344072 | tf_op jit(solution)/shard_map/ppermute | solution.py:318
  21.6 0.0 collective-permute-done.12.refs_12_
  21.6 1.4 %collective-permute-start.4 = (bf16[448,128]{1,0:T(8,128)(2,1)}, bf16[448,128]{1,0:T(8,128)(2,1)S(1)}, u32[]{:S(2)}, u32[]{:S(2)}) collective-permute-start(bf16[448,128]{1,0:T(8,128)(2,1)} %get-tuple-element.25), channel_id=1, source_target_pairs={{0,6},{1,7},{2,4},{3,5},{4,2},{5,3},{6,0},{7,1},{8,14},{9,15},{10,... | collective-permute-start | bytes 344072 | tf_op jit(solution)/shard_map/ppermute | solution.py:318
  23.0 0.0 collective-permute-done.13.refs_13_
  23.0 0.3 collective-permute-start.5
  23.3 0.0 collective-permute-done.14.refs_15_
  23.3 2.4 %collective-permute-start.6 = (bf16[448,128]{1,0:T(8,128)(2,1)}, bf16[448,128]{1,0:T(8,128)(2,1)S(1)}, u32[]{:S(2)}, u32[]{:S(2)}) collective-permute-start(bf16[448,128]{1,0:T(8,128)(2,1)} %get-tuple-element.27), channel_id=1, source_target_pairs={{0,11},{1,10},{2,9},{3,8},{4,15},{5,14},{6,13},{7,12},{8,3},{9,2},... | collective-permute-start | bytes 344072 | tf_op jit(solution)/shard_map/ppermute | solution.py:318
  25.7 0.0 collective-permute-done.2.refs_2_
  25.7 0.8 %collective-permute-start.7 = (bf16[448,128]{1,0:T(8,128)(2,1)}, bf16[448,128]{1,0:T(8,128)(2,1)S(1)}, u32[]{:S(2)}, u32[]{:S(2)}) collective-permute-start(bf16[448,128]{1,0:T(8,128)(2,1)} %get-tuple-element.28), channel_id=1, source_target_pairs={{0,7},{1,6},{2,5},{3,4},{4,3},{5,2},{6,1},{7,0},{8,15},{9,14},{10,... | collective-permute-start | bytes 344072 | tf_op jit(solution)/shard_map/ppermute | solution.py:318
  26.5 1.1 %collective-permute-done.3.refs_3_ = bf16[448,128]{1,0:T(8,128)(2,1)S(1)} collective-permute-done((bf16[448,128]{1,0:T(8,128)(2,1)}, bf16[448,128]{1,0:T(8,128)(2,1)S(1)}, u32[]{:S(2)}, u32[]{:S(2)}) %collective-permute-start.3) | collective-permute-done | bytes 114720 | tf_op jit(solution)/shard_map/ppermute | solution.py:318
  27.6 1.2 %collective-permute-start.8 = (bf16[448,128]{1,0:T(8,128)(2,1)}, bf16[448,128]{1,0:T(8,128)(2,1)S(1)}, u32[]{:S(2)}, u32[]{:S(2)}) collective-permute-start(bf16[448,128]{1,0:T(8,128)(2,1)} %get-tuple-element.29), channel_id=1, source_target_pairs={{0,8},{1,9},{2,10},{3,11},{4,12},{5,13},{6,14},{7,15},{8,0},{9,1},... | collective-permute-start | bytes 344072 | tf_op jit(solution)/shard_map/ppermute | solution.py:318
  28.9 2.4 %collective-permute-done.4.refs_4_ = bf16[448,128]{1,0:T(8,128)(2,1)S(1)} collective-permute-done((bf16[448,128]{1,0:T(8,128)(2,1)}, bf16[448,128]{1,0:T(8,128)(2,1)S(1)}, u32[]{:S(2)}, u32[]{:S(2)}) %collective-permute-start.4) | collective-permute-done | bytes 114720 | tf_op jit(solution)/shard_map/ppermute | solution.py:318
  31.3 1.5 %collective-permute-start.9 = (bf16[448,128]{1,0:T(8,128)(2,1)}, bf16[448,128]{1,0:T(8,128)(2,1)S(1)}, u32[]{:S(2)}, u32[]{:S(2)}) collective-permute-start(bf16[448,128]{1,0:T(8,128)(2,1)} %get-tuple-element.30), channel_id=1, source_target_pairs={{0,4},{1,5},{2,6},{3,7},{4,0},{5,1},{6,2},{7,3},{8,12},{9,13},{10,... | collective-permute-start | bytes 344072 | tf_op jit(solution)/shard_map/ppermute | solution.py:318
  32.8 0.0 collective-permute-done.5.refs_5_
  32.8 0.1 collective-permute-done.6.refs_6_
  32.9 2.7 %collective-permute-done.7.refs_7_ = bf16[448,128]{1,0:T(8,128)(2,1)S(1)} collective-permute-done((bf16[448,128]{1,0:T(8,128)(2,1)}, bf16[448,128]{1,0:T(8,128)(2,1)S(1)}, u32[]{:S(2)}, u32[]{:S(2)}) %collective-permute-start.7) | collective-permute-done | bytes 114720 | tf_op jit(solution)/shard_map/ppermute | solution.py:318
  35.7 0.0 collective-permute-done.8.refs_8_
  35.7 1.3 %collective-permute-done.9.refs_9_ = bf16[448,128]{1,0:T(8,128)(2,1)S(1)} collective-permute-done((bf16[448,128]{1,0:T(8,128)(2,1)}, bf16[448,128]{1,0:T(8,128)(2,1)S(1)}, u32[]{:S(2)}, u32[]{:S(2)}) %collective-permute-start.9) | collective-permute-done | bytes 114720 | tf_op jit(solution)/shard_map/ppermute | solution.py:318
  37.0 0.0 copy-done.2
  37.0 0.0 copy-done.3
  37.0 0.0 copy-start.4
  37.0 0.9 %copy-done.4 = bf16[448,128]{1,0:T(8,128)(2,1)S(1)} copy-done((bf16[448,128]{1,0:T(8,128)(2,1)S(1)}, bf16[448,128]{1,0:T(8,128)(2,1)}, u32[]{:S(2)}) %copy-start.4) | copy-done | bytes 114712
  37.9 6.8 %shard_map.101 = bf16[4,8,8,768]{3,2,1,0:T(8,128)(2,1)} custom-call(s32[1]{0:T(128)} %bitcast.me_ref, f32[2,8,1024]{2,1,0:T(8,128)S(1)} %copy-done.3, bf16[8,1024,256]{2,1,0:T(8,128)(2,1)S(1)} %copy-done.2, bf16[448,128]{1,0:T(8,128)(2,1)S(1)} %collective-permute-done.refs_0_, bf16[448,128]{1,0:T(8,128)(2,1)S(1)} %collective-permute-done.1.refs_1_, ...), custom_call_target="tpu_custom_call" | custom-call | flops 2147483648 | bytes 8388608 | tf_op jit(solution)/shard_map/pallas_call | solution.py:266
  44.7 0.0 copy-start
  44.7 0.0 copy-start.1
  44.7 4.9 %all-to-all-start = ((bf16[32,8,768]{2,1,0:T(8,128)(2,1)}), bf16[32,8,768]{2,1,0:T(8,128)(2,1)S(1)}, u32[]{:S(2)}, u32[]{:S(2)}) async-start(bf16[32,8,768]{2,1,0:T(8,128)(2,1)} %bitcast.4), calls=%async_computation | async-start | bytes 786432 | tf_op jit(solution)/shard_map/all_to_all | solution.py:370
  49.6 1.7 %copy.13 = bf16[1,768,2,512]{3,1,2,0:T(8,128)(2,1)S(1)} copy(bf16[1,768,2,512]{3,2,1,0:T(2,128)(2,1)} %param.16) | data formatting | bytes 3145728 | tf_op args[6]
  51.2 11.5 %all-to-all-done = bf16[32,8,768]{2,1,0:T(8,128)(2,1)S(1)} async-done(((bf16[32,8,768]{2,1,0:T(8,128)(2,1)}), bf16[32,8,768]{2,1,0:T(8,128)(2,1)S(1)}, u32[]{:S(2)}, u32[]{:S(2)}) %all-to-all-start) | async-done | bytes 393248 | tf_op jit(solution)/shard_map/all_to_all | solution.py:370
  62.8 0.0 copy-done
  62.8 0.0 copy-done.1
  62.8 1.3 %shard_map.102 = f32[32,8,128]{2,1,0:T(8,128)S(1)} custom-call(bf16[4,8,8,768]{3,2,1,0:T(8,128)(2,1)S(1)} %bitcast.14, f32[1,768]{1,0:T(1,128)S(1)} %bitcast.15, f32[64,64]{1,0:T(8,128)S(1)} %copy-done, bf16[2,768,512]{2,1,0:T(8,128)(2,1)S(1)} %bitcast.13), custom_call_target="tpu_custom_call" | custom-call | tf_op jit(solution)/shard_map/pallas_call | solution.py:266
  64.1 10.7 %all_to_all.10.part_ref = f32[32,8,128]{2,1,0:T(8,128)S(1)} all-to-all(f32[32,8,128]{2,1,0:T(8,128)S(1)} %shard_map.102), channel_id=1, replica_groups=mesh['patch'=4,'mode'=8] {'patch','mode'}, dimensions={0} | all-to-all | bytes 262144 | tf_op jit(solution)/shard_map/all_to_all | solution.py:389
  74.8 0.7 shard_map.103
Async XLA Ops:
  0.0 37.0 %copy-start.2 = (bf16[8,1024,256]{2,1,0:T(8,128)(2,1)S(1)}, bf16[8,1024,256]{2,1,0:T(8,128)(2,1)}, u32[]{:S(2)}) copy-start(bf16[8,1024,256]{2,1,0:T(8,128)(2,1)} %constant.31.clone.table_hbm) | copy-start | bytes 12582916
  0.0 37.0 %copy-start.3 = (f32[2,8,1024]{2,1,0:T(8,128)S(1)}, f32[2,8,1024]{2,1,0:T(8,128)}, u32[]{:S(2)}) copy-start(f32[2,8,1024]{2,1,0:T(8,128)} %constant.30.clone.twiddle_ref) | copy-start | bytes 196612
  5.0 8.8 %collective-permute-start = (bf16[448,128]{1,0:T(8,128)(2,1)}, bf16[448,128]{1,0:T(8,128)(2,1)S(1)}, u32[]{:S(2)}, u32[]{:S(2)}) collective-permute-start(bf16[448,128]{1,0:T(8,128)(2,1)} %get-tuple-element.21), channel_id=1, source_target_pairs={{0,14},{1,15},{2,12},{3,13},{4,10},{5,11},{6,8},{7,9},{8,6},{9,7},... | collective-permute-start | bytes 344072 | tf_op jit(solution)/shard_map/ppermute | solution.py:318
  9.9 7.5 %collective-permute-start.1 = (bf16[448,128]{1,0:T(8,128)(2,1)}, bf16[448,128]{1,0:T(8,128)(2,1)S(1)}, u32[]{:S(2)}, u32[]{:S(2)}) collective-permute-start(bf16[448,128]{1,0:T(8,128)(2,1)} %get-tuple-element.22), channel_id=1, source_target_pairs={{0,15},{1,14},{2,13},{3,12},{4,11},{5,10},{6,9},{7,8},{8,7},{9,6},... | collective-permute-start | bytes 344072 | tf_op jit(solution)/shard_map/ppermute | solution.py:318
  9.9 8.7 %collective-permute-start.10 = (bf16[448,128]{1,0:T(8,128)(2,1)}, bf16[448,128]{1,0:T(8,128)(2,1)S(1)}, u32[]{:S(2)}, u32[]{:S(2)}) collective-permute-start(bf16[448,128]{1,0:T(8,128)(2,1)} %get-tuple-element.31), channel_id=1, source_target_pairs={{0,2},{1,3},{2,0},{3,1},{4,6},{5,7},{6,4},{7,5},{8,10},{9,11},{10,... | collective-permute-start | bytes 344072 | tf_op jit(solution)/shard_map/ppermute | solution.py:318
  10.9 9.1 %collective-permute-start.11 = (bf16[448,128]{1,0:T(8,128)(2,1)}, bf16[448,128]{1,0:T(8,128)(2,1)S(1)}, u32[]{:S(2)}, u32[]{:S(2)}) collective-permute-start(bf16[448,128]{1,0:T(8,128)(2,1)} %get-tuple-element.32), channel_id=1, source_target_pairs={{0,9},{1,8},{2,11},{3,10},{4,13},{5,12},{6,15},{7,14},{8,1},{9,0},... | collective-permute-start | bytes 344072 | tf_op jit(solution)/shard_map/ppermute | solution.py:318
  12.8 8.8 %collective-permute-start.12 = (bf16[448,128]{1,0:T(8,128)(2,1)}, bf16[448,128]{1,0:T(8,128)(2,1)S(1)}, u32[]{:S(2)}, u32[]{:S(2)}) collective-permute-start(bf16[448,128]{1,0:T(8,128)(2,1)} %get-tuple-element.33), channel_id=1, source_target_pairs={{0,5},{1,4},{2,7},{3,6},{4,1},{5,0},{6,3},{7,2},{8,13},{9,12},{10,... | collective-permute-start | bytes 344072 | tf_op jit(solution)/shard_map/ppermute | solution.py:318
  13.8 9.2 %collective-permute-start.13 = (bf16[448,128]{1,0:T(8,128)(2,1)}, bf16[448,128]{1,0:T(8,128)(2,1)S(1)}, u32[]{:S(2)}, u32[]{:S(2)}) collective-permute-start(bf16[448,128]{1,0:T(8,128)(2,1)} %get-tuple-element.34), channel_id=1, source_target_pairs={{0,3},{1,2},{2,1},{3,0},{4,7},{5,6},{6,5},{7,4},{8,11},{9,10},{10,... | collective-permute-start | bytes 344072 | tf_op jit(solution)/shard_map/ppermute | solution.py:318
  17.4 5.9 %collective-permute-start.14 = (bf16[448,128]{1,0:T(8,128)(2,1)}, bf16[448,128]{1,0:T(8,128)(2,1)S(1)}, u32[]{:S(2)}, u32[]{:S(2)}) collective-permute-start(bf16[448,128]{1,0:T(8,128)(2,1)} %get-tuple-element.36), channel_id=1, source_target_pairs={{0,1},{1,0},{2,3},{3,2},{4,5},{5,4},{6,7},{7,6},{8,9},{9,8},{10,11... | collective-permute-start | bytes 344072 | tf_op jit(solution)/shard_map/ppermute | solution.py:318
  18.6 7.1 %collective-permute-start.2 = (bf16[448,128]{1,0:T(8,128)(2,1)}, bf16[448,128]{1,0:T(8,128)(2,1)S(1)}, u32[]{:S(2)}, u32[]{:S(2)}) collective-permute-start(bf16[448,128]{1,0:T(8,128)(2,1)} %get-tuple-element.23), channel_id=1, source_target_pairs={{0,12},{1,13},{2,14},{3,15},{4,8},{5,9},{6,10},{7,11},{8,4},{9,5},... | collective-permute-start | bytes 344072 | tf_op jit(solution)/shard_map/ppermute | solution.py:318
  20.0 7.6 %collective-permute-start.3 = (bf16[448,128]{1,0:T(8,128)(2,1)}, bf16[448,128]{1,0:T(8,128)(2,1)S(1)}, u32[]{:S(2)}, u32[]{:S(2)}) collective-permute-start(bf16[448,128]{1,0:T(8,128)(2,1)} %get-tuple-element.24), channel_id=1, source_target_pairs={{0,10},{1,11},{2,8},{3,9},{4,14},{5,15},{6,12},{7,13},{8,2},{9,3},... | collective-permute-start | bytes 344072 | tf_op jit(solution)/shard_map/ppermute | solution.py:318
  21.6 9.7 %collective-permute-start.4 = (bf16[448,128]{1,0:T(8,128)(2,1)}, bf16[448,128]{1,0:T(8,128)(2,1)S(1)}, u32[]{:S(2)}, u32[]{:S(2)}) collective-permute-start(bf16[448,128]{1,0:T(8,128)(2,1)} %get-tuple-element.25), channel_id=1, source_target_pairs={{0,6},{1,7},{2,4},{3,5},{4,2},{5,3},{6,0},{7,1},{8,14},{9,15},{10,... | collective-permute-start | bytes 344072 | tf_op jit(solution)/shard_map/ppermute | solution.py:318
  23.0 9.8 %collective-permute-start.5 = (bf16[448,128]{1,0:T(8,128)(2,1)}, bf16[448,128]{1,0:T(8,128)(2,1)S(1)}, u32[]{:S(2)}, u32[]{:S(2)}) collective-permute-start(bf16[448,128]{1,0:T(8,128)(2,1)} %get-tuple-element.26), channel_id=1, source_target_pairs={{0,13},{1,12},{2,15},{3,14},{4,9},{5,8},{6,11},{7,10},{8,5},{9,4},... | collective-permute-start | bytes 344072 | tf_op jit(solution)/shard_map/ppermute | solution.py:318
  23.3 9.6 %collective-permute-start.6 = (bf16[448,128]{1,0:T(8,128)(2,1)}, bf16[448,128]{1,0:T(8,128)(2,1)S(1)}, u32[]{:S(2)}, u32[]{:S(2)}) collective-permute-start(bf16[448,128]{1,0:T(8,128)(2,1)} %get-tuple-element.27), channel_id=1, source_target_pairs={{0,11},{1,10},{2,9},{3,8},{4,15},{5,14},{6,13},{7,12},{8,3},{9,2},... | collective-permute-start | bytes 344072 | tf_op jit(solution)/shard_map/ppermute | solution.py:318
  25.7 10.0 %collective-permute-start.7 = (bf16[448,128]{1,0:T(8,128)(2,1)}, bf16[448,128]{1,0:T(8,128)(2,1)S(1)}, u32[]{:S(2)}, u32[]{:S(2)}) collective-permute-start(bf16[448,128]{1,0:T(8,128)(2,1)} %get-tuple-element.28), channel_id=1, source_target_pairs={{0,7},{1,6},{2,5},{3,4},{4,3},{5,2},{6,1},{7,0},{8,15},{9,14},{10,... | collective-permute-start | bytes 344072 | tf_op jit(solution)/shard_map/ppermute | solution.py:318
  27.6 8.0 %collective-permute-start.8 = (bf16[448,128]{1,0:T(8,128)(2,1)}, bf16[448,128]{1,0:T(8,128)(2,1)S(1)}, u32[]{:S(2)}, u32[]{:S(2)}) collective-permute-start(bf16[448,128]{1,0:T(8,128)(2,1)} %get-tuple-element.29), channel_id=1, source_target_pairs={{0,8},{1,9},{2,10},{3,11},{4,12},{5,13},{6,14},{7,15},{8,0},{9,1},... | collective-permute-start | bytes 344072 | tf_op jit(solution)/shard_map/ppermute | solution.py:318
  31.3 5.8 %collective-permute-start.9 = (bf16[448,128]{1,0:T(8,128)(2,1)}, bf16[448,128]{1,0:T(8,128)(2,1)S(1)}, u32[]{:S(2)}, u32[]{:S(2)}) collective-permute-start(bf16[448,128]{1,0:T(8,128)(2,1)} %get-tuple-element.30), channel_id=1, source_target_pairs={{0,4},{1,5},{2,6},{3,7},{4,0},{5,1},{6,2},{7,3},{8,12},{9,13},{10,... | collective-permute-start | bytes 344072 | tf_op jit(solution)/shard_map/ppermute | solution.py:318
  37.0 0.9 %copy-start.4 = (bf16[448,128]{1,0:T(8,128)(2,1)S(1)}, bf16[448,128]{1,0:T(8,128)(2,1)}, u32[]{:S(2)}) copy-start(bf16[448,128]{1,0:T(8,128)(2,1)} %get-tuple-element.35.refs_14_) | copy-start | bytes 344068
  44.7 18.1 %copy-start = (f32[64,64]{1,0:T(8,128)S(1)}, f32[64,64]{1,0:T(8,128)}, u32[]{:S(2)}) copy-start(f32[64,64]{1,0:T(8,128)} %cov_ref.1) | copy-start | bytes 49156
  44.7 18.1 %copy-start.1 = (f32[768,1]{0,1:T(1,128)S(1)}, f32[768,1]{0,1:T(1,128)}, u32[]{:S(2)}) copy-start(f32[768,1]{0,1:T(1,128)} %param.14) | copy-start | bytes 9220
  44.7 18.1 %all-to-all-start = ((bf16[32,8,768]{2,1,0:T(8,128)(2,1)}), bf16[32,8,768]{2,1,0:T(8,128)(2,1)S(1)}, u32[]{:S(2)}, u32[]{:S(2)}) async-start(bf16[32,8,768]{2,1,0:T(8,128)(2,1)} %bitcast.4), calls=%async_computation | async-start | bytes 786432 | tf_op jit(solution)/shard_map/all_to_all | solution.py:370
where the time goes:
time: 75.8 us; the launch traced here: 75.5 us
  starting transfers between devices  25.1 us (33%)
  waiting for transfers between devices  23.3 us (31%)
  Pallas kernels  13.7 us (18%)
  blocking collectives  10.7 us (14%)
  local copies, waits for them, and re-layouts  2.58 us (3%)
    ppermute x15, starting transfers between devices, swap(): return lax.ppermute(value, everyone, pairs)  20.2 us
    pallas_call x4, Pallas kernels, call(): pl.pallas_call(kernel, out_shape=shape, in_specs=[pl.BlockSpec(memory_spa...  13.7 us
    ppermute x15, waiting for transfers between devices, swap(): return lax.ppermute(value, everyone, pairs)  11.8 us
    all_to_all x1, waiting for transfers between devices, local(): alm = lax.all_to_all(alm, everyone, 0, 0, tiled=True)  11.5 us
    all_to_all x1, blocking collectives, local(): part = lax.all_to_all(part, everyone, 0, 0, tiled=True)  10.7 us
    all_to_all x1, starting transfers between devices, local(): alm = lax.all_to_all(alm, everyone, 0, 0, tiled=True)  4.87 us
    unnamed x11, local copies, waits for them, and re-layouts  2.58 us
  transfers between devices with their start and end apart: 16, of which 8 were waited for; matrix products, arithmetic and copies ran while one was open for 2% of the time, Pallas kernels for 0%

commit v1 on v0

--- a/solution.py
+++ b/solution.py
@@ -13,7 +13,7 @@
 LANES = 128
 MIB = 1 << 20
 SUBLANES = 8
-PAIR = 2
+PAIR = 1
 
 
 def rotate(value, step, points):
@@ -58,9 +58,11 @@
     split = pixels // LANES
     sources, targets = (factor_hbm, sky_hbm, mask_hbm, leg_hbm, sort_hbm), (factor, sky, mask, leg, sort)
     copies = [pltpu.make_async_copy(a, b, sems.at[n]) for n, (a, b) in enumerate(zip(sources, targets))]
-    for copy in copies:
+    for copy in copies[:3]:
         copy.start()
     copies[0].wait()
+    copies[3].start()
+    copies[4].start()
     row_of = lax.broadcasted_iota(jnp.int32, (tall, group * chans), 0) // width
     lane_of = lax.broadcasted_iota(jnp.int32, (tall, group * chans), 1) // chans
     lefts = []
@@ -73,14 +75,13 @@
         rows = jnp.concatenate(rows, axis=0)
         high = rows.astype(jnp.bfloat16)
         low = (rows - high.astype(jnp.float32)).astype(jnp.bfloat16)
-        lefts.append((high, low))
+        lefts.append(jnp.concatenate([high, low], axis=1))
     for copy in copies[1:3]:
         copy.wait()
     cycle_of = lax.broadcasted_iota(jnp.int32, (tall, pixels), 0) // width
     for pack in range(cycles // group):
-        data = jnp.concatenate([sky[pack * group + g] for g in range(group)], axis=0)
-        value = jnp.dot(lefts[pack][0], data, preferred_element_type=jnp.float32)
-        value += jnp.dot(lefts[pack][1], data, preferred_element_type=jnp.float32)
+        data = jnp.concatenate([sky[pack * group + g] for g in range(group)] * 2, axis=0)
+        value = jnp.dot(lefts[pack], data, preferred_element_type=jnp.float32)
         keep = jnp.broadcast_to(mask[pack * group : pack * group + 1, :], (tall, pixels))
         for g in range(1, group):
             keep = jnp.where(cycle_of < g, keep, mask[pack * group + g : pack * group + g + 1, :])
@@ -119,7 +120,7 @@
 
 def modes_kernel(order, cycles, width, offsets, me_ref, twiddle_ref, table_hbm, *refs):
     slots = refs[: len(order)]
-    out_ref, table, left, leg, prod_a, prod_b, x_ref, table_sems = refs[len(order) :]
+    out_hbm, table, left, leg, prod_a, prod_b, x_ref, out_ref, table_sems, out_sems = refs[len(order) :]
     tiles = table.shape[0]
     split = twiddle_ref.shape[1]
     tall = x_ref.shape[3]
@@ -135,22 +136,35 @@
     def copy(tile):
         return pltpu.make_async_copy(table_hbm.at[tile], table.at[tile], table_sems.at[tile])
 
-    for tile in range(tiles):
-        copy(tile).start()
+    def store(step, n):
+        mode_tile = n // 2 * tiles + 2 * step + n % 2
+        lanes = pl.ds(pl.multiple_of(mode_tile % per * LANES, LANES), LANES)
+        where = (slice(None), mode_tile // per, slice(None), lanes)
+        return pltpu.make_async_copy(out_ref.at[where], out_hbm.at[where], out_sems.at[step, n])
+
+    copy(0).start()
+    copy(1).start()
     for slot, n in enumerate(order):
         q = jnp.bitwise_xor(me, n) % sources
         lanes = pl.ds(pl.multiple_of(q * LANES, LANES), LANES)
         for s in range(split):
             place = (s * PAIR + n // sources) * count
             left[place : place + count, lanes] = slots[slot][s * count : (s + 1) * count, :]
+    for tile in range(2, tiles):
+        copy(tile).start()
+
+    def product(tile, prod):
+        prod[...] = jnp.dot(left[...], table[tile], preferred_element_type=jnp.float32)
+
+    copy(0).wait()
+    product(0, prod_a)
+    for slot, n in enumerate(order):
+        q = jnp.bitwise_xor(me, n) % sources
         for j in range(per):
             lanes = pl.ds(pl.multiple_of((q * per + j) * LANES, LANES), LANES)
             place = split * count + j * high
             rows = slots[slot][place : place + high, :].astype(jnp.float32)
             leg[n // sources * high : (n // sources + 1) * high, lanes] = rows
-
-    def product(tile, prod):
-        prod[...] = jnp.dot(left[...], table[tile], preferred_element_type=jnp.float32)
 
     def use(tile, prod):
         lanes = pl.ds(pl.multiple_of(tile * LANES, LANES), LANES)
@@ -200,9 +214,6 @@
                 place = pl.ds(pl.multiple_of(n * LANES, LANES), LANES)
                 out_ref[k, d, :, place] = both.astype(jnp.bfloat16)
 
-    copy(0).wait()
-    product(0, prod_a)
-
     @pl.loop(0, tiles // 2)
     def _(step):
         copy(2 * step + 1).wait()
@@ -215,6 +226,13 @@
         use(2 * step, prod_a)
         product(jnp.minimum(2 * step + 2, tiles - 1), prod_a)
         use(2 * step + 1, prod_b)
+        for n in range(2 * blocks):
+            store(step, n).start()
+
+    @pl.loop(0, tiles // 2)
+    def _(step):
+        for n in range(2 * blocks):
+            store(step, n).wait()
 
 
 def sketch_kernel(alm_ref, band_ref, cov_ref, test_ref, out_ref, left_ref):
@@ -356,7 +374,9 @@
             vmem((PAIR * rows, 2 * LANES), f32),
             vmem((PAIR * rows, 2 * LANES), f32),
             vmem((blocks, 2, PAIR * cycles // group, group * width, LANES), f32),
+            vmem((offsets, mode_count, 2 * width, modes), bf16),
             pltpu.SemaphoreType.DMA((tiles,)),
+            pltpu.SemaphoreType.DMA((tiles // 2, 2 * blocks)),
         ],
         40,
         [pltpu.SMEM, vmem, hbm] + [vmem] * groups,
@@ -364,6 +384,7 @@
         jnp.asarray(twiddle),
         jnp.asarray(table),
         *slots,
+        out_space=hbm,
         cost=(4 * PAIR * rows * (tiles * LANES) ** 2, 8 * MIB),
     )
     alm = alm.reshape(patches * mode_count, 2 * width, modes)

time: 75.8 us -> 74.6 us (0.984)
  starting transfers between devices: 25.1 us -> 13.3 us
  waiting for transfers between devices: 23.3 us -> 32.1 us
  blocking collectives: 10.7 us -> 11.7 us
  Pallas kernels: 13.7 us -> 14.6 us
    ppermute x15 -> x7, starting transfers between devices: 20.2 us -> 7.15 us  [swap(): return lax.ppermute(value, everyone, pairs)]
    all_to_all x1, waiting for transfers between devices: 11.5 us -> 19 us  [local(): alm = lax.all_to_all(alm, everyone, 0, 0, tiled=True)]
    ppermute x15 -> x7, waiting for transfers between devices: 11.8 us -> 13.1 us  [swap(): return lax.ppermute(value, everyone, pairs)]
    all_to_all x1, starting transfers between devices: 4.87 us -> 6.11 us  [local(): alm = lax.all_to_all(alm, everyone, 0, 0, tiled=True)]
    all_to_all x1, blocking collectives: 10.7 us -> 11.7 us  [local(): part = lax.all_to_all(part, everyone, 0, 0, tiled=True)]
    pallas_call x4, Pallas kernels: 13.7 us -> 14.6 us  [call(): pl.pallas_call(kernel, out_shape=shape, in_specs=[pl.BlockSpec(memory_spa...]
  transfers between devices with their start and end apart: 16 -> 8, of which waited for: 8 -> 6; matrix products, arithmetic and copies ran while one was open for 2% -> 2% of each run, Pallas kernels for 0% -> 0%
where the time goes in v1:
time: 74.6 us; the launch traced here: 74.3 us
  waiting for transfers between devices  32.1 us (43%)
  Pallas kernels  14.6 us (20%)
  starting transfers between devices  13.3 us (18%)
  blocking collectives  11.7 us (16%)
  local copies, waits for them, and re-layouts  2.59 us (3%)
    all_to_all x1, waiting for transfers between devices, local(): alm = lax.all_to_all(alm, everyone, 0, 0, tiled=True)  19 us
    pallas_call x4, Pallas kernels, call(): pl.pallas_call(kernel, out_shape=shape, in_specs=[pl.BlockSpec(memory_spa...  14.6 us
    ppermute x7, waiting for transfers between devices, swap(): return lax.ppermute(value, everyone, pairs)  13.1 us
    all_to_all x1, blocking collectives, local(): part = lax.all_to_all(part, everyone, 0, 0, tiled=True)  11.7 us
    ppermute x7, starting transfers between devices, swap(): return lax.ppermute(value, everyone, pairs)  7.15 us
    all_to_all x1, starting transfers between devices, local(): alm = lax.all_to_all(alm, everyone, 0, 0, tiled=True)  6.11 us
    unnamed x11, local copies, waits for them, and re-layouts  2.59 us
  transfers between devices with their start and end apart: 8, of which 6 were waited for; matrix products, arithmetic and copies ran while one was open for 2% of the time, Pallas kernels for 0%

profile of v1, /device:TPU:0, one launch (start us, length us, event | category | flops | bytes accessed | tf_op | source)
XLA Modules:
  0.0 74.3 jit_solution(13759136583805980937)
XLA Ops:
  0.0 0.0 copy-start.2
  0.0 0.0 copy-start.3
  0.0 5.8 %shard_map.100 = (bf16[704,128]{1,0:T(8,128)(2,1)}, bf16[704,128]{1,0:T(8,128)(2,1)}, bf16[704,128]{1,0:T(8,128)(2,1)}, bf16[704,128]{1,0:T(8,128)(2,1)}, bf16[7...) custom-call(s32[1]{0:T(128)} %bitcast.me_ref, ...), custom_call_target="tpu_custom_call" | custom-call | flops 1342177280 | bytes 8388608 | tf_op jit(solution)/shard_map/pallas_call | solution.py:284
  5.8 4.0 %collective-permute-start = (bf16[704,128]{1,0:T(8,128)(2,1)}, bf16[704,128]{1,0:T(8,128)(2,1)S(1)}, u32[]{:S(2)}, u32[]{:S(2)}) collective-permute-start(bf16[704,128]{1,0:T(8,128)(2,1)} %get-tuple-element.13), channel_id=1, source_target_pairs={{0,6},{1,7},{2,4},{3,5},{4,2},{5,3},{6,0},{7,1},{8,14},{9,15},{10,... | collective-permute-start | bytes 540680 | tf_op jit(solution)/shard_map/ppermute | solution.py:336
  9.8 0.0 collective-permute-start.1
  9.8 1.2 %collective-permute-start.2 = (bf16[704,128]{1,0:T(8,128)(2,1)}, bf16[704,128]{1,0:T(8,128)(2,1)S(1)}, u32[]{:S(2)}, u32[]{:S(2)}) collective-permute-start(bf16[704,128]{1,0:T(8,128)(2,1)} %get-tuple-element.15), channel_id=1, source_target_pairs={{0,4},{1,5},{2,6},{3,7},{4,0},{5,1},{6,2},{7,3},{8,12},{9,13},{10,... | collective-permute-start | bytes 540680 | tf_op jit(solution)/shard_map/ppermute | solution.py:336
  10.9 1.5 %collective-permute-start.3 = (bf16[704,128]{1,0:T(8,128)(2,1)}, bf16[704,128]{1,0:T(8,128)(2,1)S(1)}, u32[]{:S(2)}, u32[]{:S(2)}) collective-permute-start(bf16[704,128]{1,0:T(8,128)(2,1)} %get-tuple-element.16), channel_id=1, source_target_pairs={{0,2},{1,3},{2,0},{3,1},{4,6},{5,7},{6,4},{7,5},{8,10},{9,11},{10,... | collective-permute-start | bytes 540680 | tf_op jit(solution)/shard_map/ppermute | solution.py:336
  12.4 0.5 collective-permute-start.4
  13.0 2.3 %collective-permute-done.refs_0_ = bf16[704,128]{1,0:T(8,128)(2,1)S(1)} collective-permute-done((bf16[704,128]{1,0:T(8,128)(2,1)}, bf16[704,128]{1,0:T(8,128)(2,1)S(1)}, u32[]{:S(2)}, u32[]{:S(2)}) %collective-permute-start) | collective-permute-done | bytes 180256 | tf_op jit(solution)/shard_map/ppermute | solution.py:336
  15.2 0.0 collective-permute-start.5
  15.2 3.7 %collective-permute-done.1.refs_1_ = bf16[704,128]{1,0:T(8,128)(2,1)S(1)} collective-permute-done((bf16[704,128]{1,0:T(8,128)(2,1)}, bf16[704,128]{1,0:T(8,128)(2,1)S(1)}, u32[]{:S(2)}, u32[]{:S(2)}) %collective-permute-start.1) | collective-permute-done | bytes 180256 | tf_op jit(solution)/shard_map/ppermute | solution.py:336
  19.0 0.0 collective-permute-start.6
  19.0 3.4 %collective-permute-done.2.refs_2_ = bf16[704,128]{1,0:T(8,128)(2,1)S(1)} collective-permute-done((bf16[704,128]{1,0:T(8,128)(2,1)}, bf16[704,128]{1,0:T(8,128)(2,1)S(1)}, u32[]{:S(2)}, u32[]{:S(2)}) %collective-permute-start.2) | collective-permute-done | bytes 180256 | tf_op jit(solution)/shard_map/ppermute | solution.py:336
  22.3 1.4 %collective-permute-done.3.refs_3_ = bf16[704,128]{1,0:T(8,128)(2,1)S(1)} collective-permute-done((bf16[704,128]{1,0:T(8,128)(2,1)}, bf16[704,128]{1,0:T(8,128)(2,1)S(1)}, u32[]{:S(2)}, u32[]{:S(2)}) %collective-permute-start.3) | collective-permute-done | bytes 180256 | tf_op jit(solution)/shard_map/ppermute | solution.py:336
  23.7 2.4 %collective-permute-done.4.refs_4_ = bf16[704,128]{1,0:T(8,128)(2,1)S(1)} collective-permute-done((bf16[704,128]{1,0:T(8,128)(2,1)}, bf16[704,128]{1,0:T(8,128)(2,1)S(1)}, u32[]{:S(2)}, u32[]{:S(2)}) %collective-permute-start.4) | collective-permute-done | bytes 180256 | tf_op jit(solution)/shard_map/ppermute | solution.py:336
  26.1 0.0 collective-permute-done.5.refs_5_
  26.1 0.0 collective-permute-done.6.refs_7_
  26.1 0.0 copy-done.2
  26.1 0.0 copy-done.3
  26.1 0.0 copy-start.4
  26.1 0.9 %copy-done.4 = bf16[704,128]{1,0:T(8,128)(2,1)S(1)} copy-done((bf16[704,128]{1,0:T(8,128)(2,1)S(1)}, bf16[704,128]{1,0:T(8,128)(2,1)}, u32[]{:S(2)}) %copy-start.4) | copy-done | bytes 180248
  27.0 6.8 %shard_map.101 = bf16[4,8,16,768]{3,2,1,0:T(8,128)(2,1)} custom-call(s32[1]{0:T(128)} %bitcast.me_ref, f32[2,8,1024]{2,1,0:T(8,128)S(1)} %copy-done.3, bf16[8,1024,256]{2,1,0:T(8,128)(2,1)S(1)} %copy-done.2, bf16[704,128]{1,0:T(8,128)(2,1)S(1)} %collective-permute-done.refs_0_, bf16[704,128]{1,0:T(8,128)(2,1)S(1)} %collective-permute-done.1.refs_1_, ...), custom_call_target="tpu_custom_call" | custom-call | flops 2147483648 | bytes 8388608 | tf_op jit(solution)/shard_map/pallas_call | solution.py:284
  33.8 0.0 copy-start
  33.8 0.0 copy-start.1
  33.9 6.1 %all-to-all-start = ((bf16[32,16,768]{2,1,0:T(8,128)(2,1)}), bf16[32,16,768]{2,1,0:T(8,128)(2,1)S(1)}, u32[]{:S(2)}, u32[]{:S(2)}) async-start(bf16[32,16,768]{2,1,0:T(8,128)(2,1)} %bitcast.4), calls=%async_computation | async-start | bytes 1572864 | tf_op jit(solution)/shard_map/all_to_all | solution.py:391
  40.0 1.7 %copy.13 = bf16[1,768,2,512]{3,1,2,0:T(8,128)(2,1)S(1)} copy(bf16[1,768,2,512]{3,2,1,0:T(2,128)(2,1)} %param.16) | data formatting | bytes 3145728 | tf_op args[6]
  41.6 19.0 %all-to-all-done = bf16[32,16,768]{2,1,0:T(8,128)(2,1)S(1)} async-done(((bf16[32,16,768]{2,1,0:T(8,128)(2,1)}), bf16[32,16,768]{2,1,0:T(8,128)(2,1)S(1)}, u32[]{:S(2)}, u32[]{:S(2)}) %all-to-all-start) | async-done | bytes 786464 | tf_op jit(solution)/shard_map/all_to_all | solution.py:391
  60.6 0.0 copy-done
  60.6 0.0 copy-done.1
  60.6 1.3 %shard_map.102 = f32[32,8,128]{2,1,0:T(8,128)S(1)} custom-call(bf16[4,8,16,768]{3,2,1,0:T(8,128)(2,1)S(1)} %bitcast.14, f32[1,768]{1,0:T(1,128)S(1)} %bitcast.15, f32[64,64]{1,0:T(8,128)S(1)} %copy-done, bf16[2,768,512]{2,1,0:T(8,128)(2,1)S(1)} %bitcast.13), custom_call_target="tpu_custom_call" | custom-call | tf_op jit(solution)/shard_map/pallas_call | solution.py:284
  61.9 11.7 %all_to_all.10.part_ref = f32[32,8,128]{2,1,0:T(8,128)S(1)} all-to-all(f32[32,8,128]{2,1,0:T(8,128)S(1)} %shard_map.102), channel_id=1, replica_groups=mesh['patch'=4,'mode'=8] {'patch','mode'}, dimensions={0} | all-to-all | bytes 262144 | tf_op jit(solution)/shard_map/all_to_all | solution.py:410
  73.6 0.7 shard_map.103
Async XLA Ops:
  0.0 26.1 %copy-start.2 = (bf16[8,1024,256]{2,1,0:T(8,128)(2,1)S(1)}, bf16[8,1024,256]{2,1,0:T(8,128)(2,1)}, u32[]{:S(2)}) copy-start(bf16[8,1024,256]{2,1,0:T(8,128)(2,1)} %constant.27.clone.table_hbm) | copy-start | bytes 12582916
  0.0 26.1 %copy-start.3 = (f32[2,8,1024]{2,1,0:T(8,128)S(1)}, f32[2,8,1024]{2,1,0:T(8,128)}, u32[]{:S(2)}) copy-start(f32[2,8,1024]{2,1,0:T(8,128)} %constant.26.clone.twiddle_ref) | copy-start | bytes 196612
  5.8 9.4 %collective-permute-start = (bf16[704,128]{1,0:T(8,128)(2,1)}, bf16[704,128]{1,0:T(8,128)(2,1)S(1)}, u32[]{:S(2)}, u32[]{:S(2)}) collective-permute-start(bf16[704,128]{1,0:T(8,128)(2,1)} %get-tuple-element.13), channel_id=1, source_target_pairs={{0,6},{1,7},{2,4},{3,5},{4,2},{5,3},{6,0},{7,1},{8,14},{9,15},{10,... | collective-permute-start | bytes 540680 | tf_op jit(solution)/shard_map/ppermute | solution.py:336
  9.8 9.2 %collective-permute-start.1 = (bf16[704,128]{1,0:T(8,128)(2,1)}, bf16[704,128]{1,0:T(8,128)(2,1)S(1)}, u32[]{:S(2)}, u32[]{:S(2)}) collective-permute-start(bf16[704,128]{1,0:T(8,128)(2,1)} %get-tuple-element.14), channel_id=1, source_target_pairs={{0,7},{1,6},{2,5},{3,4},{4,3},{5,2},{6,1},{7,0},{8,15},{9,14},{10,... | collective-permute-start | bytes 540680 | tf_op jit(solution)/shard_map/ppermute | solution.py:336
  9.8 12.5 %collective-permute-start.2 = (bf16[704,128]{1,0:T(8,128)(2,1)}, bf16[704,128]{1,0:T(8,128)(2,1)S(1)}, u32[]{:S(2)}, u32[]{:S(2)}) collective-permute-start(bf16[704,128]{1,0:T(8,128)(2,1)} %get-tuple-element.15), channel_id=1, source_target_pairs={{0,4},{1,5},{2,6},{3,7},{4,0},{5,1},{6,2},{7,3},{8,12},{9,13},{10,... | collective-permute-start | bytes 540680 | tf_op jit(solution)/shard_map/ppermute | solution.py:336
  10.9 12.8 %collective-permute-start.3 = (bf16[704,128]{1,0:T(8,128)(2,1)}, bf16[704,128]{1,0:T(8,128)(2,1)S(1)}, u32[]{:S(2)}, u32[]{:S(2)}) collective-permute-start(bf16[704,128]{1,0:T(8,128)(2,1)} %get-tuple-element.16), channel_id=1, source_target_pairs={{0,2},{1,3},{2,0},{3,1},{4,6},{5,7},{6,4},{7,5},{8,10},{9,11},{10,... | collective-permute-start | bytes 540680 | tf_op jit(solution)/shard_map/ppermute | solution.py:336
  12.4 13.6 %collective-permute-start.4 = (bf16[704,128]{1,0:T(8,128)(2,1)}, bf16[704,128]{1,0:T(8,128)(2,1)S(1)}, u32[]{:S(2)}, u32[]{:S(2)}) collective-permute-start(bf16[704,128]{1,0:T(8,128)(2,1)} %get-tuple-element.17), channel_id=1, source_target_pairs={{0,5},{1,4},{2,7},{3,6},{4,1},{5,0},{6,3},{7,2},{8,13},{9,12},{10,... | collective-permute-start | bytes 540680 | tf_op jit(solution)/shard_map/ppermute | solution.py:336
  15.2 10.8 %collective-permute-start.5 = (bf16[704,128]{1,0:T(8,128)(2,1)}, bf16[704,128]{1,0:T(8,128)(2,1)S(1)}, u32[]{:S(2)}, u32[]{:S(2)}) collective-permute-start(bf16[704,128]{1,0:T(8,128)(2,1)} %get-tuple-element.18), channel_id=1, source_target_pairs={{0,3},{1,2},{2,1},{3,0},{4,7},{5,6},{6,5},{7,4},{8,11},{9,10},{10,... | collective-permute-start | bytes 540680 | tf_op jit(solution)/shard_map/ppermute | solution.py:336
  19.0 7.1 %collective-permute-start.6 = (bf16[704,128]{1,0:T(8,128)(2,1)}, bf16[704,128]{1,0:T(8,128)(2,1)S(1)}, u32[]{:S(2)}, u32[]{:S(2)}) collective-permute-start(bf16[704,128]{1,0:T(8,128)(2,1)} %get-tuple-element.20), channel_id=1, source_target_pairs={{0,1},{1,0},{2,3},{3,2},{4,5},{5,4},{6,7},{7,6},{8,9},{9,8},{10,11... | collective-permute-start | bytes 540680 | tf_op jit(solution)/shard_map/ppermute | solution.py:336
  26.1 0.9 %copy-start.4 = (bf16[704,128]{1,0:T(8,128)(2,1)S(1)}, bf16[704,128]{1,0:T(8,128)(2,1)}, u32[]{:S(2)}) copy-start(bf16[704,128]{1,0:T(8,128)(2,1)} %get-tuple-element.19.refs_6_) | copy-start | bytes 540676
  33.8 26.8 %copy-start = (f32[64,64]{1,0:T(8,128)S(1)}, f32[64,64]{1,0:T(8,128)}, u32[]{:S(2)}) copy-start(f32[64,64]{1,0:T(8,128)} %cov_ref.1) | copy-start | bytes 49156
  33.8 26.8 %copy-start.1 = (f32[768,1]{0,1:T(1,128)S(1)}, f32[768,1]{0,1:T(1,128)}, u32[]{:S(2)}) copy-start(f32[768,1]{0,1:T(1,128)} %param.14) | copy-start | bytes 9220
  33.9 26.7 %all-to-all-start = ((bf16[32,16,768]{2,1,0:T(8,128)(2,1)}), bf16[32,16,768]{2,1,0:T(8,128)(2,1)S(1)}, u32[]{:S(2)}, u32[]{:S(2)}) async-start(bf16[32,16,768]{2,1,0:T(8,128)(2,1)} %bitcast.4), calls=%async_computation | async-start | bytes 1572864 | tf_op jit(solution)/shard_map/all_to_all | solution.py:391

commit v2 on v1

--- a/solution.py
+++ b/solution.py
@@ -13,7 +13,6 @@
 LANES = 128
 MIB = 1 << 20
 SUBLANES = 8
-PAIR = 1
 
 
 def rotate(value, step, points):
@@ -47,22 +46,19 @@
     return out
 
 
-def whiten_kernel(order, me_ref, sky_hbm, mask_hbm, factor_hbm, leg_hbm, sort_hbm, *refs):
-    sky, mask, factor, leg, sort, white, stage, sems = refs[-8:]
-    outs = refs[:-8]
+def whiten_kernel(sky_hbm, mask_hbm, factor_hbm, leg_hbm, sort_hbm, out_hbm, *refs):
+    sky, mask, factor, leg, sort, white, stage, sems = refs
     cycles, chans, pixels = sky.shape
-    groups = len(outs)
+    groups = stage.shape[0]
     width = chans // groups
     group = max(1, SUBLANES // width)
     tall = group * width
     split = pixels // LANES
     sources, targets = (factor_hbm, sky_hbm, mask_hbm, leg_hbm, sort_hbm), (factor, sky, mask, leg, sort)
     copies = [pltpu.make_async_copy(a, b, sems.at[n]) for n, (a, b) in enumerate(zip(sources, targets))]
-    for copy in copies[:3]:
+    for copy in copies:
         copy.start()
     copies[0].wait()
-    copies[3].start()
-    copies[4].start()
     row_of = lax.broadcasted_iota(jnp.int32, (tall, group * chans), 0) // width
     lane_of = lax.broadcasted_iota(jnp.int32, (tall, group * chans), 1) // chans
     lefts = []
@@ -97,6 +93,14 @@
         for e in range(groups):
             place = split * count + n * high
             stage[e, place : place + high, :] = rows[:, n * LANES : (n + 1) * LANES]
+    sends = []
+
+    def send(first, last):
+        where = (slice(None), slice(first, last))
+        sends.append(pltpu.make_async_copy(stage.at[where], out_hbm.at[where], sems.at[5 + len(sends)]))
+        sends[-1].start()
+
+    send(split * count, stage.shape[1])
     copies[4].wait()
     for pair in range(split // 2):
         wide = slice(pair * 2 * LANES, (pair + 1) * 2 * LANES)
@@ -107,31 +111,25 @@
                 stage[e, s * count : (s + 1) * count, :] = value[
                     e * count : (e + 1) * count, side * LANES : (side + 1) * LANES
                 ]
-    me = me_ref[0]
-    sends = [
-        pltpu.make_async_copy(stage.at[jnp.bitwise_xor(me, n)], outs[slot], sems.at[5 + slot])
-        for slot, n in enumerate(order)
-    ]
-    for send in sends:
-        send.start()
+        send(pair * 2 * count, (pair + 1) * 2 * count)
     for send in sends:
         send.wait()
 
 
-def modes_kernel(order, cycles, width, offsets, me_ref, twiddle_ref, table_hbm, *refs):
-    slots = refs[: len(order)]
-    out_hbm, table, left, leg, prod_a, prod_b, x_ref, out_ref, table_sems, out_sems = refs[len(order) :]
+def modes_kernel(width, offsets, twiddle_ref, table_hbm, z_ref, out_hbm, *refs):
+    table, left, leg, prod_a, prod_b, x_ref, out_ref, table_sems, out_sems = refs
     tiles = table.shape[0]
     split = twiddle_ref.shape[1]
     tall = x_ref.shape[3]
     group = tall // width
     modes = out_ref.shape[3]
-    sources = len(order) // PAIR
+    sources = out_ref.shape[1]
+    parts = z_ref.shape[0] // sources
+    cycles = leg.shape[0] // offsets
     blocks = sources * modes // (tiles * LANES)
     per = modes // LANES
-    count = cycles // PAIR * width
-    high = cycles // PAIR * offsets
-    me = me_ref[0]
+    count = cycles // parts * width
+    high = cycles // parts * offsets
 
     def copy(tile):
         return pltpu.make_async_copy(table_hbm.at[tile], table.at[tile], table_sems.at[tile])
@@ -144,12 +142,12 @@
 
     copy(0).start()
     copy(1).start()
-    for slot, n in enumerate(order):
-        q = jnp.bitwise_xor(me, n) % sources
-        lanes = pl.ds(pl.multiple_of(q * LANES, LANES), LANES)
-        for s in range(split):
-            place = (s * PAIR + n // sources) * count
-            left[place : place + count, lanes] = slots[slot][s * count : (s + 1) * count, :]
+    for p in range(parts):
+        for q in range(sources):
+            for n in range(split):
+                place = (n * parts + p) * count
+                rows = z_ref[p * sources + q, n * count : (n + 1) * count, :]
+                left[place : place + count, q * LANES : (q + 1) * LANES] = rows
     for tile in range(2, tiles):
         copy(tile).start()
 
@@ -158,13 +156,12 @@
 
     copy(0).wait()
     product(0, prod_a)
-    for slot, n in enumerate(order):
-        q = jnp.bitwise_xor(me, n) % sources
-        for j in range(per):
-            lanes = pl.ds(pl.multiple_of((q * per + j) * LANES, LANES), LANES)
-            place = split * count + j * high
-            rows = slots[slot][place : place + high, :].astype(jnp.float32)
-            leg[n // sources * high : (n // sources + 1) * high, lanes] = rows
+    for p in range(parts):
+        for q in range(sources):
+            for n in range(per):
+                place = split * count + n * high
+                rows = z_ref[p * sources + q, place : place + high, :].astype(jnp.float32)
+                leg[p * high : (p + 1) * high, (q * per + n) * LANES : (q * per + n + 1) * LANES] = rows
 
     def use(tile, prod):
         lanes = pl.ds(pl.multiple_of(tile * LANES, LANES), LANES)
@@ -239,15 +236,13 @@
     patches, groups, rows, lanes = alm_ref.shape
     chans = cov_ref.shape[0]
     width = rows // 2
-    for low in range(PAIR):
-        for g in range(groups):
-            part = alm_ref[low, g].astype(jnp.float32)
-            for p in range(low + PAIR, patches, PAIR):
-                part += alm_ref[p, g].astype(jnp.float32)
-            part = part * band_ref[...]
-            place = (low * groups + g) * width
-            for t in range(2):
-                left_ref[t, place : place + width, :] = part[t * width : (t + 1) * width]
+    for g in range(groups):
+        part = alm_ref[0, g].astype(jnp.float32)
+        for p in range(1, patches):
+            part += alm_ref[p, g].astype(jnp.float32)
+        part = part * band_ref[...]
+        for t in range(2):
+            left_ref[t, g * width : (g + 1) * width, :] = part[t * width : (t + 1) * width]
     sketch = None
     for t in range(2):
         term = lax.dot_general(
@@ -313,8 +308,9 @@
     modes, _ = band_power.shape
     offsets = cycle_legendre.shape[2]
     columns = test_matrix.shape[3]
-    mode_count, patches = lax.axis_size("mode"), lax.axis_size("patch")
-    groups = PAIR * mode_count
+    mode_count, pair = lax.axis_size("mode"), lax.axis_size("low")
+    groups = pair * mode_count
+    devices = lax.axis_size("high") * groups
     width = chans // groups
     group = max(1, SUBLANES // width)
     split = pixels // LANES
@@ -322,25 +318,13 @@
     legs = cycles * offsets * (modes // LANES)
     tiles = mode_count
     blocks = modes * mode_count // (tiles * LANES)
-    everyone = ("patch", "mode")
+    everyone = ("high", "low", "mode")
     hbm, vmem, bf16, f32, shape = pl.ANY, pltpu.VMEM, jnp.bfloat16, jnp.float32, jax.ShapeDtypeStruct
-
-    place = lax.axis_index("patch") % PAIR * mode_count + lax.axis_index("mode")
-    me = place.astype(jnp.int32).reshape(1)
-
-    def partner(place, n):
-        return (place // groups) * groups + (place % groups ^ n)
-
-    def swap(value, n):
-        pairs = [(i, partner(i, n)) for i in range(patches * mode_count)]
-        return lax.ppermute(value, everyone, pairs)
-
     twiddle, table = transform_tables(split, pixels * mode_count)
-    order = sorted(range(groups), key=lambda n: (-(n >> 1).bit_count(), n % 2 - (n < 2), -n))
-
-    messages = call(
-        functools.partial(whiten_kernel, order),
-        [shape((rows + legs, LANES), bf16)] * groups,
+
+    message = call(
+        whiten_kernel,
+        shape((groups, rows + legs, LANES), bf16),
         [
             vmem((cycles, chans, pixels), bf16),
             vmem((cycles, pixels), jnp.int32),
@@ -349,11 +333,10 @@
             vmem((pixels, pixels), bf16),
             vmem((cycles * chans, pixels), bf16),
             vmem((groups, rows + legs, LANES), bf16),
-            pltpu.SemaphoreType.DMA((5 + groups,)),
+            pltpu.SemaphoreType.DMA((6 + split // 2,)),
         ],
         56,
-        [pltpu.SMEM] + [hbm] * 5,
-        me,
+        [hbm] * 5,
         jnp.transpose(sky_map, (0, 2, 1)),
         pixel_mask,
         noise_factor[:, 0],
@@ -362,41 +345,40 @@
         out_space=hbm,
         cost=(2 * cycles * chans * pixels * (pixels + 4 * chans), 8 * MIB),
     )
-    slots = [messages[slot] if n == 0 else swap(messages[slot], n) for slot, n in enumerate(order)]
+    message = lax.all_to_all(message, ("low", "mode"), 0, 0, tiled=True)
 
     alm = call(
-        functools.partial(modes_kernel, order, PAIR * cycles, width, offsets),
+        functools.partial(modes_kernel, width, offsets),
         shape((offsets, mode_count, 2 * width, modes), bf16),
         [
             vmem((tiles, tiles * LANES, 2 * LANES), bf16),
-            vmem((PAIR * rows, tiles * LANES), bf16),
-            vmem((PAIR * cycles * offsets, mode_count * modes), f32),
-            vmem((PAIR * rows, 2 * LANES), f32),
-            vmem((PAIR * rows, 2 * LANES), f32),
-            vmem((blocks, 2, PAIR * cycles // group, group * width, LANES), f32),
+            vmem((pair * rows, tiles * LANES), bf16),
+            vmem((pair * cycles * offsets, mode_count * modes), f32),
+            vmem((pair * rows, 2 * LANES), f32),
+            vmem((pair * rows, 2 * LANES), f32),
+            vmem((blocks, 2, pair * cycles // group, group * width, LANES), f32),
             vmem((offsets, mode_count, 2 * width, modes), bf16),
             pltpu.SemaphoreType.DMA((tiles,)),
             pltpu.SemaphoreType.DMA((tiles // 2, 2 * blocks)),
         ],
         40,
-        [pltpu.SMEM, vmem, hbm] + [vmem] * groups,
-        me,
+        [vmem, hbm, vmem],
         jnp.asarray(twiddle),
         jnp.asarray(table),
-        *slots,
+        message,
         out_space=hbm,
-        cost=(4 * PAIR * rows * (tiles * LANES) ** 2, 8 * MIB),
+        cost=(4 * pair * rows * (tiles * LANES) ** 2, 8 * MIB),
     )
-    alm = alm.reshape(patches * mode_count, 2 * width, modes)
+    alm = alm.reshape(devices, 2 * width, modes)
     alm = lax.all_to_all(alm, everyone, 0, 0, tiled=True)
-    alm = alm.reshape(patches, mode_count, 2 * width, modes)
-
-    share = columns // (patches * mode_count)
+    alm = alm.reshape(devices // groups, groups, 2 * width, modes)
+
+    share = columns // (devices)
     fold = LANES // chans
     packed = share % (8 * fold) == 0
     part = call(
         sketch_kernel,
-        shape((patches * mode_count, share // fold, LANES) if packed else (columns, chans), f32),
+        shape((devices, share // fold, LANES) if packed else (columns, chans), f32),
         [vmem((2, chans, modes), f32)],
         24,
         [vmem] * 4,
@@ -406,24 +388,27 @@
         jnp.transpose(test_matrix[0], (1, 0, 2)),
     )
     if not packed:
-        part = part.reshape(patches * mode_count, share, chans)
+        part = part.reshape(devices, share, chans)
     part = lax.all_to_all(part, everyone, 0, 0, tiled=True)
     return jnp.transpose(call(total_kernel, shape((share, chans), f32), [], 16, [vmem], part))
 
 
 def solution(mesh):
+    patches, modes = mesh.shape["patch"], mesh.shape["mode"]
+    mesh = jax.sharding.Mesh(mesh.devices.reshape(patches // 2, 2, modes), ("high", "low", "mode"))
+    patch = ("high", "low")
     return jax.shard_map(
         local,
         mesh=mesh,
         in_specs=(
-            P("patch", "mode", None),
-            P("patch", "mode"),
-            P("patch", "mode", None, None),
-            P("patch", "mode", None),
-            P("mode", "patch"),
+            P(patch, "mode", None),
+            P(patch, "mode"),
+            P(patch, "mode", None, None),
+            P(patch, "mode", None),
+            P("mode", patch),
             P(),
-            P("patch", "mode", None, None),
+            P(patch, "mode", None, None),
         ),
-        out_specs=P(None, ("patch", "mode")),
+        out_specs=P(None, (*patch, "mode")),
         check_vma=False,
     )

time: 74.6 us -> 71.7 us (0.961)
  blocking collectives: 11.7 us -> 41.7 us
  waiting for transfers between devices: 32.1 us -> 11.5 us
  starting transfers between devices: 13.3 us -> 2.95 us
  Pallas kernels: 14.6 us -> 13.5 us
  local copies, waits for them, and re-layouts: 2.59 us -> 1.68 us
    all_to_all x0 -> x1, blocking collectives: none -> 31 us  [local(): message = lax.all_to_all(message, ('low', 'mode'), 0, 0, tiled=True)]
    ppermute x7 -> x0, waiting for transfers between devices: 13.1 us -> none  [swap(): return lax.ppermute(value, everyone, pairs)]
    all_to_all x1, waiting for transfers between devices: 19 us -> 11.5 us  [local(): alm = lax.all_to_all(alm, everyone, 0, 0, tiled=True)]
    ppermute x7 -> x0, starting transfers between devices: 7.15 us -> none  [swap(): return lax.ppermute(value, everyone, pairs)]
    all_to_all x1, starting transfers between devices: 6.11 us -> 2.95 us  [local(): alm = lax.all_to_all(alm, everyone, 0, 0, tiled=True)]
    pallas_call x4, Pallas kernels: 14.6 us -> 13.5 us  [call(): pl.pallas_call(kernel, out_shape=shape, in_specs=[pl.BlockSpec(memory_spa...]
    all_to_all x1, blocking collectives: 11.7 us -> 10.7 us  [local(): part = lax.all_to_all(part, everyone, 0, 0, tiled=True)]
    unnamed x11 -> x9, local copies, waits for them, and re-layouts: 2.59 us -> 1.68 us
  transfers between devices with their start and end apart: 8 -> 1, of which waited for: 6 -> 1; matrix products, arithmetic and copies ran while one was open for 2% -> 2% of each run, Pallas kernels for 0% -> 0%
where the time goes in v2:
time: 71.7 us; the launch traced here: 71.4 us
  blocking collectives  41.7 us (58%)
  Pallas kernels  13.5 us (19%)
  waiting for transfers between devices  11.5 us (16%)
  starting transfers between devices  2.95 us (4%)
  local copies, waits for them, and re-layouts  1.68 us (2%)
    all_to_all x1, blocking collectives, local(): message = lax.all_to_all(message, ('low', 'mode'), 0, 0, tiled=True)  31 us
    pallas_call x4, Pallas kernels, call(): pl.pallas_call(kernel, out_shape=shape, in_specs=[pl.BlockSpec(memory_spa...  13.5 us
    all_to_all x1, waiting for transfers between devices, local(): alm = lax.all_to_all(alm, everyone, 0, 0, tiled=True)  11.5 us
    all_to_all x1, blocking collectives, local(): part = lax.all_to_all(part, everyone, 0, 0, tiled=True)  10.7 us
    all_to_all x1, starting transfers between devices, local(): alm = lax.all_to_all(alm, everyone, 0, 0, tiled=True)  2.95 us
    unnamed x9, local copies, waits for them, and re-layouts  1.68 us
  transfers between devices with their start and end apart: 1, of which 1 were waited for; matrix products, arithmetic and copies ran while one was open for 2% of the time, Pallas kernels for 0%

profile of v2, /device:TPU:0, one launch (start us, length us, event | category | flops | bytes accessed | tf_op | source)
XLA Modules:
  0.0 71.4 jit_solution(3679157660213002095)
XLA Ops:
  0.0 0.0 copy-start.2
  0.0 4.4 %shard_map.100 = bf16[16,448,128]{2,1,0:T(8,128)(2,1)} custom-call(bf16[8,64,1024]{2,1,0:T(8,128)(2,1)} %bitcast.15, s32[8,1024]{1,0:T(8,128)} %mask_hbm.1, f32[8,64,64]{2,1,0:T(8,128)} %bitcast.16, f32[8,4,768]{2,1,0:T(4,128)} %bitcast.17, bf16[1024,1024]{1,0:T(8,128)(2,1)} %constant.6.clone.sort_hbm), custom_call_target="tpu_custom_call" | custom-call | flops 1342177280 | bytes 8388608 | tf_op jit(solution)/shard_map/pallas_call | solution.py:279
  4.4 0.0 copy-start.3
  4.4 31.0 %all_to_all.15.z_ref = bf16[16,448,128]{2,1,0:T(8,128)(2,1)S(1)} all-to-all(bf16[16,448,128]{2,1,0:T(8,128)(2,1)} %shard_map.100), channel_id=1, replica_groups=mesh['high'=2,'low'=2,'mode'=8] {'low','mode'}, dimensions={0} | all-to-all | bytes 3670016 | tf_op jit(solution)/shard_map/all_to_all | solution.py:348
  35.4 0.0 copy-done.2
  35.4 0.0 copy-done.3
  35.4 7.1 %shard_map.101 = bf16[4,8,8,768]{3,2,1,0:T(8,128)(2,1)} custom-call(f32[2,8,1024]{2,1,0:T(8,128)S(1)} %copy-done.3, bf16[8,1024,256]{2,1,0:T(8,128)(2,1)S(1)} %copy-done.2, bf16[16,448,128]{2,1,0:T(8,128)(2,1)S(1)} %all_to_all.15.z_ref), custom_call_target="tpu_custom_call" | custom-call | flops 2147483648 | bytes 8388608 | tf_op jit(solution)/shard_map/pallas_call | solution.py:279
  42.5 0.0 copy-start
  42.5 0.0 copy-start.1
  42.5 3.0 %all-to-all-start.1 = ((bf16[32,8,768]{2,1,0:T(8,128)(2,1)}), bf16[32,8,768]{2,1,0:T(8,128)(2,1)S(1)}, u32[]{:S(2)}, u32[]{:S(2)}) async-start(bf16[32,8,768]{2,1,0:T(8,128)(2,1)} %bitcast.3), calls=%async_computation.1 | async-start | bytes 786432 | tf_op jit(solution)/shard_map/all_to_all | solution.py:373
  45.5 1.7 %copy.13 = bf16[1,768,2,512]{3,1,2,0:T(8,128)(2,1)S(1)} copy(bf16[1,768,2,512]{3,2,1,0:T(2,128)(2,1)} %param.16) | data formatting | bytes 3145728 | tf_op args[6]
  47.1 11.5 %all-to-all-done.1 = bf16[32,8,768]{2,1,0:T(8,128)(2,1)S(1)} async-done(((bf16[32,8,768]{2,1,0:T(8,128)(2,1)}), bf16[32,8,768]{2,1,0:T(8,128)(2,1)S(1)}, u32[]{:S(2)}, u32[]{:S(2)}) %all-to-all-start.1) | async-done | bytes 393248 | tf_op jit(solution)/shard_map/all_to_all | solution.py:373
  58.7 0.0 copy-done
  58.7 0.0 copy-done.1
  58.7 1.3 %shard_map.102 = f32[32,8,128]{2,1,0:T(8,128)S(1)} custom-call(bf16[2,16,8,768]{3,2,1,0:T(8,128)(2,1)S(1)} %bitcast.13, f32[1,768]{1,0:T(1,128)S(1)} %bitcast.14, f32[64,64]{1,0:T(8,128)S(1)} %copy-done, bf16[2,768,512]{2,1,0:T(8,128)(2,1)S(1)} %bitcast.12), custom_call_target="tpu_custom_call" | custom-call | tf_op jit(solution)/shard_map/pallas_call | solution.py:279
  60.0 10.7 %all_to_all.16.part_ref = f32[32,8,128]{2,1,0:T(8,128)S(1)} all-to-all(f32[32,8,128]{2,1,0:T(8,128)S(1)} %shard_map.102), channel_id=1, replica_groups=mesh['high'=2,'low'=2,'mode'=8] {'high','low','mode'}, dimensions={0} | all-to-all | bytes 262144 | tf_op jit(solution)/shard_map/all_to_all | solution.py:392
  70.7 0.7 shard_map.103
Async XLA Ops:
  0.0 35.4 %copy-start.2 = (bf16[8,1024,256]{2,1,0:T(8,128)(2,1)S(1)}, bf16[8,1024,256]{2,1,0:T(8,128)(2,1)}, u32[]{:S(2)}) copy-start(bf16[8,1024,256]{2,1,0:T(8,128)(2,1)} %constant.8.clone.table_hbm) | copy-start | bytes 12582916
  4.4 31.0 %copy-start.3 = (f32[2,8,1024]{2,1,0:T(8,128)S(1)}, f32[2,8,1024]{2,1,0:T(8,128)}, u32[]{:S(2)}) copy-start(f32[2,8,1024]{2,1,0:T(8,128)} %constant.7.clone.twiddle_ref) | copy-start | bytes 196612
  42.5 16.2 %copy-start = (f32[64,64]{1,0:T(8,128)S(1)}, f32[64,64]{1,0:T(8,128)}, u32[]{:S(2)}) copy-start(f32[64,64]{1,0:T(8,128)} %cov_ref.1) | copy-start | bytes 49156
  42.5 16.2 %copy-start.1 = (f32[768,1]{0,1:T(1,128)S(1)}, f32[768,1]{0,1:T(1,128)}, u32[]{:S(2)}) copy-start(f32[768,1]{0,1:T(1,128)} %param.14) | copy-start | bytes 9220
  42.5 16.1 %all-to-all-start.1 = ((bf16[32,8,768]{2,1,0:T(8,128)(2,1)}), bf16[32,8,768]{2,1,0:T(8,128)(2,1)S(1)}, u32[]{:S(2)}, u32[]{:S(2)}) async-start(bf16[32,8,768]{2,1,0:T(8,128)(2,1)} %bitcast.3), calls=%async_computation.1 | async-start | bytes 786432 | tf_op jit(solution)/shard_map/all_to_all | solution.py:373

commit v3 on v2

--- a/solution.py
+++ b/solution.py
@@ -46,18 +46,24 @@
     return out
 
 
-def whiten_kernel(sky_hbm, mask_hbm, factor_hbm, leg_hbm, sort_hbm, out_hbm, *refs):
-    sky, mask, factor, leg, sort, white, stage, sems = refs
+def whiten_kernel(sky_hbm, mask_hbm, factor_hbm, leg_hbm, out_hbm, leg_out, *refs):
+    sky, mask, factor, leg, sort, white, stage, leg_rows, sems = refs
     cycles, chans, pixels = sky.shape
     groups = stage.shape[0]
     width = chans // groups
     group = max(1, SUBLANES // width)
     tall = group * width
     split = pixels // LANES
-    sources, targets = (factor_hbm, sky_hbm, mask_hbm, leg_hbm, sort_hbm), (factor, sky, mask, leg, sort)
+    sources, targets = (factor_hbm, sky_hbm, mask_hbm, leg_hbm), (factor, sky, mask, leg)
     copies = [pltpu.make_async_copy(a, b, sems.at[n]) for n, (a, b) in enumerate(zip(sources, targets))]
     for copy in copies:
         copy.start()
+    shape = (2 * LANES, LANES)
+    ahead = lax.broadcasted_iota(jnp.int32, shape, 0) - split * lax.broadcasted_iota(jnp.int32, shape, 1)
+    for first in range(0, pixels, 2 * LANES):
+        for s in range(split):
+            block = jnp.where(ahead == s - first, 1.0, 0.0).astype(jnp.bfloat16)
+            sort[first : first + 2 * LANES, s * LANES : (s + 1) * LANES] = block
     copies[0].wait()
     row_of = lax.broadcasted_iota(jnp.int32, (tall, group * chans), 0) // width
     lane_of = lax.broadcasted_iota(jnp.int32, (tall, group * chans), 1) // chans
@@ -90,18 +96,15 @@
     rows = jnp.concatenate([leg[r] for r in range(cycles)], axis=0).astype(jnp.bfloat16)
     high = rows.shape[0]
     for n in range(rows.shape[1] // LANES):
-        for e in range(groups):
-            place = split * count + n * high
-            stage[e, place : place + high, :] = rows[:, n * LANES : (n + 1) * LANES]
-    sends = []
+        leg_rows[n * high : (n + 1) * high, :] = rows[:, n * LANES : (n + 1) * LANES]
+    sends = [pltpu.make_async_copy(leg_rows, leg_out, sems.at[4])]
+    sends[0].start()
 
     def send(first, last):
         where = (slice(None), slice(first, last))
-        sends.append(pltpu.make_async_copy(stage.at[where], out_hbm.at[where], sems.at[5 + len(sends)]))
+        sends.append(pltpu.make_async_copy(stage.at[where], out_hbm.at[where], sems.at[4 + len(sends)]))
         sends[-1].start()
 
-    send(split * count, stage.shape[1])
-    copies[4].wait()
     for pair in range(split // 2):
         wide = slice(pair * 2 * LANES, (pair + 1) * 2 * LANES)
         value = jnp.dot(white[...], sort[:, wide], preferred_element_type=jnp.float32).astype(jnp.bfloat16)
@@ -116,8 +119,8 @@
         send.wait()
 
 
-def modes_kernel(width, offsets, twiddle_ref, table_hbm, z_ref, out_hbm, *refs):
-    table, left, leg, prod_a, prod_b, x_ref, out_ref, table_sems, out_sems = refs
+def modes_kernel(width, offsets, twiddle_ref, table_hbm, leg_hbm, z_ref, out_hbm, *refs):
+    table, left, leg_in, leg, prod_a, prod_b, x_ref, out_ref, table_sems, leg_sem, out_sems = refs
     tiles = table.shape[0]
     split = twiddle_ref.shape[1]
     tall = x_ref.shape[3]
@@ -141,6 +144,8 @@
         return pltpu.make_async_copy(out_ref.at[where], out_hbm.at[where], out_sems.at[step, n])
 
     copy(0).start()
+    leg_copy = pltpu.make_async_copy(leg_hbm, leg_in, leg_sem)
+    leg_copy.start()
     copy(1).start()
     for p in range(parts):
         for q in range(sources):
@@ -156,11 +161,11 @@
 
     copy(0).wait()
     product(0, prod_a)
+    leg_copy.wait()
     for p in range(parts):
         for q in range(sources):
             for n in range(per):
-                place = split * count + n * high
-                rows = z_ref[p * sources + q, place : place + high, :].astype(jnp.float32)
+                rows = leg_in[p * sources + q, n * high : (n + 1) * high, :].astype(jnp.float32)
                 leg[p * high : (p + 1) * high, (q * per + n) * LANES : (q * per + n + 1) * LANES] = rows
 
     def use(tile, prod):
@@ -186,6 +191,7 @@
             mode_tile = b * tiles + tile
             d, n = mode_tile // per, mode_tile % per
             mode = pl.ds(pl.multiple_of(mode_tile * LANES, LANES), LANES)
+            parts = [[x_ref[b, t, pack] for pack in range(cycles // group)] for t in range(2)]
             for k in range(offsets):
                 total = [None, None]
                 for pack in range(cycles // group):
@@ -198,7 +204,7 @@
                         else:
                             row = jnp.where(cycle_of < g, row, next_row)
                     for t in range(2):
-                        term = row * x_ref[b, t, pack]
+                        term = row * parts[t][pack]
                         total[t] = term if pack == 0 else total[t] + term
                 step = tall // 2
                 while step >= width:
@@ -298,11 +304,6 @@
     return twiddle, table.astype(ml_dtypes.bfloat16)
 
 
-def sorting(pixels, split):
-    place = np.arange(pixels) % split * (pixels // split) + np.arange(pixels) // split
-    return (place[:, None] == np.arange(pixels)[None, :]).astype(ml_dtypes.bfloat16)
-
-
 def local(sky_map, pixel_mask, noise_factor, cycle_legendre, band_power, channel_cov, test_matrix):
     cycles, pixels, chans = sky_map.shape
     modes, _ = band_power.shape
@@ -322,9 +323,9 @@
     hbm, vmem, bf16, f32, shape = pl.ANY, pltpu.VMEM, jnp.bfloat16, jnp.float32, jax.ShapeDtypeStruct
     twiddle, table = transform_tables(split, pixels * mode_count)
 
-    message = call(
+    message, leg = call(
         whiten_kernel,
-        shape((groups, rows + legs, LANES), bf16),
+        [shape((groups, rows, LANES), bf16), shape((legs, LANES), bf16)],
         [
             vmem((cycles, chans, pixels), bf16),
             vmem((cycles, pixels), jnp.int32),
@@ -332,20 +333,21 @@
             vmem((cycles, offsets, modes), f32),
             vmem((pixels, pixels), bf16),
             vmem((cycles * chans, pixels), bf16),
-            vmem((groups, rows + legs, LANES), bf16),
-            pltpu.SemaphoreType.DMA((6 + split // 2,)),
+            vmem((groups, rows, LANES), bf16),
+            vmem((legs, LANES), bf16),
+            pltpu.SemaphoreType.DMA((5 + split // 2,)),
         ],
         56,
-        [hbm] * 5,
+        [hbm] * 4,
         jnp.transpose(sky_map, (0, 2, 1)),
         pixel_mask,
         noise_factor[:, 0],
         jnp.transpose(cycle_legendre, (0, 2, 1)),
-        jnp.asarray(sorting(pixels, split)),
         out_space=hbm,
         cost=(2 * cycles * chans * pixels * (pixels + 4 * chans), 8 * MIB),
     )
     message = lax.all_to_all(message, ("low", "mode"), 0, 0, tiled=True)
+    leg = lax.all_gather(leg, ("low", "mode"), axis=0, tiled=False)
 
     alm = call(
         functools.partial(modes_kernel, width, offsets),
@@ -353,18 +355,21 @@
         [
             vmem((tiles, tiles * LANES, 2 * LANES), bf16),
             vmem((pair * rows, tiles * LANES), bf16),
+            vmem((groups, legs, LANES), bf16),
             vmem((pair * cycles * offsets, mode_count * modes), f32),
             vmem((pair * rows, 2 * LANES), f32),
             vmem((pair * rows, 2 * LANES), f32),
             vmem((blocks, 2, pair * cycles // group, group * width, LANES), f32),
             vmem((offsets, mode_count, 2 * width, modes), bf16),
             pltpu.SemaphoreType.DMA((tiles,)),
+            pltpu.SemaphoreType.DMA(()),
             pltpu.SemaphoreType.DMA((tiles // 2, 2 * blocks)),
         ],
         40,
-        [vmem, hbm, vmem],
+        [vmem, hbm, hbm, vmem],
         jnp.asarray(twiddle),
         jnp.asarray(table),
+        leg,
         message,
         out_space=hbm,
         cost=(4 * pair * rows * (tiles * LANES) ** 2, 8 * MIB),

time: 71.7 us -> 81.3 us (1.13)
  starting transfers between devices: 2.95 us -> 11 us
  local copies, waits for them, and re-layouts: 1.68 us -> 3.88 us
    all_to_all x1 -> x0, blocking collectives: 31 us -> none  [local(): message = lax.all_to_all(message, ('low', 'mode'), 0, 0, tiled=True)]
    all_gather x0 -> x1, blocking collectives: none -> 30.6 us  [local(): leg = lax.all_gather(leg, ('low', 'mode'), axis=0, tiled=False)]
    all_to_all x0 -> x1, starting transfers between devices: none -> 6.44 us  [local(): message = lax.all_to_all(message, ('low', 'mode'), 0, 0, tiled=True)]
    unnamed x9 -> x11, local copies, waits for them, and re-layouts: 1.68 us -> 3.88 us
    all_to_all x1, starting transfers between devices: 2.95 us -> 4.54 us  [local(): alm = lax.all_to_all(alm, everyone, 0, 0, tiled=True)]
  transfers between devices with their start and end apart: 1 -> 2, of which waited for: 1 -> 1; matrix products, arithmetic and copies ran while one was open for 2% -> 2% of each run, Pallas kernels for 0% -> 0%
where the time goes in v3:
time: 81.3 us; the launch traced here: 80.9 us
  blocking collectives  41.3 us (51%)
  Pallas kernels  13.1 us (16%)
  waiting for transfers between devices  11.5 us (14%)
  starting transfers between devices  11 us (14%)
  local copies, waits for them, and re-layouts  3.88 us (5%)
    all_gather x1, blocking collectives, local(): leg = lax.all_gather(leg, ('low', 'mode'), axis=0, tiled=False)  30.6 us
    pallas_call x4, Pallas kernels, call(): pl.pallas_call(kernel, out_shape=shape, in_specs=[pl.BlockSpec(memory_spa...  13.1 us
    all_to_all x1, waiting for transfers between devices, local(): alm = lax.all_to_all(alm, everyone, 0, 0, tiled=True)  11.5 us
    all_to_all x1, blocking collectives, local(): part = lax.all_to_all(part, everyone, 0, 0, tiled=True)  10.7 us
    all_to_all x1, starting transfers between devices, local(): message = lax.all_to_all(message, ('low', 'mode'), 0, 0, tiled=True)  6.44 us
    all_to_all x1, starting transfers between devices, local(): alm = lax.all_to_all(alm, everyone, 0, 0, tiled=True)  4.54 us
    unnamed x11, local copies, waits for them, and re-layouts  3.88 us
  transfers between devices with their start and end apart: 2, of which 1 were waited for; matrix products, arithmetic and copies ran while one was open for 2% of the time, Pallas kernels for 0%

profile of v3, /device:TPU:0, one launch (start us, length us, event | category | flops | bytes accessed | tf_op | source)
XLA Modules:
  0.0 80.9 jit_solution(16434854869347430116)
XLA Ops:
  0.0 3.9 %shard_map.91 = (bf16[16,256,128]{2,1,0:T(8,128)(2,1)}, bf16[192,128]{1,0:T(8,128)(2,1)}) custom-call(bf16[8,64,1024]{2,1,0:T(8,128)(2,1)} %bitcast.17, s32[8,1024]{1,0:T(8,128)} %mask_hbm.1, f32[8,64,64]{2,1,0:T(8,128)} %bitcast.18, f32[8,4,768]{2,1,0:T(4,128)} %bitcast.19), custom_call_target="tpu_custom_call" | custom-call | flops 1342177280 | bytes 8388608 | tf_op jit(solution)/shard_map/pallas_call | solution.py:285
  3.9 0.0 copy-start.4
  3.9 0.0 copy-start.3
  3.9 6.4 %all-to-all-start = ((bf16[16,256,128]{2,1,0:T(8,128)(2,1)}), bf16[16,256,128]{2,1,0:T(8,128)(2,1)S(1)}, u32[]{:S(2)}, u32[]{:S(2)}) async-start(bf16[16,256,128]{2,1,0:T(8,128)(2,1)} %get-tuple-element.8), calls=%async_computation | async-start | bytes 2097152 | tf_op jit(solution)/shard_map/all_to_all | solution.py:349
  10.4 0.0 copy-done.4
  10.4 30.6 %all-gather = bf16[3072,128]{1,0:T(8,128)(2,1)S(1)} all-gather(bf16[192,128]{1,0:T(8,128)(2,1)S(1)} %copy-done.4), channel_id=2, replica_groups=mesh['high'=2,'low'=2,'mode'=8] {'low','mode'}, dimensions={0}, use_global_device_ids=true | all-gather | bytes 835584 | tf_op jit(solution)/shard_map/all_gather | solution.py:350
  41.0 0.0 all-to-all-done.z_ref
  41.0 0.0 copy-done.3
  41.0 0.0 copy-start.2
  41.0 2.2 %copy-done.2 = bf16[8,1024,256]{2,1,0:T(8,128)(2,1)S(1)} copy-done((bf16[8,1024,256]{2,1,0:T(8,128)(2,1)S(1)}, bf16[8,1024,256]{2,1,0:T(8,128)(2,1)}, u32[]{:S(2)}) %copy-start.2) | copy-done | bytes 4194328
  43.2 7.2 %shard_map.92 = bf16[4,8,8,768]{3,2,1,0:T(8,128)(2,1)} custom-call(f32[2,8,1024]{2,1,0:T(8,128)S(1)} %copy-done.3, bf16[8,1024,256]{2,1,0:T(8,128)(2,1)S(1)} %copy-done.2, bf16[16,192,128]{2,1,0:T(8,128)(2,1)S(1)} %bitcast.15, bf16[16,256,128]{2,1,0:T(8,128)(2,1)S(1)} %all-to-all-done.z_ref), custom_call_target="tpu_custom_call" | custom-call | flops 2147483648 | bytes 8388608 | tf_op jit(solution)/shard_map/pallas_call | solution.py:285
  50.4 4.5 %all-to-all-start.1 = ((bf16[32,8,768]{2,1,0:T(8,128)(2,1)}), bf16[32,8,768]{2,1,0:T(8,128)(2,1)S(1)}, u32[]{:S(2)}, u32[]{:S(2)}) async-start(bf16[32,8,768]{2,1,0:T(8,128)(2,1)} %bitcast.4), calls=%async_computation.1 | async-start | bytes 786432 | tf_op jit(solution)/shard_map/all_to_all | solution.py:378
  55.0 0.0 copy-start
  55.0 0.0 copy-start.1
  55.0 1.7 %copy.12 = bf16[1,768,2,512]{3,1,2,0:T(8,128)(2,1)S(1)} copy(bf16[1,768,2,512]{3,2,1,0:T(2,128)(2,1)} %param.15) | data formatting | bytes 3145728 | tf_op args[6]
  56.7 11.5 %all-to-all-done.1 = bf16[32,8,768]{2,1,0:T(8,128)(2,1)S(1)} async-done(((bf16[32,8,768]{2,1,0:T(8,128)(2,1)}), bf16[32,8,768]{2,1,0:T(8,128)(2,1)S(1)}, u32[]{:S(2)}, u32[]{:S(2)}) %all-to-all-start.1) | async-done | bytes 393248 | tf_op jit(solution)/shard_map/all_to_all | solution.py:378
  68.1 0.0 copy-done
  68.1 0.0 copy-done.1
  68.1 1.3 %shard_map.93 = f32[32,8,128]{2,1,0:T(8,128)S(1)} custom-call(bf16[2,16,8,768]{3,2,1,0:T(8,128)(2,1)S(1)} %bitcast.14, f32[1,768]{1,0:T(1,128)S(1)} %bitcast.16, f32[64,64]{1,0:T(8,128)S(1)} %copy-done, bf16[2,768,512]{2,1,0:T(8,128)(2,1)S(1)} %bitcast.13), custom_call_target="tpu_custom_call" | custom-call | tf_op jit(solution)/shard_map/pallas_call | solution.py:285
  69.5 10.7 %all_to_all.15.part_ref = f32[32,8,128]{2,1,0:T(8,128)S(1)} all-to-all(f32[32,8,128]{2,1,0:T(8,128)S(1)} %shard_map.93), channel_id=1, replica_groups=mesh['high'=2,'low'=2,'mode'=8] {'high','low','mode'}, dimensions={0} | all-to-all | bytes 262144 | tf_op jit(solution)/shard_map/all_to_all | solution.py:397
  80.2 0.7 shard_map.94
Async XLA Ops:
  3.9 6.5 %copy-start.4 = (bf16[192,128]{1,0:T(8,128)(2,1)S(1)}, bf16[192,128]{1,0:T(8,128)(2,1)}, u32[]{:S(2)}) copy-start(bf16[192,128]{1,0:T(8,128)(2,1)} %get-tuple-element.7) | copy-start | bytes 147460
  3.9 37.1 %copy-start.3 = (f32[2,8,1024]{2,1,0:T(8,128)S(1)}, f32[2,8,1024]{2,1,0:T(8,128)}, u32[]{:S(2)}) copy-start(f32[2,8,1024]{2,1,0:T(8,128)} %constant.4.clone.twiddle_ref) | copy-start | bytes 196612
  3.9 37.1 %all-to-all-start = ((bf16[16,256,128]{2,1,0:T(8,128)(2,1)}), bf16[16,256,128]{2,1,0:T(8,128)(2,1)S(1)}, u32[]{:S(2)}, u32[]{:S(2)}) async-start(bf16[16,256,128]{2,1,0:T(8,128)(2,1)} %get-tuple-element.8), calls=%async_computation | async-start | bytes 2097152 | tf_op jit(solution)/shard_map/all_to_all | solution.py:349
  41.0 2.2 %copy-start.2 = (bf16[8,1024,256]{2,1,0:T(8,128)(2,1)S(1)}, bf16[8,1024,256]{2,1,0:T(8,128)(2,1)}, u32[]{:S(2)}) copy-start(bf16[8,1024,256]{2,1,0:T(8,128)(2,1)} %constant.5.clone.table_hbm) | copy-start | bytes 12582916
  50.4 17.7 %all-to-all-start.1 = ((bf16[32,8,768]{2,1,0:T(8,128)(2,1)}), bf16[32,8,768]{2,1,0:T(8,128)(2,1)S(1)}, u32[]{:S(2)}, u32[]{:S(2)}) async-start(bf16[32,8,768]{2,1,0:T(8,128)(2,1)} %bitcast.4), calls=%async_computation.1 | async-start | bytes 786432 | tf_op jit(solution)/shard_map/all_to_all | solution.py:378
  55.0 13.2 %copy-start = (f32[64,64]{1,0:T(8,128)S(1)}, f32[64,64]{1,0:T(8,128)}, u32[]{:S(2)}) copy-start(f32[64,64]{1,0:T(8,128)} %cov_ref.1) | copy-start | bytes 49156
  55.0 13.2 %copy-start.1 = (f32[768,1]{0,1:T(1,128)S(1)}, f32[768,1]{0,1:T(1,128)}, u32[]{:S(2)}) copy-start(f32[768,1]{0,1:T(1,128)} %param.13) | copy-start | bytes 9220

commit v4 on v3

--- a/solution.py
+++ b/solution.py
@@ -119,7 +119,7 @@
         send.wait()
 
 
-def modes_kernel(width, offsets, twiddle_ref, table_hbm, leg_hbm, z_ref, out_hbm, *refs):
+def modes_kernel(width, offsets, mine_ref, twiddle_ref, table_hbm, leg_hbm, z_ref, out_hbm, *refs):
     table, left, leg_in, leg, prod_a, prod_b, x_ref, out_ref, table_sems, leg_sem, out_sems = refs
     tiles = table.shape[0]
     split = twiddle_ref.shape[1]
@@ -134,6 +134,8 @@
     count = cycles // parts * width
     high = cycles // parts * offsets
 
+    mine = mine_ref[0]
+
     def copy(tile):
         return pltpu.make_async_copy(table_hbm.at[tile], table.at[tile], table_sems.at[tile])
 
@@ -165,8 +167,10 @@
     for p in range(parts):
         for q in range(sources):
             for n in range(per):
-                rows = leg_in[p * sources + q, n * high : (n + 1) * high, :].astype(jnp.float32)
-                leg[p * high : (p + 1) * high, (q * per + n) * LANES : (q * per + n + 1) * LANES] = rows
+                place = (p * per + n) * high
+                rows = leg_in[q, place : place + high, :].astype(jnp.float32)
+                place = pl.ds(pl.multiple_of((mine + parts - p) % parts * high, high), high)
+                leg[place, (q * per + n) * LANES : (q * per + n + 1) * LANES] = rows
 
     def use(tile, prod):
         lanes = pl.ds(pl.multiple_of(tile * LANES, LANES), LANES)
@@ -347,7 +351,11 @@
         cost=(2 * cycles * chans * pixels * (pixels + 4 * chans), 8 * MIB),
     )
     message = lax.all_to_all(message, ("low", "mode"), 0, 0, tiled=True)
-    leg = lax.all_gather(leg, ("low", "mode"), axis=0, tiled=False)
+    legendre = [leg]
+    for n in range(1, pair):
+        legendre.append(lax.ppermute(leg, "low", [(i, (i + n) % pair) for i in range(pair)]))
+    leg = lax.all_gather(jnp.concatenate(legendre), "mode", axis=0, tiled=False)
+    mine = lax.axis_index("low").astype(jnp.int32).reshape(1)
 
     alm = call(
         functools.partial(modes_kernel, width, offsets),
@@ -355,7 +363,7 @@
         [
             vmem((tiles, tiles * LANES, 2 * LANES), bf16),
             vmem((pair * rows, tiles * LANES), bf16),
-            vmem((groups, legs, LANES), bf16),
+            vmem((mode_count, pair * legs, LANES), bf16),
             vmem((pair * cycles * offsets, mode_count * modes), f32),
             vmem((pair * rows, 2 * LANES), f32),
             vmem((pair * rows, 2 * LANES), f32),
@@ -365,8 +373,9 @@
             pltpu.SemaphoreType.DMA(()),
             pltpu.SemaphoreType.DMA((tiles // 2, 2 * blocks)),
         ],
-        40,
-        [vmem, hbm, hbm, vmem],
+        56,
+        [pltpu.SMEM, vmem, hbm, hbm, vmem],
+        mine,
         jnp.asarray(twiddle),
         jnp.asarray(table),
         leg,

time: 81.3 us -> 78 us (0.959)
  blocking collectives: 41.3 us -> 22.1 us
  waiting for transfers between devices: 11.5 us -> 24.9 us
  Pallas kernels: 13.1 us -> 15.6 us
  starting transfers between devices: 11 us -> 12.3 us
  local copies, waits for them, and re-layouts: 3.88 us -> 2.65 us
    all_gather x1, blocking collectives: 30.6 us -> 11.4 us  [local(): leg = lax.all_gather(jnp.concatenate(legendre), 'mode', axis=0, tiled=False)]
    ppermute x0 -> x1, waiting for transfers between devices: none -> 13.4 us  [local(): lax.ppermute(leg, 'low', [(i, (i + n) % pair) for i in range(pair)])]
    pallas_call x4, Pallas kernels: 13.1 us -> 15.6 us  [call(): pl.pallas_call(kernel, out_shape=shape, in_specs=[pl.BlockSpec(memory_spa...]
    ppermute x0 -> x1, starting transfers between devices: none -> 1.99 us  [local(): lax.ppermute(leg, 'low', [(i, (i + n) % pair) for i in range(pair)])]
    unnamed x11 -> x9, local copies, waits for them, and re-layouts: 3.88 us -> 2.65 us
  transfers between devices with their start and end apart: 2 -> 3, of which waited for: 1 -> 2; matrix products, arithmetic and copies ran while one was open for 2% -> 2% of each run, Pallas kernels for 0% -> 0%
where the time goes in v4:
time: 78 us; the launch traced here: 77.6 us
  waiting for transfers between devices  24.9 us (32%)
  blocking collectives  22.1 us (28%)
  Pallas kernels  15.6 us (20%)
  starting transfers between devices  12.3 us (16%)
  local copies, waits for them, and re-layouts  2.65 us (3%)
    pallas_call x4, Pallas kernels, call(): pl.pallas_call(kernel, out_shape=shape, in_specs=[pl.BlockSpec(memory_spa...  15.6 us
    ppermute x1, waiting for transfers between devices, local(): lax.ppermute(leg, 'low', [(i, (i + n) % pair) for i in range(pair)])  13.4 us
    all_to_all x1, waiting for transfers between devices, local(): alm = lax.all_to_all(alm, everyone, 0, 0, tiled=True)  11.5 us
    all_gather x1, blocking collectives, local(): leg = lax.all_gather(jnp.concatenate(legendre), 'mode', axis=0, tiled=False)  11.4 us
    all_to_all x1, blocking collectives, local(): part = lax.all_to_all(part, everyone, 0, 0, tiled=True)  10.7 us
    all_to_all x1, starting transfers between devices, local(): message = lax.all_to_all(message, ('low', 'mode'), 0, 0, tiled=True)  6.44 us
    all_to_all x1, starting transfers between devices, local(): alm = lax.all_to_all(alm, everyone, 0, 0, tiled=True)  3.88 us
    unnamed x9, local copies, waits for them, and re-layouts  2.65 us
  transfers between devices with their start and end apart: 3, of which 2 were waited for; matrix products, arithmetic and copies ran while one was open for 2% of the time, Pallas kernels for 0%

profile of v4, /device:TPU:0, one launch (start us, length us, event | category | flops | bytes accessed | tf_op | source)
XLA Modules:
  0.0 77.6 jit_solution(4062293739176251579)
XLA Ops:
  0.0 3.9 %shard_map.91 = (bf16[16,256,128]{2,1,0:T(8,128)(2,1)}, bf16[192,128]{1,0:T(8,128)(2,1)}) custom-call(bf16[8,64,1024]{2,1,0:T(8,128)(2,1)} %bitcast.19, s32[8,1024]{1,0:T(8,128)} %mask_hbm.1, f32[8,64,64]{2,1,0:T(8,128)} %bitcast.20, f32[8,4,768]{2,1,0:T(4,128)} %bitcast.21), custom_call_target="tpu_custom_call" | custom-call | flops 1342177280 | bytes 8388608 | tf_op jit(solution)/shard_map/pallas_call | solution.py:289
  3.9 0.0 copy-start.3
  3.9 6.4 %all-to-all-start = ((bf16[16,256,128]{2,1,0:T(8,128)(2,1)}), bf16[16,256,128]{2,1,0:T(8,128)(2,1)S(1)}, u32[]{:S(2)}, u32[]{:S(2)}) async-start(bf16[16,256,128]{2,1,0:T(8,128)(2,1)} %get-tuple-element.8), calls=%async_computation | async-start | bytes 2097152 | tf_op jit(solution)/shard_map/all_to_all | solution.py:353
  10.4 0.0 copy-done.3
  10.4 2.0 %collective-permute-start = (bf16[192,128]{1,0:T(8,128)(2,1)S(1)}, bf16[192,128]{1,0:T(8,128)(2,1)S(1)}, u32[]{:S(2)}, u32[]{:S(2)}) collective-permute-start(bf16[192,128]{1,0:T(8,128)(2,1)S(1)} %copy-done.3), channel_id=1, source_target_pairs={{0,8},{8,0},{1,9},{9,1},{2,10},{10,2},{3,11},{11,3},{4,12},{12,4},... | collective-permute-start | bytes 147464 | tf_op jit(solution)/shard_map/ppermute | solution.py:356
  12.4 13.4 %collective-permute-done = bf16[192,128]{1,0:T(8,128)(2,1)S(1)} collective-permute-done((bf16[192,128]{1,0:T(8,128)(2,1)S(1)}, bf16[192,128]{1,0:T(8,128)(2,1)S(1)}, u32[]{:S(2)}, u32[]{:S(2)}) %collective-permute-start) | collective-permute-done | bytes 49184 | tf_op jit(solution)/shard_map/ppermute | solution.py:356
  25.8 11.4 %all-gather = bf16[3072,128]{1,0:T(8,128)(2,1)} all-gather(bf16[384,128]{1,0:T(8,128)(2,1)S(1)} %pad_maximum_fusion), channel_id=2, replica_groups=mesh['high'=2,'low'=2,'mode'=8] {'mode'}, dimensions={0}, use_global_device_ids=true | all-gather | bytes 884736 | tf_op jit(solution)/shard_map/all_gather | solution.py:357
  37.2 0.0 all-to-all-done.z_ref
  37.2 0.0 copy-start.2
  37.2 1.0 %copy-done.2 = bf16[16,256,128]{2,1,0:T(8,128)(2,1)} copy-done((bf16[16,256,128]{2,1,0:T(8,128)(2,1)}, bf16[16,256,128]{2,1,0:T(8,128)(2,1)S(1)}, u32[]{:S(2)}) %copy-start.2) | copy-done | bytes 1048600
  38.2 9.6 %shard_map.92 = bf16[4,8,8,768]{3,2,1,0:T(8,128)(2,1)} custom-call(s32[1]{0:T(128)} %bitcast.mine_ref, f32[2,8,1024]{2,1,0:T(8,128)} %constant.10.clone.twiddle_ref, bf16[8,1024,256]{2,1,0:T(8,128)(2,1)} %constant.11.clone.table_hbm, bf16[8,384,128]{2,1,0:T(8,128)(2,1)} %bitcast.17, bf16[16,256,128]{2,1,0:T(8,128)(2,1)} %copy-done.2), custom_call_target="tpu_custom_call" | custom-call | flops 2147483648 | bytes 8388608 | tf_op jit(solution)/shard_map/pallas_call | solution.py:289
  47.8 3.9 %all-to-all-start.1 = ((bf16[32,8,768]{2,1,0:T(8,128)(2,1)}), bf16[32,8,768]{2,1,0:T(8,128)(2,1)S(1)}, u32[]{:S(2)}, u32[]{:S(2)}) async-start(bf16[32,8,768]{2,1,0:T(8,128)(2,1)} %bitcast.18), calls=%async_computation.1 | async-start | bytes 786432 | tf_op jit(solution)/shard_map/all_to_all | solution.py:387
  51.7 0.0 copy-start
  51.7 0.0 copy-start.1
  51.7 1.7 %copy.12 = bf16[1,768,2,512]{3,1,2,0:T(8,128)(2,1)S(1)} copy(bf16[1,768,2,512]{3,2,1,0:T(2,128)(2,1)} %param.15) | data formatting | bytes 3145728 | tf_op args[6]
  53.4 11.5 %all-to-all-done.1 = bf16[32,8,768]{2,1,0:T(8,128)(2,1)S(1)} async-done(((bf16[32,8,768]{2,1,0:T(8,128)(2,1)}), bf16[32,8,768]{2,1,0:T(8,128)(2,1)S(1)}, u32[]{:S(2)}, u32[]{:S(2)}) %all-to-all-start.1) | async-done | bytes 393248 | tf_op jit(solution)/shard_map/all_to_all | solution.py:387
  64.9 0.0 copy-done
  64.9 0.0 copy-done.1
  64.9 1.3 %shard_map.93 = f32[32,8,128]{2,1,0:T(8,128)S(1)} custom-call(bf16[2,16,8,768]{3,2,1,0:T(8,128)(2,1)S(1)} %bitcast.15, f32[1,768]{1,0:T(1,128)S(1)} %bitcast.16, f32[64,64]{1,0:T(8,128)S(1)} %copy-done, bf16[2,768,512]{2,1,0:T(8,128)(2,1)S(1)} %bitcast.14), custom_call_target="tpu_custom_call" | custom-call | tf_op jit(solution)/shard_map/pallas_call | solution.py:289
  66.2 10.7 %all_to_all.15.part_ref = f32[32,8,128]{2,1,0:T(8,128)S(1)} all-to-all(f32[32,8,128]{2,1,0:T(8,128)S(1)} %shard_map.93), channel_id=1, replica_groups=mesh['high'=2,'low'=2,'mode'=8] {'high','low','mode'}, dimensions={0} | all-to-all | bytes 262144 | tf_op jit(solution)/shard_map/all_to_all | solution.py:406
  76.9 0.7 shard_map.94
  (1 shorter events, 0.0 us)
Async XLA Ops:
  3.9 6.5 %copy-start.3 = (bf16[192,128]{1,0:T(8,128)(2,1)S(1)}, bf16[192,128]{1,0:T(8,128)(2,1)}, u32[]{:S(2)}) copy-start(bf16[192,128]{1,0:T(8,128)(2,1)} %get-tuple-element.7) | copy-start | bytes 147460
  3.9 33.3 %all-to-all-start = ((bf16[16,256,128]{2,1,0:T(8,128)(2,1)}), bf16[16,256,128]{2,1,0:T(8,128)(2,1)S(1)}, u32[]{:S(2)}, u32[]{:S(2)}) async-start(bf16[16,256,128]{2,1,0:T(8,128)(2,1)} %get-tuple-element.8), calls=%async_computation | async-start | bytes 2097152 | tf_op jit(solution)/shard_map/all_to_all | solution.py:353
  10.4 15.4 %collective-permute-start = (bf16[192,128]{1,0:T(8,128)(2,1)S(1)}, bf16[192,128]{1,0:T(8,128)(2,1)S(1)}, u32[]{:S(2)}, u32[]{:S(2)}) collective-permute-start(bf16[192,128]{1,0:T(8,128)(2,1)S(1)} %copy-done.3), channel_id=1, source_target_pairs={{0,8},{8,0},{1,9},{9,1},{2,10},{10,2},{3,11},{11,3},{4,12},{12,4},... | collective-permute-start | bytes 147464 | tf_op jit(solution)/shard_map/ppermute | solution.py:356
  37.2 1.0 %copy-start.2 = (bf16[16,256,128]{2,1,0:T(8,128)(2,1)}, bf16[16,256,128]{2,1,0:T(8,128)(2,1)S(1)}, u32[]{:S(2)}) copy-start(bf16[16,256,128]{2,1,0:T(8,128)(2,1)S(1)} %all-to-all-done.z_ref) | copy-start | bytes 3145732
  47.8 17.1 %all-to-all-start.1 = ((bf16[32,8,768]{2,1,0:T(8,128)(2,1)}), bf16[32,8,768]{2,1,0:T(8,128)(2,1)S(1)}, u32[]{:S(2)}, u32[]{:S(2)}) async-start(bf16[32,8,768]{2,1,0:T(8,128)(2,1)} %bitcast.18), calls=%async_computation.1 | async-start | bytes 786432 | tf_op jit(solution)/shard_map/all_to_all | solution.py:387
  51.7 13.2 %copy-start = (f32[64,64]{1,0:T(8,128)S(1)}, f32[64,64]{1,0:T(8,128)}, u32[]{:S(2)}) copy-start(f32[64,64]{1,0:T(8,128)} %cov_ref.1) | copy-start | bytes 49156
  51.7 13.2 %copy-start.1 = (f32[768,1]{0,1:T(1,128)S(1)}, f32[768,1]{0,1:T(1,128)}, u32[]{:S(2)}) copy-start(f32[768,1]{0,1:T(1,128)} %param.13) | copy-start | bytes 9220

commit v5 on v3

--- a/solution.py
+++ b/solution.py
@@ -119,8 +119,23 @@
         send.wait()
 
 
-def modes_kernel(width, offsets, twiddle_ref, table_hbm, leg_hbm, z_ref, out_hbm, *refs):
-    table, left, leg_in, leg, prod_a, prod_b, x_ref, out_ref, table_sems, leg_sem, out_sems = refs
+def legendre_kernel(mine_ref, own_ref, *refs):
+    out_ref = refs[-1]
+    mine, pair, high = mine_ref[0], len(refs), own_ref.shape[0]
+
+    def place(n):
+        return pl.ds(pl.multiple_of((mine + pair - n) % pair * high, high), high)
+
+    out_ref[place(0), :] = own_ref[...]
+    for n in range(1, pair):
+        leg = refs[n - 1]
+        rows = jnp.concatenate([leg[r] for r in range(leg.shape[0])], axis=0).astype(jnp.bfloat16)
+        tiles = [rows[:, n * LANES : (n + 1) * LANES] for n in range(rows.shape[1] // LANES)]
+        out_ref[place(n), :] = jnp.concatenate(tiles, axis=0)
+
+
+def modes_kernel(width, offsets, twiddle_ref, table_hbm, leg_in, z_ref, out_hbm, *refs):
+    table, left, leg, prod_a, prod_b, x_ref, out_ref, table_sems, out_sems = refs
     tiles = table.shape[0]
     split = twiddle_ref.shape[1]
     tall = x_ref.shape[3]
@@ -144,8 +159,6 @@
         return pltpu.make_async_copy(out_ref.at[where], out_hbm.at[where], out_sems.at[step, n])
 
     copy(0).start()
-    leg_copy = pltpu.make_async_copy(leg_hbm, leg_in, leg_sem)
-    leg_copy.start()
     copy(1).start()
     for p in range(parts):
         for q in range(sources):
@@ -161,11 +174,11 @@
 
     copy(0).wait()
     product(0, prod_a)
-    leg_copy.wait()
     for p in range(parts):
         for q in range(sources):
             for n in range(per):
-                rows = leg_in[p * sources + q, n * high : (n + 1) * high, :].astype(jnp.float32)
+                place = (p * per + n) * high
+                rows = leg_in[q, place : place + high, :].astype(jnp.float32)
                 leg[p * high : (p + 1) * high, (q * per + n) * LANES : (q * per + n + 1) * LANES] = rows
 
     def use(tile, prod):
@@ -323,6 +336,9 @@
     hbm, vmem, bf16, f32, shape = pl.ANY, pltpu.VMEM, jnp.bfloat16, jnp.float32, jax.ShapeDtypeStruct
     twiddle, table = transform_tables(split, pixels * mode_count)
 
+    own_leg = jnp.transpose(cycle_legendre, (0, 2, 1))
+    others = [lax.ppermute(own_leg, "low", [(i, (i + n) % pair) for i in range(pair)]) for n in range(1, pair)]
+
     message, leg = call(
         whiten_kernel,
         [shape((groups, rows, LANES), bf16), shape((legs, LANES), bf16)],
@@ -342,12 +358,22 @@
         jnp.transpose(sky_map, (0, 2, 1)),
         pixel_mask,
         noise_factor[:, 0],
-        jnp.transpose(cycle_legendre, (0, 2, 1)),
+        own_leg,
         out_space=hbm,
         cost=(2 * cycles * chans * pixels * (pixels + 4 * chans), 8 * MIB),
     )
     message = lax.all_to_all(message, ("low", "mode"), 0, 0, tiled=True)
-    leg = lax.all_gather(leg, ("low", "mode"), axis=0, tiled=False)
+    leg = call(
+        legendre_kernel,
+        shape((pair * legs, LANES), bf16),
+        [],
+        16,
+        [pltpu.SMEM] + [vmem] * pair,
+        lax.axis_index("low").astype(jnp.int32).reshape(1),
+        leg,
+        *others,
+    )
+    leg = lax.all_gather(leg, "mode", axis=0, tiled=False)
 
     alm = call(
         functools.partial(modes_kernel, width, offsets),
@@ -355,18 +381,16 @@
         [
             vmem((tiles, tiles * LANES, 2 * LANES), bf16),
             vmem((pair * rows, tiles * LANES), bf16),
-            vmem((groups, legs, LANES), bf16),
             vmem((pair * cycles * offsets, mode_count * modes), f32),
             vmem((pair * rows, 2 * LANES), f32),
             vmem((pair * rows, 2 * LANES), f32),
             vmem((blocks, 2, pair * cycles // group, group * width, LANES), f32),
             vmem((offsets, mode_count, 2 * width, modes), bf16),
             pltpu.SemaphoreType.DMA((tiles,)),
-            pltpu.SemaphoreType.DMA(()),
             pltpu.SemaphoreType.DMA((tiles // 2, 2 * blocks)),
         ],
         40,
-        [vmem, hbm, hbm, vmem],
+        [vmem, hbm, vmem, vmem],
         jnp.asarray(twiddle),
         jnp.asarray(table),
         leg,

time: 81.3 us -> 76.8 us (0.945)
  blocking collectives: 41.3 us -> 21.1 us
  waiting for transfers between devices: 11.5 us -> 26 us
  starting transfers between devices: 11 us -> 12.3 us
    all_gather x1, blocking collectives: 30.6 us -> 10.4 us  [local(): leg = lax.all_gather(leg, 'mode', axis=0, tiled=False)]
    ppermute x0 -> x1, waiting for transfers between devices: none -> 14.5 us  [local(): lax.ppermute(own_leg, 'low', [(i, (i + n) % pair) for i in range(pair)])]
    ppermute x0 -> x1, starting transfers between devices: none -> 1.99 us  [local(): lax.ppermute(own_leg, 'low', [(i, (i + n) % pair) for i in range(pair)])]
    pallas_call x4 -> x5, Pallas kernels: 13.1 us -> 13.1 us  [call(): pl.pallas_call(kernel, out_shape=shape, in_specs=[pl.BlockSpec(memory_spa...]
    unnamed x11 -> x13, local copies, waits for them, and re-layouts: 3.88 us -> 3.89 us
  transfers between devices with their start and end apart: 2 -> 3, of which waited for: 1 -> 2; matrix products, arithmetic and copies ran while one was open for 2% -> 2% of each run, Pallas kernels for 0% -> 0%
where the time goes in v5:
time: 76.8 us; the launch traced here: 76.4 us
  waiting for transfers between devices  26 us (34%)
  blocking collectives  21.1 us (27%)
  Pallas kernels  13.1 us (17%)
  starting transfers between devices  12.3 us (16%)
  local copies, waits for them, and re-layouts  3.89 us (5%)
    ppermute x1, waiting for transfers between devices, local(): lax.ppermute(own_leg, 'low', [(i, (i + n) % pair) for i in range(pair)])  14.5 us
    pallas_call x5, Pallas kernels, call(): pl.pallas_call(kernel, out_shape=shape, in_specs=[pl.BlockSpec(memory_spa...  13.1 us
    all_to_all x1, waiting for transfers between devices, local(): alm = lax.all_to_all(alm, everyone, 0, 0, tiled=True)  11.5 us
    all_to_all x1, blocking collectives, local(): part = lax.all_to_all(part, everyone, 0, 0, tiled=True)  10.7 us
    all_gather x1, blocking collectives, local(): leg = lax.all_gather(leg, 'mode', axis=0, tiled=False)  10.4 us
    all_to_all x1, starting transfers between devices, local(): message = lax.all_to_all(message, ('low', 'mode'), 0, 0, tiled=True)  6.44 us
    unnamed x13, local copies, waits for them, and re-layouts  3.89 us
    all_to_all x1, starting transfers between devices, local(): alm = lax.all_to_all(alm, everyone, 0, 0, tiled=True)  3.88 us
  transfers between devices with their start and end apart: 3, of which 2 were waited for; matrix products, arithmetic and copies ran while one was open for 2% of the time, Pallas kernels for 0%

profile of v5, /device:TPU:0, one launch (start us, length us, event | category | flops | bytes accessed | tf_op | source)
XLA Modules:
  0.0 76.4 jit_solution(12350903724953310959)
XLA Ops:
  0.0 3.9 %shard_map.91 = (bf16[16,256,128]{2,1,0:T(8,128)(2,1)}, bf16[192,128]{1,0:T(8,128)(2,1)}) custom-call(bf16[8,64,1024]{2,1,0:T(8,128)(2,1)} %bitcast.18, s32[8,1024]{1,0:T(8,128)} %mask_hbm.1, f32[8,64,64]{2,1,0:T(8,128)} %bitcast.19, f32[8,4,768]{2,1,0:T(4,128)} %bitcast.20), custom_call_target="tpu_custom_call" | custom-call | flops 1342177280 | bytes 8388608 | tf_op jit(solution)/shard_map/pallas_call | solution.py:298
  3.9 0.0 copy-start.5
  3.9 0.0 copy-start
  4.0 0.0 copy-start.4
  4.0 6.4 %all-to-all-start = ((bf16[16,256,128]{2,1,0:T(8,128)(2,1)}), bf16[16,256,128]{2,1,0:T(8,128)(2,1)S(1)}, u32[]{:S(2)}, u32[]{:S(2)}) async-start(bf16[16,256,128]{2,1,0:T(8,128)(2,1)} %get-tuple-element.8), calls=%async_computation | async-start | bytes 2097152 | tf_op jit(solution)/shard_map/all_to_all | solution.py:365
  10.4 0.0 copy-done.5
  10.4 2.0 %collective-permute-start = (f32[8,4,768]{2,1,0:T(4,128)S(1)}, f32[8,4,768]{2,1,0:T(4,128)S(1)}, u32[]{:S(2)}, u32[]{:S(2)}) collective-permute-start(f32[8,4,768]{2,1,0:T(4,128)S(1)} %bitcast.21), channel_id=1, source_target_pairs={{0,8},{8,0},{1,9},{9,1},{2,10},{10,2},{3,11},{11,3},{4,12},{12,4},... | collective-permute-start | bytes 294920 | tf_op jit(solution)/shard_map/ppermute | solution.py:340
  12.4 14.5 %collective-permute-done.refs_0_ = f32[8,4,768]{2,1,0:T(4,128)S(1)} collective-permute-done((f32[8,4,768]{2,1,0:T(4,128)S(1)}, f32[8,4,768]{2,1,0:T(4,128)S(1)}, u32[]{:S(2)}, u32[]{:S(2)}) %collective-permute-start) | collective-permute-done | bytes 98336 | tf_op jit(solution)/shard_map/ppermute | solution.py:340
  26.9 0.0 copy-done
  26.9 10.4 %all-gather = bf16[3072,128]{1,0:T(8,128)(2,1)S(1)} all-gather(bf16[384,128]{1,0:T(8,128)(2,1)S(1)} %shard_map.92), channel_id=2, replica_groups=mesh['high'=2,'low'=2,'mode'=8] {'mode'}, dimensions={0}, use_global_device_ids=true | all-gather | bytes 884736 | tf_op jit(solution)/shard_map/all_gather | solution.py:376
  37.3 0.0 all-to-all-done.z_ref
  37.3 0.0 copy-done.4
  37.3 0.0 copy-start.3
  37.3 2.2 %copy-done.3 = bf16[8,1024,256]{2,1,0:T(8,128)(2,1)S(1)} copy-done((bf16[8,1024,256]{2,1,0:T(8,128)(2,1)S(1)}, bf16[8,1024,256]{2,1,0:T(8,128)(2,1)}, u32[]{:S(2)}) %copy-start.3) | copy-done | bytes 4194328
  39.5 7.1 %shard_map.93 = bf16[4,8,8,768]{3,2,1,0:T(8,128)(2,1)} custom-call(f32[2,8,1024]{2,1,0:T(8,128)S(1)} %copy-done.4, bf16[8,1024,256]{2,1,0:T(8,128)(2,1)S(1)} %copy-done.3, bf16[8,384,128]{2,1,0:T(8,128)(2,1)S(1)} %bitcast.16, bf16[16,256,128]{2,1,0:T(8,128)(2,1)S(1)} %all-to-all-done.z_ref), custom_call_target="tpu_custom_call" | custom-call | flops 2147483648 | bytes 8388608 | tf_op jit(solution)/shard_map/pallas_call | solution.py:298
  46.6 3.9 %all-to-all-start.1 = ((bf16[32,8,768]{2,1,0:T(8,128)(2,1)}), bf16[32,8,768]{2,1,0:T(8,128)(2,1)S(1)}, u32[]{:S(2)}, u32[]{:S(2)}) async-start(bf16[32,8,768]{2,1,0:T(8,128)(2,1)} %bitcast.5), calls=%async_computation.1 | async-start | bytes 786432 | tf_op jit(solution)/shard_map/all_to_all | solution.py:402
  50.5 0.0 copy-start.1
  50.5 0.0 copy-start.2
  50.5 1.7 %copy.12 = bf16[1,768,2,512]{3,1,2,0:T(8,128)(2,1)S(1)} copy(bf16[1,768,2,512]{3,2,1,0:T(2,128)(2,1)} %param.15) | data formatting | bytes 3145728 | tf_op args[6]
  52.2 11.5 %all-to-all-done.1 = bf16[32,8,768]{2,1,0:T(8,128)(2,1)S(1)} async-done(((bf16[32,8,768]{2,1,0:T(8,128)(2,1)}), bf16[32,8,768]{2,1,0:T(8,128)(2,1)S(1)}, u32[]{:S(2)}, u32[]{:S(2)}) %all-to-all-start.1) | async-done | bytes 393248 | tf_op jit(solution)/shard_map/all_to_all | solution.py:402
  63.6 0.0 copy-done.1
  63.6 0.0 copy-done.2
  63.6 1.3 %shard_map.94 = f32[32,8,128]{2,1,0:T(8,128)S(1)} custom-call(bf16[2,16,8,768]{3,2,1,0:T(8,128)(2,1)S(1)} %bitcast.15, f32[1,768]{1,0:T(1,128)S(1)} %bitcast.17, f32[64,64]{1,0:T(8,128)S(1)} %copy-done.1, bf16[2,768,512]{2,1,0:T(8,128)(2,1)S(1)} %bitcast.14), custom_call_target="tpu_custom_call" | custom-call | tf_op jit(solution)/shard_map/pallas_call | solution.py:298
  65.0 10.7 %all_to_all.15.part_ref = f32[32,8,128]{2,1,0:T(8,128)S(1)} all-to-all(f32[32,8,128]{2,1,0:T(8,128)S(1)} %shard_map.94), channel_id=1, replica_groups=mesh['high'=2,'low'=2,'mode'=8] {'high','low','mode'}, dimensions={0} | all-to-all | bytes 262144 | tf_op jit(solution)/shard_map/all_to_all | solution.py:421
  75.7 0.7 shard_map.95
  (1 shorter events, 0.0 us)
Async XLA Ops:
  3.9 6.5 %copy-start.5 = (f32[8,768,4]{1,2,0:T(4,128)S(1)}, f32[8,768,4]{1,2,0:T(4,128)}, u32[]{:S(2)}) copy-start(f32[8,768,4]{1,2,0:T(4,128)} %param.12) | copy-start | bytes 294916
  3.9 22.9 %copy-start = (bf16[192,128]{1,0:T(8,128)(2,1)S(1)}, bf16[192,128]{1,0:T(8,128)(2,1)}, u32[]{:S(2)}) copy-start(bf16[192,128]{1,0:T(8,128)(2,1)} %get-tuple-element.7.own_ref) | copy-start | bytes 147460
  4.0 33.3 %copy-start.4 = (f32[2,8,1024]{2,1,0:T(8,128)S(1)}, f32[2,8,1024]{2,1,0:T(8,128)}, u32[]{:S(2)}) copy-start(f32[2,8,1024]{2,1,0:T(8,128)} %constant.10.clone.twiddle_ref) | copy-start | bytes 196612
  4.0 33.3 %all-to-all-start = ((bf16[16,256,128]{2,1,0:T(8,128)(2,1)}), bf16[16,256,128]{2,1,0:T(8,128)(2,1)S(1)}, u32[]{:S(2)}, u32[]{:S(2)}) async-start(bf16[16,256,128]{2,1,0:T(8,128)(2,1)} %get-tuple-element.8), calls=%async_computation | async-start | bytes 2097152 | tf_op jit(solution)/shard_map/all_to_all | solution.py:365
  10.4 16.5 %collective-permute-start = (f32[8,4,768]{2,1,0:T(4,128)S(1)}, f32[8,4,768]{2,1,0:T(4,128)S(1)}, u32[]{:S(2)}, u32[]{:S(2)}) collective-permute-start(f32[8,4,768]{2,1,0:T(4,128)S(1)} %bitcast.21), channel_id=1, source_target_pairs={{0,8},{8,0},{1,9},{9,1},{2,10},{10,2},{3,11},{11,3},{4,12},{12,4},... | collective-permute-start | bytes 294920 | tf_op jit(solution)/shard_map/ppermute | solution.py:340
  37.3 2.2 %copy-start.3 = (bf16[8,1024,256]{2,1,0:T(8,128)(2,1)S(1)}, bf16[8,1024,256]{2,1,0:T(8,128)(2,1)}, u32[]{:S(2)}) copy-start(bf16[8,1024,256]{2,1,0:T(8,128)(2,1)} %constant.11.clone.table_hbm) | copy-start | bytes 12582916
  46.6 17.1 %all-to-all-start.1 = ((bf16[32,8,768]{2,1,0:T(8,128)(2,1)}), bf16[32,8,768]{2,1,0:T(8,128)(2,1)S(1)}, u32[]{:S(2)}, u32[]{:S(2)}) async-start(bf16[32,8,768]{2,1,0:T(8,128)(2,1)} %bitcast.5), calls=%async_computation.1 | async-start | bytes 786432 | tf_op jit(solution)/shard_map/all_to_all | solution.py:402
  50.5 13.2 %copy-start.1 = (f32[64,64]{1,0:T(8,128)S(1)}, f32[64,64]{1,0:T(8,128)}, u32[]{:S(2)}) copy-start(f32[64,64]{1,0:T(8,128)} %cov_ref.1) | copy-start | bytes 49156
  50.5 13.2 %copy-start.2 = (f32[768,1]{0,1:T(1,128)S(1)}, f32[768,1]{0,1:T(1,128)}, u32[]{:S(2)}) copy-start(f32[768,1]{0,1:T(1,128)} %param.13) | copy-start | bytes 9220

commit v6 on v5

--- a/solution.py
+++ b/solution.py
@@ -46,7 +46,7 @@
     return out
 
 
-def whiten_kernel(sky_hbm, mask_hbm, factor_hbm, leg_hbm, out_hbm, leg_out, *refs):
+def whiten_kernel(sky_hbm, mask_hbm, factor_hbm, leg_hbm, after_hbm, out_hbm, leg_out, *refs):
     sky, mask, factor, leg, sort, white, stage, leg_rows, sems = refs
     cycles, chans, pixels = sky.shape
     groups = stage.shape[0]
@@ -354,11 +354,12 @@
             pltpu.SemaphoreType.DMA((5 + split // 2,)),
         ],
         56,
-        [hbm] * 4,
+        [hbm] * 5,
         jnp.transpose(sky_map, (0, 2, 1)),
         pixel_mask,
         noise_factor[:, 0],
         own_leg,
+        others[0],
         out_space=hbm,
         cost=(2 * cycles * chans * pixels * (pixels + 4 * chans), 8 * MIB),
     )

time: 76.8 us -> 77.2 us (level)
  waiting for transfers between devices: 26 us -> 14.5 us
  blocking collectives: 21.1 us -> 31.4 us
  starting transfers between devices: 12.3 us -> 13.2 us
    ppermute x1, waiting for transfers between devices: 14.5 us -> 3 us  [local(): lax.ppermute(own_leg, 'low', [(i, (i + n) % pair) for i in range(pair)])]
    all_gather x1, blocking collectives: 10.4 us -> 20.7 us  [local(): leg = lax.all_gather(leg, 'mode', axis=0, tiled=False)]
    all_to_all x1, starting transfers between devices: 6.44 us -> 5.23 us  [local(): message = lax.all_to_all(message, ('low', 'mode'), 0, 0, tiled=True)]
    all_to_all x1, starting transfers between devices: 3.88 us -> 4.92 us  [local(): alm = lax.all_to_all(alm, everyone, 0, 0, tiled=True)]
    ppermute x1, starting transfers between devices: 1.99 us -> 3.02 us  [local(): lax.ppermute(own_leg, 'low', [(i, (i + n) % pair) for i in range(pair)])]
    unnamed x13 -> x15, local copies, waits for them, and re-layouts: 3.89 us -> 4.51 us
where the time goes in v6:
time: 77.2 us; the launch traced here: 76.8 us
  blocking collectives  31.4 us (41%)
  waiting for transfers between devices  14.5 us (19%)
  starting transfers between devices  13.2 us (17%)
  Pallas kernels  13.1 us (17%)
  local copies, waits for them, and re-layouts  4.51 us (6%)
    all_gather x1, blocking collectives, local(): leg = lax.all_gather(leg, 'mode', axis=0, tiled=False)  20.7 us
    pallas_call x5, Pallas kernels, call(): pl.pallas_call(kernel, out_shape=shape, in_specs=[pl.BlockSpec(memory_spa...  13.1 us
    all_to_all x1, waiting for transfers between devices, local(): alm = lax.all_to_all(alm, everyone, 0, 0, tiled=True)  11.5 us
    all_to_all x1, blocking collectives, local(): part = lax.all_to_all(part, everyone, 0, 0, tiled=True)  10.7 us
    all_to_all x1, starting transfers between devices, local(): message = lax.all_to_all(message, ('low', 'mode'), 0, 0, tiled=True)  5.23 us
    all_to_all x1, starting transfers between devices, local(): alm = lax.all_to_all(alm, everyone, 0, 0, tiled=True)  4.92 us
    unnamed x15, local copies, waits for them, and re-layouts  4.51 us
    ppermute x1, starting transfers between devices, local(): lax.ppermute(own_leg, 'low', [(i, (i + n) % pair) for i in range(pair)])  3.02 us
  transfers between devices with their start and end apart: 3, of which 2 were waited for; matrix products, arithmetic and copies ran while one was open for 2% of the time, Pallas kernels for 0%

profile of v6, /device:TPU:0, one launch (start us, length us, event | category | flops | bytes accessed | tf_op | source)
XLA Modules:
  0.0 76.8 jit_solution(15452338757848463198)
XLA Ops:
  0.0 3.0 %collective-permute-start = (f32[8,4,768]{2,1,0:T(4,128)}, f32[8,4,768]{2,1,0:T(4,128)S(1)}, u32[]{:S(2)}, u32[]{:S(2)}) collective-permute-start(f32[8,4,768]{2,1,0:T(4,128)} %bitcast.20), channel_id=1, source_target_pairs={{0,8},{8,0},{1,9},{9,1},{2,10},{10,2},{3,11},{11,3},{4,12},{12,4},... | collective-permute-start | bytes 294920 | tf_op jit(solution)/shard_map/ppermute | solution.py:340
  3.0 3.0 %collective-permute-done.after_hbm.refs_0_ = f32[8,4,768]{2,1,0:T(4,128)S(1)} collective-permute-done((f32[8,4,768]{2,1,0:T(4,128)}, f32[8,4,768]{2,1,0:T(4,128)S(1)}, u32[]{:S(2)}, u32[]{:S(2)}) %collective-permute-start) | collective-permute-done | bytes 98336 | tf_op jit(solution)/shard_map/ppermute | solution.py:340
  6.0 0.0 copy-start
  6.0 0.6 copy-done
  6.7 3.9 %shard_map.91 = (bf16[16,256,128]{2,1,0:T(8,128)(2,1)}, bf16[192,128]{1,0:T(8,128)(2,1)}) custom-call(bf16[8,64,1024]{2,1,0:T(8,128)(2,1)} %bitcast.18, s32[8,1024]{1,0:T(8,128)} %mask_hbm.1, f32[8,64,64]{2,1,0:T(8,128)} %bitcast.19, f32[8,4,768]{2,1,0:T(4,128)} %bitcast.21, f32[8,4,768]{2,1,0:T(4,128)} %copy-done), custom_call_target="tpu_custom_call" | custom-call | flops 1342177280 | bytes 8388608 | tf_op jit(solution)/shard_map/pallas_call | solution.py:298
  10.6 0.0 copy-start.1
  10.6 0.0 copy-start.2
  10.6 0.0 copy-start.6
  10.6 5.2 %all-to-all-start = ((bf16[16,256,128]{2,1,0:T(8,128)(2,1)}), bf16[16,256,128]{2,1,0:T(8,128)(2,1)S(1)}, u32[]{:S(2)}, u32[]{:S(2)}) async-start(bf16[16,256,128]{2,1,0:T(8,128)(2,1)} %get-tuple-element.8), calls=%async_computation | async-start | bytes 2097152 | tf_op jit(solution)/shard_map/all_to_all | solution.py:366
  15.9 0.0 copy-done.1
  15.9 0.0 copy-done.2
  15.9 20.7 %all-gather = bf16[3072,128]{1,0:T(8,128)(2,1)S(1)} all-gather(bf16[384,128]{1,0:T(8,128)(2,1)S(1)} %shard_map.92), channel_id=2, replica_groups=mesh['high'=2,'low'=2,'mode'=8] {'mode'}, dimensions={0}, use_global_device_ids=true | all-gather | bytes 884736 | tf_op jit(solution)/shard_map/all_gather | solution.py:377
  36.7 0.0 all-to-all-done.z_ref
  36.7 0.0 copy-done.6
  36.7 0.0 copy-start.5
  36.7 2.2 %copy-done.5 = bf16[8,1024,256]{2,1,0:T(8,128)(2,1)S(1)} copy-done((bf16[8,1024,256]{2,1,0:T(8,128)(2,1)S(1)}, bf16[8,1024,256]{2,1,0:T(8,128)(2,1)}, u32[]{:S(2)}) %copy-start.5) | copy-done | bytes 4194328
  38.9 7.1 %shard_map.93 = bf16[4,8,8,768]{3,2,1,0:T(8,128)(2,1)} custom-call(f32[2,8,1024]{2,1,0:T(8,128)S(1)} %copy-done.6, bf16[8,1024,256]{2,1,0:T(8,128)(2,1)S(1)} %copy-done.5, bf16[8,384,128]{2,1,0:T(8,128)(2,1)S(1)} %bitcast.16, bf16[16,256,128]{2,1,0:T(8,128)(2,1)S(1)} %all-to-all-done.z_ref), custom_call_target="tpu_custom_call" | custom-call | flops 2147483648 | bytes 8388608 | tf_op jit(solution)/shard_map/pallas_call | solution.py:298
  45.9 4.9 %all-to-all-start.1 = ((bf16[32,8,768]{2,1,0:T(8,128)(2,1)}), bf16[32,8,768]{2,1,0:T(8,128)(2,1)S(1)}, u32[]{:S(2)}, u32[]{:S(2)}) async-start(bf16[32,8,768]{2,1,0:T(8,128)(2,1)} %bitcast.5), calls=%async_computation.1 | async-start | bytes 786432 | tf_op jit(solution)/shard_map/all_to_all | solution.py:403
  50.9 0.0 copy-start.3
  50.9 0.0 copy-start.4
  50.9 1.7 %copy.12 = bf16[1,768,2,512]{3,1,2,0:T(8,128)(2,1)S(1)} copy(bf16[1,768,2,512]{3,2,1,0:T(2,128)(2,1)} %param.15) | data formatting | bytes 3145728 | tf_op args[6]
  52.6 11.5 %all-to-all-done.1 = bf16[32,8,768]{2,1,0:T(8,128)(2,1)S(1)} async-done(((bf16[32,8,768]{2,1,0:T(8,128)(2,1)}), bf16[32,8,768]{2,1,0:T(8,128)(2,1)S(1)}, u32[]{:S(2)}, u32[]{:S(2)}) %all-to-all-start.1) | async-done | bytes 393248 | tf_op jit(solution)/shard_map/all_to_all | solution.py:403
  64.0 0.0 copy-done.3
  64.1 0.0 copy-done.4
  64.1 1.3 %shard_map.94 = f32[32,8,128]{2,1,0:T(8,128)S(1)} custom-call(bf16[2,16,8,768]{3,2,1,0:T(8,128)(2,1)S(1)} %bitcast.15, f32[1,768]{1,0:T(1,128)S(1)} %bitcast.17, f32[64,64]{1,0:T(8,128)S(1)} %copy-done.3, bf16[2,768,512]{2,1,0:T(8,128)(2,1)S(1)} %bitcast.14), custom_call_target="tpu_custom_call" | custom-call | tf_op jit(solution)/shard_map/pallas_call | solution.py:298
  65.4 10.7 %all_to_all.15.part_ref = f32[32,8,128]{2,1,0:T(8,128)S(1)} all-to-all(f32[32,8,128]{2,1,0:T(8,128)S(1)} %shard_map.94), channel_id=1, replica_groups=mesh['high'=2,'low'=2,'mode'=8] {'high','low','mode'}, dimensions={0} | all-to-all | bytes 262144 | tf_op jit(solution)/shard_map/all_to_all | solution.py:422
  76.1 0.7 shard_map.95
  (1 shorter events, 0.0 us)
Async XLA Ops:
  0.0 6.0 %collective-permute-start = (f32[8,4,768]{2,1,0:T(4,128)}, f32[8,4,768]{2,1,0:T(4,128)S(1)}, u32[]{:S(2)}, u32[]{:S(2)}) collective-permute-start(f32[8,4,768]{2,1,0:T(4,128)} %bitcast.20), channel_id=1, source_target_pairs={{0,8},{8,0},{1,9},{9,1},{2,10},{10,2},{3,11},{11,3},{4,12},{12,4},... | collective-permute-start | bytes 294920 | tf_op jit(solution)/shard_map/ppermute | solution.py:340
  6.0 0.6 copy-start
  10.6 5.3 %copy-start.1 = (f32[8,4,768]{2,1,0:T(4,128)S(1)}, f32[8,4,768]{2,1,0:T(4,128)}, u32[]{:S(2)}) copy-start(f32[8,4,768]{2,1,0:T(4,128)} %copy-done) | copy-start | bytes 294916
  10.6 5.3 %copy-start.2 = (bf16[192,128]{1,0:T(8,128)(2,1)S(1)}, bf16[192,128]{1,0:T(8,128)(2,1)}, u32[]{:S(2)}) copy-start(bf16[192,128]{1,0:T(8,128)(2,1)} %get-tuple-element.7.own_ref) | copy-start | bytes 147460
  10.6 26.1 %copy-start.6 = (f32[2,8,1024]{2,1,0:T(8,128)S(1)}, f32[2,8,1024]{2,1,0:T(8,128)}, u32[]{:S(2)}) copy-start(f32[2,8,1024]{2,1,0:T(8,128)} %constant.10.clone.twiddle_ref) | copy-start | bytes 196612
  10.6 26.0 %all-to-all-start = ((bf16[16,256,128]{2,1,0:T(8,128)(2,1)}), bf16[16,256,128]{2,1,0:T(8,128)(2,1)S(1)}, u32[]{:S(2)}, u32[]{:S(2)}) async-start(bf16[16,256,128]{2,1,0:T(8,128)(2,1)} %get-tuple-element.8), calls=%async_computation | async-start | bytes 2097152 | tf_op jit(solution)/shard_map/all_to_all | solution.py:366
  36.7 2.2 %copy-start.5 = (bf16[8,1024,256]{2,1,0:T(8,128)(2,1)S(1)}, bf16[8,1024,256]{2,1,0:T(8,128)(2,1)}, u32[]{:S(2)}) copy-start(bf16[8,1024,256]{2,1,0:T(8,128)(2,1)} %constant.11.clone.table_hbm) | copy-start | bytes 12582916
  45.9 18.1 %all-to-all-start.1 = ((bf16[32,8,768]{2,1,0:T(8,128)(2,1)}), bf16[32,8,768]{2,1,0:T(8,128)(2,1)S(1)}, u32[]{:S(2)}, u32[]{:S(2)}) async-start(bf16[32,8,768]{2,1,0:T(8,128)(2,1)} %bitcast.5), calls=%async_computation.1 | async-start | bytes 786432 | tf_op jit(solution)/shard_map/all_to_all | solution.py:403
  50.9 13.2 %copy-start.3 = (f32[64,64]{1,0:T(8,128)S(1)}, f32[64,64]{1,0:T(8,128)}, u32[]{:S(2)}) copy-start(f32[64,64]{1,0:T(8,128)} %cov_ref.1) | copy-start | bytes 49156
  50.9 13.2 %copy-start.4 = (f32[768,1]{0,1:T(1,128)S(1)}, f32[768,1]{0,1:T(1,128)}, u32[]{:S(2)}) copy-start(f32[768,1]{0,1:T(1,128)} %param.13) | copy-start | bytes 9220

commit v7 on v2

--- a/solution.py
+++ b/solution.py
@@ -46,18 +46,25 @@
     return out
 
 
-def whiten_kernel(sky_hbm, mask_hbm, factor_hbm, leg_hbm, sort_hbm, out_hbm, *refs):
-    sky, mask, factor, leg, sort, white, stage, sems = refs
+def whiten_kernel(order, place_ref, sky_hbm, mask_hbm, factor_hbm, leg_hbm, *refs):
+    sky, mask, factor, leg, sort, white, stage, sems = refs[-8:]
+    outs = refs[:-8]
     cycles, chans, pixels = sky.shape
-    groups = stage.shape[0]
+    groups = len(outs)
     width = chans // groups
     group = max(1, SUBLANES // width)
     tall = group * width
     split = pixels // LANES
-    sources, targets = (factor_hbm, sky_hbm, mask_hbm, leg_hbm, sort_hbm), (factor, sky, mask, leg, sort)
+    sources, targets = (factor_hbm, sky_hbm, mask_hbm, leg_hbm), (factor, sky, mask, leg)
     copies = [pltpu.make_async_copy(a, b, sems.at[n]) for n, (a, b) in enumerate(zip(sources, targets))]
     for copy in copies:
         copy.start()
+    shape = (2 * LANES, LANES)
+    ahead = lax.broadcasted_iota(jnp.int32, shape, 0) - split * lax.broadcasted_iota(jnp.int32, shape, 1)
+    for first in range(0, pixels, 2 * LANES):
+        for s in range(split):
+            block = jnp.where(ahead == s - first, 1.0, 0.0).astype(jnp.bfloat16)
+            sort[first : first + 2 * LANES, s * LANES : (s + 1) * LANES] = block
     copies[0].wait()
     row_of = lax.broadcasted_iota(jnp.int32, (tall, group * chans), 0) // width
     lane_of = lax.broadcasted_iota(jnp.int32, (tall, group * chans), 1) // chans
@@ -93,15 +100,6 @@
         for e in range(groups):
             place = split * count + n * high
             stage[e, place : place + high, :] = rows[:, n * LANES : (n + 1) * LANES]
-    sends = []
-
-    def send(first, last):
-        where = (slice(None), slice(first, last))
-        sends.append(pltpu.make_async_copy(stage.at[where], out_hbm.at[where], sems.at[5 + len(sends)]))
-        sends[-1].start()
-
-    send(split * count, stage.shape[1])
-    copies[4].wait()
     for pair in range(split // 2):
         wide = slice(pair * 2 * LANES, (pair + 1) * 2 * LANES)
         value = jnp.dot(white[...], sort[:, wide], preferred_element_type=jnp.float32).astype(jnp.bfloat16)
@@ -111,43 +109,55 @@
                 stage[e, s * count : (s + 1) * count, :] = value[
                     e * count : (e + 1) * count, side * LANES : (side + 1) * LANES
                 ]
-        send(pair * 2 * count, (pair + 1) * 2 * count)
+    me = place_ref[0]
+    sends = [
+        pltpu.make_async_copy(stage.at[jnp.bitwise_xor(me, n)], outs[slot], sems.at[4 + slot])
+        for slot, n in enumerate(order)
+    ]
+    for send in sends:
+        send.start()
     for send in sends:
         send.wait()
 
 
-def modes_kernel(width, offsets, twiddle_ref, table_hbm, z_ref, out_hbm, *refs):
-    table, left, leg, prod_a, prod_b, x_ref, out_ref, table_sems, out_sems = refs
+def modes_kernel(order, cycles, width, offsets, place_ref, twiddle_ref, table_hbm, *refs):
+    slots = refs[: len(order)]
+    keep_hbm, give_hbm, table, left, leg, prod_a, prod_b, x_ref, out_ref, table_sems, out_sems = refs[len(order) :]
     tiles = table.shape[0]
     split = twiddle_ref.shape[1]
     tall = x_ref.shape[3]
     group = tall // width
-    modes = out_ref.shape[3]
-    sources = out_ref.shape[1]
-    parts = z_ref.shape[0] // sources
-    cycles = leg.shape[0] // offsets
+    modes = out_ref.shape[4]
+    sources = len(order)
     blocks = sources * modes // (tiles * LANES)
     per = modes // LANES
-    count = cycles // parts * width
-    high = cycles // parts * offsets
+    count = cycles * width
+    high = cycles * offsets
+    half = sources // 2
+    core = place_ref[3]
+
+    def chunk(n):
+        return jnp.bitwise_xor(place_ref[1], n % half) * 2 + jnp.bitwise_xor(place_ref[2], n // half)
+
 
     def copy(tile):
         return pltpu.make_async_copy(table_hbm.at[tile], table.at[tile], table_sems.at[tile])
 
-    def store(step, n):
+    def store(step, n, given):
         mode_tile = n // 2 * tiles + 2 * step + n % 2
         lanes = pl.ds(pl.multiple_of(mode_tile % per * LANES, LANES), LANES)
         where = (slice(None), mode_tile // per, slice(None), lanes)
-        return pltpu.make_async_copy(out_ref.at[where], out_hbm.at[where], out_sems.at[step, n])
+        source = out_ref.at[(jnp.bitwise_xor(core, given), *where)]
+        return pltpu.make_async_copy(source, (keep_hbm, give_hbm)[given].at[where], out_sems.at[step, n, given])
 
     copy(0).start()
     copy(1).start()
-    for p in range(parts):
-        for q in range(sources):
-            for n in range(split):
-                place = (n * parts + p) * count
-                rows = z_ref[p * sources + q, n * count : (n + 1) * count, :]
-                left[place : place + count, q * LANES : (q + 1) * LANES] = rows
+    for slot, n in enumerate(order):
+        q = chunk(n)
+        lanes = pl.ds(pl.multiple_of(q * LANES, LANES), LANES)
+        for s in range(split):
+            place = s * count
+            left[place : place + count, lanes] = slots[slot][s * count : (s + 1) * count, :]
     for tile in range(2, tiles):
         copy(tile).start()
 
@@ -156,17 +166,19 @@
 
     copy(0).wait()
     product(0, prod_a)
-    for p in range(parts):
-        for q in range(sources):
-            for n in range(per):
-                place = split * count + n * high
-                rows = z_ref[p * sources + q, place : place + high, :].astype(jnp.float32)
-                leg[p * high : (p + 1) * high, (q * per + n) * LANES : (q * per + n + 1) * LANES] = rows
+    for slot, n in enumerate(order):
+        q = chunk(n)
+        for j in range(per):
+            lanes = pl.ds(pl.multiple_of((q * per + j) * LANES, LANES), LANES)
+            place = split * count + j * high
+            rows = slots[slot][place : place + high, :].astype(jnp.float32)
+            leg[:, lanes] = rows
 
     def use(tile, prod):
         lanes = pl.ds(pl.multiple_of(tile * LANES, LANES), LANES)
         cosine, sine = twiddle_ref[0, :, lanes], twiddle_ref[1, :, lanes]
-        cycle_of = lax.broadcasted_iota(jnp.int32, (tall, LANES), 0) // width
+        row_in = lax.broadcasted_iota(jnp.int32, (tall, LANES), 0)
+        cycle_of = row_in // width
         for pack in range(cycles // group):
             values = []
             for s in range(split):
@@ -204,12 +216,12 @@
                 while step >= width:
                     total = [value + pltpu.roll(value, step, 0) for value in total]
                     step //= 2
-                if group == 1:
-                    both = jnp.concatenate(total, axis=0)
-                else:
-                    both = jnp.where(cycle_of < 1, total[0], total[1])[: 2 * width]
                 place = pl.ds(pl.multiple_of(n * LANES, LANES), LANES)
-                out_ref[k, d, :, place] = both.astype(jnp.bfloat16)
+                for part in range(2):
+                    shift = (tall - part * width // 2, tall + width // 2 - part * width // 2)
+                    rows = [pltpu.roll(v, m % tall, 0) if m % tall else v for v, m in zip(total, shift)]
+                    both = jnp.where(row_in < width // 2, rows[0], rows[1])[:width]
+                    out_ref[part, k, d, :, place] = both.astype(jnp.bfloat16)
 
     @pl.loop(0, tiles // 2)
     def _(step):
@@ -224,12 +236,18 @@
         product(jnp.minimum(2 * step + 2, tiles - 1), prod_a)
         use(2 * step + 1, prod_b)
         for n in range(2 * blocks):
-            store(step, n).start()
+            store(step, n, 0).start()
+            store(step, n, 1).start()
 
     @pl.loop(0, tiles // 2)
     def _(step):
         for n in range(2 * blocks):
-            store(step, n).wait()
+            store(step, n, 0).wait()
+            store(step, n, 1).wait()
+
+
+def pair_kernel(one_ref, two_ref, out_ref):
+    out_ref[...] = (one_ref[...].astype(jnp.float32) + two_ref[...].astype(jnp.float32)).astype(jnp.bfloat16)
 
 
 def sketch_kernel(alm_ref, band_ref, cov_ref, test_ref, out_ref, left_ref):
@@ -298,20 +316,15 @@
     return twiddle, table.astype(ml_dtypes.bfloat16)
 
 
-def sorting(pixels, split):
-    place = np.arange(pixels) % split * (pixels // split) + np.arange(pixels) // split
-    return (place[:, None] == np.arange(pixels)[None, :]).astype(ml_dtypes.bfloat16)
-
-
 def local(sky_map, pixel_mask, noise_factor, cycle_legendre, band_power, channel_cov, test_matrix):
     cycles, pixels, chans = sky_map.shape
     modes, _ = band_power.shape
     offsets = cycle_legendre.shape[2]
     columns = test_matrix.shape[3]
-    mode_count, pair = lax.axis_size("mode"), lax.axis_size("low")
-    groups = pair * mode_count
-    devices = lax.axis_size("high") * groups
-    width = chans // groups
+    mode_count = lax.axis_size("mode")
+    half = mode_count // 2
+    devices = lax.axis_size("high") * 2 * mode_count
+    width = chans // mode_count
     group = max(1, SUBLANES // width)
     split = pixels // LANES
     rows = split * cycles * width
@@ -322,9 +335,17 @@
     hbm, vmem, bf16, f32, shape = pl.ANY, pltpu.VMEM, jnp.bfloat16, jnp.float32, jax.ShapeDtypeStruct
     twiddle, table = transform_tables(split, pixels * mode_count)
 
-    message = call(
-        whiten_kernel,
-        shape((groups, rows + legs, LANES), bf16),
+    low, mode = lax.axis_index("low"), lax.axis_index("mode")
+    place = jnp.stack([mode % 2 * half + mode // 2, mode // 2, low, mode % 2]).astype(jnp.int32)
+    order = sorted(range(mode_count), key=lambda n: -(n % half).bit_count())
+
+    def target(i, n):
+        i_low, i_mode = i // mode_count, i % mode_count
+        return (i_mode % 2 ^ n // half) * mode_count + (i_mode // 2 ^ n % half) * 2 + i_low
+
+    messages = call(
+        functools.partial(whiten_kernel, order),
+        [shape((rows + legs, LANES), bf16)] * mode_count,
         [
             vmem((cycles, chans, pixels), bf16),
             vmem((cycles, pixels), jnp.int32),
@@ -332,46 +353,52 @@
             vmem((cycles, offsets, modes), f32),
             vmem((pixels, pixels), bf16),
             vmem((cycles * chans, pixels), bf16),
-            vmem((groups, rows + legs, LANES), bf16),
-            pltpu.SemaphoreType.DMA((6 + split // 2,)),
+            vmem((mode_count, rows + legs, LANES), bf16),
+            pltpu.SemaphoreType.DMA((4 + mode_count,)),
         ],
         56,
-        [hbm] * 5,
+        [pltpu.SMEM] + [hbm] * 4,
+        place,
         jnp.transpose(sky_map, (0, 2, 1)),
         pixel_mask,
         noise_factor[:, 0],
         jnp.transpose(cycle_legendre, (0, 2, 1)),
-        jnp.asarray(sorting(pixels, split)),
         out_space=hbm,
         cost=(2 * cycles * chans * pixels * (pixels + 4 * chans), 8 * MIB),
     )
-    message = lax.all_to_all(message, ("low", "mode"), 0, 0, tiled=True)
-
-    alm = call(
-        functools.partial(modes_kernel, width, offsets),
-        shape((offsets, mode_count, 2 * width, modes), bf16),
+    slots = [
+        lax.ppermute(message, ("low", "mode"), [(i, target(i, n)) for i in range(2 * mode_count)])
+        for message, n in zip(messages, order)
+    ]
+
+    keep, give = call(
+        functools.partial(modes_kernel, order, cycles, width, offsets),
+        [shape((offsets, mode_count, width, modes), bf16)] * 2,
         [
             vmem((tiles, tiles * LANES, 2 * LANES), bf16),
-            vmem((pair * rows, tiles * LANES), bf16),
-            vmem((pair * cycles * offsets, mode_count * modes), f32),
-            vmem((pair * rows, 2 * LANES), f32),
-            vmem((pair * rows, 2 * LANES), f32),
-            vmem((blocks, 2, pair * cycles // group, group * width, LANES), f32),
-            vmem((offsets, mode_count, 2 * width, modes), bf16),
+            vmem((rows, tiles * LANES), bf16),
+            vmem((cycles * offsets, mode_count * modes), f32),
+            vmem((rows, 2 * LANES), f32),
+            vmem((rows, 2 * LANES), f32),
+            vmem((blocks, 2, cycles // group, group * width, LANES), f32),
+            vmem((2, offsets, mode_count, width, modes), bf16),
             pltpu.SemaphoreType.DMA((tiles,)),
-            pltpu.SemaphoreType.DMA((tiles // 2, 2 * blocks)),
+            pltpu.SemaphoreType.DMA((tiles // 2, 2 * blocks, 2)),
         ],
         40,
-        [vmem, hbm, vmem],
+        [pltpu.SMEM, vmem, hbm] + [vmem] * mode_count,
+        place,
         jnp.asarray(twiddle),
         jnp.asarray(table),
-        message,
+        *slots,
         out_space=hbm,
-        cost=(4 * pair * rows * (tiles * LANES) ** 2, 8 * MIB),
+        cost=(4 * rows * (tiles * LANES) ** 2, 8 * MIB),
     )
-    alm = alm.reshape(devices, 2 * width, modes)
+    other = lax.ppermute(give, "mode", [(i, i ^ 1) for i in range(mode_count)])
+    alm = call(pair_kernel, shape(keep.shape, bf16), [], 16, [vmem] * 2, keep, other)
+    alm = alm.reshape(devices, width, modes)
     alm = lax.all_to_all(alm, everyone, 0, 0, tiled=True)
-    alm = alm.reshape(devices // groups, groups, 2 * width, modes)
+    alm = alm.reshape(devices // (2 * mode_count), 2 * mode_count, width, modes)
 
     share = columns // (devices)
     fold = LANES // chans

time: 71.7 us -> 75.1 us (1.047)
  blocking collectives: 41.7 us -> 10.7 us
  waiting for transfers between devices: 11.5 us -> 27.6 us
  starting transfers between devices: 2.95 us -> 18.3 us
  Pallas kernels: 13.5 us -> 15.9 us
    all_to_all x1 -> x0, blocking collectives: 31 us -> none  [local(): message = lax.all_to_all(message, ('low', 'mode'), 0, 0, tiled=True)]
    ppermute x0 -> x9, waiting for transfers between devices: none -> 16.1 us  [the longest x8 14.8 us: local(): lax.ppermute(message, ('low', 'mode'), [(i, target(i, n)) for i in range(...]
    ppermute x0 -> x9, starting transfers between devices: none -> 13.5 us  [the longest x8 11.8 us: local(): lax.ppermute(message, ('low', 'mode'), [(i, target(i, n)) for i in range(...]
    pallas_call x4 -> x5, Pallas kernels: 13.5 us -> 15.9 us  [call(): pl.pallas_call(kernel, out_shape=shape, in_specs=[pl.BlockSpec(memory_spa...]
    all_to_all x1, starting transfers between devices: 2.95 us -> 4.81 us  [local(): alm = lax.all_to_all(alm, everyone, 0, 0, tiled=True)]
    unnamed x9 -> x11, local copies, waits for them, and re-layouts: 1.68 us -> 1.69 us
  transfers between devices with their start and end apart: 1 -> 10, of which waited for: 1 -> 6; matrix products, arithmetic and copies ran while one was open for 2% -> 2% of each run, Pallas kernels for 0% -> 0%
where the time goes in v7:
time: 75.1 us; the launch traced here: 74.9 us
  waiting for transfers between devices  27.6 us (37%)
  starting transfers between devices  18.3 us (24%)
  Pallas kernels  15.9 us (21%)
  blocking collectives  10.7 us (14%)
  local copies, waits for them, and re-layouts  1.69 us (2%)
    pallas_call x5, Pallas kernels, call(): pl.pallas_call(kernel, out_shape=shape, in_specs=[pl.BlockSpec(memory_spa...  15.9 us
    ppermute x8, waiting for transfers between devices, local(): lax.ppermute(message, ('low', 'mode'), [(i, target(i, n)) for i in range(...  14.8 us
    ppermute x8, starting transfers between devices, local(): lax.ppermute(message, ('low', 'mode'), [(i, target(i, n)) for i in range(...  11.8 us
    all_to_all x1, waiting for transfers between devices, local(): alm = lax.all_to_all(alm, everyone, 0, 0, tiled=True)  11.5 us
    all_to_all x1, blocking collectives, local(): part = lax.all_to_all(part, everyone, 0, 0, tiled=True)  10.7 us
    all_to_all x1, starting transfers between devices, local(): alm = lax.all_to_all(alm, everyone, 0, 0, tiled=True)  4.81 us
    unnamed x11, local copies, waits for them, and re-layouts  1.69 us
    ppermute x1, starting transfers between devices, local(): other = lax.ppermute(give, 'mode', [(i, i ^ 1) for i in range(mode_count)])  1.62 us
  transfers between devices with their start and end apart: 10, of which 6 were waited for; matrix products, arithmetic and copies ran while one was open for 2% of the time, Pallas kernels for 0%

profile of v7, /device:TPU:0, one launch (start us, length us, event | category | flops | bytes accessed | tf_op | source)
XLA Modules:
  0.0 74.9 jit_solution(7915119219918686902)
XLA Ops:
  0.0 0.7 pad_add_fusion.place_ref
  0.7 0.0 copy-start.2
  0.7 0.0 copy-start.3
  0.7 0.0 copy-start.4
  0.7 5.4 %shard_map.91 = (bf16[704,128]{1,0:T(8,128)(2,1)}, bf16[704,128]{1,0:T(8,128)(2,1)}, bf16[704,128]{1,0:T(8,128)(2,1)}, bf16[704,128]{1,0:T(8,128)(2,1)}, bf16[70...) custom-call(s32[4]{0:T(128)} %pad_add_fusion.place_ref, ...), custom_call_target="tpu_custom_call" | custom-call | flops 1342177280 | bytes 8388608 | tf_op jit(solution)/shard_map/pallas_call | solution.py:297
  6.1 4.0 %collective-permute-start = (bf16[704,128]{1,0:T(8,128)(2,1)}, bf16[704,128]{1,0:T(8,128)(2,1)S(1)}, u32[]{:S(2)}, u32[]{:S(2)}) collective-permute-start(bf16[704,128]{1,0:T(8,128)(2,1)} %get-tuple-element.15), channel_id=1, source_target_pairs={{0,6},{1,14},{2,4},{3,12},{4,2},{5,10},{6,0},{7,8},{8,7},{9,15},{1... | collective-permute-start | bytes 540680 | tf_op jit(solution)/shard_map/ppermute | solution.py:370
  10.0 1.1 %collective-permute-start.1 = (bf16[704,128]{1,0:T(8,128)(2,1)}, bf16[704,128]{1,0:T(8,128)(2,1)S(1)}, u32[]{:S(2)}, u32[]{:S(2)}) collective-permute-start(bf16[704,128]{1,0:T(8,128)(2,1)} %get-tuple-element.16), channel_id=1, source_target_pairs={{0,14},{1,6},{2,12},{3,4},{4,10},{5,2},{6,8},{7,0},{8,15},{9,7},{1... | collective-permute-start | bytes 540680 | tf_op jit(solution)/shard_map/ppermute | solution.py:370
  11.1 1.2 %collective-permute-start.2 = (bf16[704,128]{1,0:T(8,128)(2,1)}, bf16[704,128]{1,0:T(8,128)(2,1)S(1)}, u32[]{:S(2)}, u32[]{:S(2)}) collective-permute-start(bf16[704,128]{1,0:T(8,128)(2,1)} %get-tuple-element.17), channel_id=1, source_target_pairs={{0,2},{1,10},{2,0},{3,8},{4,6},{5,14},{6,4},{7,12},{8,3},{9,11},{1... | collective-permute-start | bytes 540680 | tf_op jit(solution)/shard_map/ppermute | solution.py:370
  12.3 1.5 %collective-permute-start.3 = (bf16[704,128]{1,0:T(8,128)(2,1)}, bf16[704,128]{1,0:T(8,128)(2,1)S(1)}, u32[]{:S(2)}, u32[]{:S(2)}) collective-permute-start(bf16[704,128]{1,0:T(8,128)(2,1)} %get-tuple-element.18), channel_id=1, source_target_pairs={{0,4},{1,12},{2,6},{3,14},{4,0},{5,8},{6,2},{7,10},{8,5},{9,13},{1... | collective-permute-start | bytes 540680 | tf_op jit(solution)/shard_map/ppermute | solution.py:370
  13.8 1.0 %collective-permute-start.4 = (bf16[704,128]{1,0:T(8,128)(2,1)}, bf16[704,128]{1,0:T(8,128)(2,1)S(1)}, u32[]{:S(2)}, u32[]{:S(2)}) collective-permute-start(bf16[704,128]{1,0:T(8,128)(2,1)} %get-tuple-element.19), channel_id=1, source_target_pairs={{0,10},{1,2},{2,8},{3,0},{4,14},{5,6},{6,12},{7,4},{8,11},{9,3},{1... | collective-permute-start | bytes 540680 | tf_op jit(solution)/shard_map/ppermute | solution.py:370
  14.8 8.0 %collective-permute-done.refs_0_ = bf16[704,128]{1,0:T(8,128)(2,1)S(1)} collective-permute-done((bf16[704,128]{1,0:T(8,128)(2,1)}, bf16[704,128]{1,0:T(8,128)(2,1)S(1)}, u32[]{:S(2)}, u32[]{:S(2)}) %collective-permute-start) | collective-permute-done | bytes 180256 | tf_op jit(solution)/shard_map/ppermute | solution.py:370
  22.9 0.0 collective-permute-start.5
  22.9 1.9 %collective-permute-done.1.refs_1_ = bf16[704,128]{1,0:T(8,128)(2,1)S(1)} collective-permute-done((bf16[704,128]{1,0:T(8,128)(2,1)}, bf16[704,128]{1,0:T(8,128)(2,1)S(1)}, u32[]{:S(2)}, u32[]{:S(2)}) %collective-permute-start.1) | collective-permute-done | bytes 180256 | tf_op jit(solution)/shard_map/ppermute | solution.py:370
  24.8 1.6 %collective-permute-start.6 = (bf16[704,128]{1,0:T(8,128)(2,1)}, bf16[704,128]{1,0:T(8,128)(2,1)S(1)}, u32[]{:S(2)}, u32[]{:S(2)}) collective-permute-start(bf16[704,128]{1,0:T(8,128)(2,1)} %get-tuple-element.21), channel_id=1, source_target_pairs={{0,0},{1,8},{2,2},{3,10},{4,4},{5,12},{6,6},{7,14},{8,1},{9,9},{10... | collective-permute-start | bytes 540680 | tf_op jit(solution)/shard_map/ppermute | solution.py:370
  26.3 1.5 %collective-permute-done.2.refs_2_ = bf16[704,128]{1,0:T(8,128)(2,1)S(1)} collective-permute-done((bf16[704,128]{1,0:T(8,128)(2,1)}, bf16[704,128]{1,0:T(8,128)(2,1)S(1)}, u32[]{:S(2)}, u32[]{:S(2)}) %collective-permute-start.2) | collective-permute-done | bytes 180256 | tf_op jit(solution)/shard_map/ppermute | solution.py:370
  27.9 1.5 %collective-permute-start.7 = (bf16[704,128]{1,0:T(8,128)(2,1)}, bf16[704,128]{1,0:T(8,128)(2,1)S(1)}, u32[]{:S(2)}, u32[]{:S(2)}) collective-permute-start(bf16[704,128]{1,0:T(8,128)(2,1)} %get-tuple-element.22), channel_id=1, source_target_pairs={{0,8},{1,0},{2,10},{3,2},{4,12},{5,4},{6,14},{7,6},{8,9},{9,1},{10... | collective-permute-start | bytes 540680 | tf_op jit(solution)/shard_map/ppermute | solution.py:370
  29.4 0.0 collective-permute-done.3.refs_3_
  29.4 0.0 collective-permute-done.4.refs_4_
  29.4 0.0 collective-permute-done.5.refs_5_
  29.4 0.0 collective-permute-done.6.refs_6_
  29.4 3.3 %collective-permute-done.7.refs_7_ = bf16[704,128]{1,0:T(8,128)(2,1)S(1)} collective-permute-done((bf16[704,128]{1,0:T(8,128)(2,1)}, bf16[704,128]{1,0:T(8,128)(2,1)S(1)}, u32[]{:S(2)}, u32[]{:S(2)}) %collective-permute-start.7) | collective-permute-done | bytes 180256 | tf_op jit(solution)/shard_map/ppermute | solution.py:370
  32.7 0.0 copy-done.2
  32.7 0.0 copy-done.3
  32.7 0.0 copy-done.4
  32.7 7.6 %shard_map.92 = (bf16[4,8,8,768]{3,2,1,0:T(8,128)(2,1)S(1)}, bf16[4,8,8,768]{3,2,1,0:T(8,128)(2,1)S(1)}) custom-call(s32[4]{0:T(128)S(1)} %copy-done.2, f32[2,8,1024]{2,1,0:T(8,128)S(1)} %copy-done.4, bf16[8,1024,256]{2,1,0:T(8,128)(2,1)S(1)} %copy-done.3, bf16[704,128]{1,0:T(8,128)(2,1)S(1)} %collective-permute-done.refs_0_, ...), custom_call_target="tpu_custom_call" | custom-call | flops 2147483648 | bytes 8388608 | tf_op jit(solution)/shard_map/pallas_call | solution.py:297
  40.3 1.6 %collective-permute-start.8 = (bf16[4,8,8,768]{3,2,1,0:T(8,128)(2,1)S(1)}, bf16[4,8,8,768]{3,2,1,0:T(8,128)(2,1)S(1)}, u32[]{:S(2)}, u32[]{:S(2)}) collective-permute-start(bf16[4,8,8,768]{3,2,1,0:T(8,128)(2,1)S(1)} %get-tuple-element.24), channel_id=1, source_target_pairs={{0,1},{1,0},{2,3},{3,2},{4,5},{5,4},{6,7},{7,6},{8,9},{9,8},{10,11... | collective-permute-start | bytes 1179656 | tf_op jit(solution)/shard_map/ppermute | solution.py:397
  42.0 1.3 %collective-permute-done.8.two_ref = bf16[4,8,8,768]{3,2,1,0:T(8,128)(2,1)S(1)} collective-permute-done((bf16[4,8,8,768]{3,2,1,0:T(8,128)(2,1)S(1)}, bf16[4,8,8,768]{3,2,1,0:T(8,128)(2,1)S(1)}, u32[]{:S(2)}, u32[]{:S(2)}) %collective-permute-start.8) | collective-permute-done | bytes 393248 | tf_op jit(solution)/shard_map/ppermute | solution.py:397
  43.3 0.8 %shard_map.93 = bf16[4,8,8,768]{3,2,1,0:T(8,128)(2,1)} custom-call(bf16[4,8,8,768]{3,2,1,0:T(8,128)(2,1)S(1)} %get-tuple-element.23.one_ref, bf16[4,8,8,768]{3,2,1,0:T(8,128)(2,1)S(1)} %collective-permute-done.8.two_ref), custom_call_target="tpu_custom_call" | custom-call | tf_op jit(solution)/shard_map/pallas_call | solution.py:297
  44.2 4.8 %all-to-all-start = ((bf16[32,8,768]{2,1,0:T(8,128)(2,1)}), bf16[32,8,768]{2,1,0:T(8,128)(2,1)S(1)}, u32[]{:S(2)}, u32[]{:S(2)}) async-start(bf16[32,8,768]{2,1,0:T(8,128)(2,1)} %bitcast.7), calls=%async_computation | async-start | bytes 786432 | tf_op jit(solution)/shard_map/all_to_all | solution.py:400
  49.0 0.0 copy-start
  49.0 0.0 copy-start.1
  49.0 1.7 %copy.12 = bf16[1,768,2,512]{3,1,2,0:T(8,128)(2,1)S(1)} copy(bf16[1,768,2,512]{3,2,1,0:T(2,128)(2,1)} %param.15) | data formatting | bytes 3145728 | tf_op args[6]
  50.7 11.5 %all-to-all-done = bf16[32,8,768]{2,1,0:T(8,128)(2,1)S(1)} async-done(((bf16[32,8,768]{2,1,0:T(8,128)(2,1)}), bf16[32,8,768]{2,1,0:T(8,128)(2,1)S(1)}, u32[]{:S(2)}, u32[]{:S(2)}) %all-to-all-start) | async-done | bytes 393248 | tf_op jit(solution)/shard_map/all_to_all | solution.py:400
  62.1 0.0 copy-done
  62.2 0.0 copy-done.1
  62.2 1.3 %shard_map.94 = f32[32,8,128]{2,1,0:T(8,128)S(1)} custom-call(bf16[2,16,8,768]{3,2,1,0:T(8,128)(2,1)S(1)} %bitcast.17, f32[1,768]{1,0:T(1,128)S(1)} %bitcast.18, f32[64,64]{1,0:T(8,128)S(1)} %copy-done, bf16[2,768,512]{2,1,0:T(8,128)(2,1)S(1)} %bitcast.16), custom_call_target="tpu_custom_call" | custom-call | tf_op jit(solution)/shard_map/pallas_call | solution.py:297
  63.5 10.7 %all_to_all.10.part_ref = f32[32,8,128]{2,1,0:T(8,128)S(1)} all-to-all(f32[32,8,128]{2,1,0:T(8,128)S(1)} %shard_map.94), channel_id=1, replica_groups=mesh['high'=2,'low'=2,'mode'=8] {'high','low','mode'}, dimensions={0} | all-to-all | bytes 262144 | tf_op jit(solution)/shard_map/all_to_all | solution.py:419
  74.2 0.7 shard_map.95
Async XLA Ops:
  0.7 32.0 %copy-start.2 = (s32[4]{0:T(128)S(1)}, s32[4]{0:T(128)}, u32[]{:S(2)}) copy-start(s32[4]{0:T(128)} %pad_add_fusion.place_ref) | copy-start | bytes 52
  0.7 32.0 %copy-start.3 = (bf16[8,1024,256]{2,1,0:T(8,128)(2,1)S(1)}, bf16[8,1024,256]{2,1,0:T(8,128)(2,1)}, u32[]{:S(2)}) copy-start(bf16[8,1024,256]{2,1,0:T(8,128)(2,1)} %constant.44.clone.table_hbm) | copy-start | bytes 12582916
  0.7 32.0 %copy-start.4 = (f32[2,8,1024]{2,1,0:T(8,128)S(1)}, f32[2,8,1024]{2,1,0:T(8,128)}, u32[]{:S(2)}) copy-start(f32[2,8,1024]{2,1,0:T(8,128)} %constant.43.clone.twiddle_ref) | copy-start | bytes 196612
  6.1 16.8 %collective-permute-start = (bf16[704,128]{1,0:T(8,128)(2,1)}, bf16[704,128]{1,0:T(8,128)(2,1)S(1)}, u32[]{:S(2)}, u32[]{:S(2)}) collective-permute-start(bf16[704,128]{1,0:T(8,128)(2,1)} %get-tuple-element.15), channel_id=1, source_target_pairs={{0,6},{1,14},{2,4},{3,12},{4,2},{5,10},{6,0},{7,8},{8,7},{9,15},{1... | collective-permute-start | bytes 540680 | tf_op jit(solution)/shard_map/ppermute | solution.py:370
  10.0 14.8 %collective-permute-start.1 = (bf16[704,128]{1,0:T(8,128)(2,1)}, bf16[704,128]{1,0:T(8,128)(2,1)S(1)}, u32[]{:S(2)}, u32[]{:S(2)}) collective-permute-start(bf16[704,128]{1,0:T(8,128)(2,1)} %get-tuple-element.16), channel_id=1, source_target_pairs={{0,14},{1,6},{2,12},{3,4},{4,10},{5,2},{6,8},{7,0},{8,15},{9,7},{1... | collective-permute-start | bytes 540680 | tf_op jit(solution)/shard_map/ppermute | solution.py:370
  11.1 16.8 %collective-permute-start.2 = (bf16[704,128]{1,0:T(8,128)(2,1)}, bf16[704,128]{1,0:T(8,128)(2,1)S(1)}, u32[]{:S(2)}, u32[]{:S(2)}) collective-permute-start(bf16[704,128]{1,0:T(8,128)(2,1)} %get-tuple-element.17), channel_id=1, source_target_pairs={{0,2},{1,10},{2,0},{3,8},{4,6},{5,14},{6,4},{7,12},{8,3},{9,11},{1... | collective-permute-start | bytes 540680 | tf_op jit(solution)/shard_map/ppermute | solution.py:370
  12.3 17.0 %collective-permute-start.3 = (bf16[704,128]{1,0:T(8,128)(2,1)}, bf16[704,128]{1,0:T(8,128)(2,1)S(1)}, u32[]{:S(2)}, u32[]{:S(2)}) collective-permute-start(bf16[704,128]{1,0:T(8,128)(2,1)} %get-tuple-element.18), channel_id=1, source_target_pairs={{0,4},{1,12},{2,6},{3,14},{4,0},{5,8},{6,2},{7,10},{8,5},{9,13},{1... | collective-permute-start | bytes 540680 | tf_op jit(solution)/shard_map/ppermute | solution.py:370
  13.8 15.5 %collective-permute-start.4 = (bf16[704,128]{1,0:T(8,128)(2,1)}, bf16[704,128]{1,0:T(8,128)(2,1)S(1)}, u32[]{:S(2)}, u32[]{:S(2)}) collective-permute-start(bf16[704,128]{1,0:T(8,128)(2,1)} %get-tuple-element.19), channel_id=1, source_target_pairs={{0,10},{1,2},{2,8},{3,0},{4,14},{5,6},{6,12},{7,4},{8,11},{9,3},{1... | collective-permute-start | bytes 540680 | tf_op jit(solution)/shard_map/ppermute | solution.py:370
  22.9 6.5 %collective-permute-start.5 = (bf16[704,128]{1,0:T(8,128)(2,1)}, bf16[704,128]{1,0:T(8,128)(2,1)S(1)}, u32[]{:S(2)}, u32[]{:S(2)}) collective-permute-start(bf16[704,128]{1,0:T(8,128)(2,1)} %get-tuple-element.20), channel_id=1, source_target_pairs={{0,12},{1,4},{2,14},{3,6},{4,8},{5,0},{6,10},{7,2},{8,13},{9,5},{1... | collective-permute-start | bytes 540680 | tf_op jit(solution)/shard_map/ppermute | solution.py:370
  24.8 4.6 %collective-permute-start.6 = (bf16[704,128]{1,0:T(8,128)(2,1)}, bf16[704,128]{1,0:T(8,128)(2,1)S(1)}, u32[]{:S(2)}, u32[]{:S(2)}) collective-permute-start(bf16[704,128]{1,0:T(8,128)(2,1)} %get-tuple-element.21), channel_id=1, source_target_pairs={{0,0},{1,8},{2,2},{3,10},{4,4},{5,12},{6,6},{7,14},{8,1},{9,9},{10... | collective-permute-start | bytes 540680 | tf_op jit(solution)/shard_map/ppermute | solution.py:370
  27.9 4.8 %collective-permute-start.7 = (bf16[704,128]{1,0:T(8,128)(2,1)}, bf16[704,128]{1,0:T(8,128)(2,1)S(1)}, u32[]{:S(2)}, u32[]{:S(2)}) collective-permute-start(bf16[704,128]{1,0:T(8,128)(2,1)} %get-tuple-element.22), channel_id=1, source_target_pairs={{0,8},{1,0},{2,10},{3,2},{4,12},{5,4},{6,14},{7,6},{8,9},{9,1},{10... | collective-permute-start | bytes 540680 | tf_op jit(solution)/shard_map/ppermute | solution.py:370
  40.3 3.0 %collective-permute-start.8 = (bf16[4,8,8,768]{3,2,1,0:T(8,128)(2,1)S(1)}, bf16[4,8,8,768]{3,2,1,0:T(8,128)(2,1)S(1)}, u32[]{:S(2)}, u32[]{:S(2)}) collective-permute-start(bf16[4,8,8,768]{3,2,1,0:T(8,128)(2,1)S(1)} %get-tuple-element.24), channel_id=1, source_target_pairs={{0,1},{1,0},{2,3},{3,2},{4,5},{5,4},{6,7},{7,6},{8,9},{9,8},{10,11... | collective-permute-start | bytes 1179656 | tf_op jit(solution)/shard_map/ppermute | solution.py:397
  44.2 18.0 %all-to-all-start = ((bf16[32,8,768]{2,1,0:T(8,128)(2,1)}), bf16[32,8,768]{2,1,0:T(8,128)(2,1)S(1)}, u32[]{:S(2)}, u32[]{:S(2)}) async-start(bf16[32,8,768]{2,1,0:T(8,128)(2,1)} %bitcast.7), calls=%async_computation | async-start | bytes 786432 | tf_op jit(solution)/shard_map/all_to_all | solution.py:400
  49.0 13.2 %copy-start = (f32[64,64]{1,0:T(8,128)S(1)}, f32[64,64]{1,0:T(8,128)}, u32[]{:S(2)}) copy-start(f32[64,64]{1,0:T(8,128)} %cov_ref.1) | copy-start | bytes 49156
  49.0 13.2 %copy-start.1 = (f32[768,1]{0,1:T(1,128)S(1)}, f32[768,1]{0,1:T(1,128)}, u32[]{:S(2)}) copy-start(f32[768,1]{0,1:T(1,128)} %param.13) | copy-start | bytes 9220

commit v8 on v2

--- a/solution.py
+++ b/solution.py
@@ -46,7 +46,7 @@
     return out
 
 
-def whiten_kernel(sky_hbm, mask_hbm, factor_hbm, leg_hbm, sort_hbm, out_hbm, *refs):
+def whiten_kernel(fold, sky_hbm, mask_hbm, factor_hbm, leg_hbm, out_hbm, *refs):
     sky, mask, factor, leg, sort, white, stage, sems = refs
     cycles, chans, pixels = sky.shape
     groups = stage.shape[0]
@@ -54,10 +54,16 @@
     group = max(1, SUBLANES // width)
     tall = group * width
     split = pixels // LANES
-    sources, targets = (factor_hbm, sky_hbm, mask_hbm, leg_hbm, sort_hbm), (factor, sky, mask, leg, sort)
+    sources, targets = (factor_hbm, sky_hbm, mask_hbm, leg_hbm), (factor, sky, mask, leg)
     copies = [pltpu.make_async_copy(a, b, sems.at[n]) for n, (a, b) in enumerate(zip(sources, targets))]
     for copy in copies:
         copy.start()
+    shape = (2 * LANES, LANES)
+    ahead = lax.broadcasted_iota(jnp.int32, shape, 0) - split * lax.broadcasted_iota(jnp.int32, shape, 1)
+    for first in range(0, pixels, 2 * LANES):
+        for s in range(split):
+            block = jnp.where(ahead == s - first, 1.0, 0.0).astype(jnp.bfloat16)
+            sort[first : first + 2 * LANES, s * LANES : (s + 1) * LANES] = block
     copies[0].wait()
     row_of = lax.broadcasted_iota(jnp.int32, (tall, group * chans), 0) // width
     lane_of = lax.broadcasted_iota(jnp.int32, (tall, group * chans), 1) // chans
@@ -89,6 +95,16 @@
     count = cycles * width
     rows = jnp.concatenate([leg[r] for r in range(cycles)], axis=0).astype(jnp.bfloat16)
     high = rows.shape[0]
+    if fold > 1:
+        shape = (fold * LANES, LANES)
+        ahead = lax.broadcasted_iota(jnp.int32, shape, 0) - fold * lax.broadcasted_iota(jnp.int32, shape, 1)
+        places = [jnp.where(ahead == n, 1.0, 0.0).astype(jnp.bfloat16) for n in range(fold)]
+        places = jnp.concatenate(places, axis=1)
+        rows = [
+            jnp.dot(rows[:, n : n + fold * LANES], places, preferred_element_type=jnp.float32)
+            for n in range(0, rows.shape[1], fold * LANES)
+        ]
+        rows = jnp.concatenate(rows, axis=1).astype(jnp.bfloat16)
     for n in range(rows.shape[1] // LANES):
         for e in range(groups):
             place = split * count + n * high
@@ -97,11 +113,10 @@
 
     def send(first, last):
         where = (slice(None), slice(first, last))
-        sends.append(pltpu.make_async_copy(stage.at[where], out_hbm.at[where], sems.at[5 + len(sends)]))
+        sends.append(pltpu.make_async_copy(stage.at[where], out_hbm.at[where], sems.at[4 + len(sends)]))
         sends[-1].start()
 
     send(split * count, stage.shape[1])
-    copies[4].wait()
     for pair in range(split // 2):
         wide = slice(pair * 2 * LANES, (pair + 1) * 2 * LANES)
         value = jnp.dot(white[...], sort[:, wide], preferred_element_type=jnp.float32).astype(jnp.bfloat16)
@@ -142,20 +157,28 @@
 
     copy(0).start()
     copy(1).start()
+    fold = left.shape[0]
     for p in range(parts):
-        for q in range(sources):
+        for q in range(sources // fold):
+            lanes = slice(q * LANES, (q + 1) * LANES)
             for n in range(split):
                 place = (n * parts + p) * count
                 rows = z_ref[p * sources + q, n * count : (n + 1) * count, :]
-                left[place : place + count, q * LANES : (q + 1) * LANES] = rows
+                if fold == 1:
+                    left[0, place : place + count, lanes] = rows
+                else:
+                    rows = rows.astype(jnp.float32)
+                    more = z_ref[p * sources + sources // 2 + q, n * count : (n + 1) * count, :].astype(jnp.float32)
+                    left[0, place : place + count, lanes] = (rows + more).astype(jnp.bfloat16)
+                    left[1, place : place + count, lanes] = (rows - more).astype(jnp.bfloat16)
     for tile in range(2, tiles):
         copy(tile).start()
 
-    def product(tile, prod):
-        prod[...] = jnp.dot(left[...], table[tile], preferred_element_type=jnp.float32)
+    def product(tile, prod, kind):
+        prod[...] = jnp.dot(left[kind % fold], table[tile], preferred_element_type=jnp.float32)
 
     copy(0).wait()
-    product(0, prod_a)
+    product(0, prod_a, 0)
     for p in range(parts):
         for q in range(sources):
             for n in range(per):
@@ -219,9 +242,9 @@
         def _():
             copy(2 * step + 2).wait()
 
-        product(2 * step + 1, prod_b)
+        product(2 * step + 1, prod_b, 1)
         use(2 * step, prod_a)
-        product(jnp.minimum(2 * step + 2, tiles - 1), prod_a)
+        product(jnp.minimum(2 * step + 2, tiles - 2), prod_a, 0)
         use(2 * step + 1, prod_b)
         for n in range(2 * blocks):
             store(step, n).start()
@@ -287,20 +310,20 @@
     )(*operands)
 
 
-def transform_tables(split, cycle):
+def in_order(modes, fold):
+    return np.arange(modes).reshape(-1, LANES, fold).swapaxes(1, 2).reshape(-1)
+
+
+def transform_tables(split, cycle, fold):
     half = cycle // split
-    step = np.arange(split)[:, None] * np.arange(half)[None, :] % cycle
+    modes = in_order(half, fold)
+    step = np.arange(split)[:, None] * modes[None, :] % cycle
     angle = step * (2.0 * math.pi / cycle)
     twiddle = np.stack([np.cos(angle), np.sin(angle)]).astype(np.float32)
-    step = np.arange(half)[:, None] * np.arange(half)[None, :] % half
-    angle = (step * (2.0 * math.pi / half)).reshape(half, half // LANES, LANES)
+    step = np.arange(half // fold)[:, None] * modes[None, :] % half
+    angle = (step * (2.0 * math.pi / half)).reshape(half // fold, half // LANES, LANES)
     table = np.transpose(np.concatenate([np.cos(angle), np.sin(angle)], axis=2), (1, 0, 2))
     return twiddle, table.astype(ml_dtypes.bfloat16)
-
-
-def sorting(pixels, split):
-    place = np.arange(pixels) % split * (pixels // split) + np.arange(pixels) // split
-    return (place[:, None] == np.arange(pixels)[None, :]).astype(ml_dtypes.bfloat16)
 
 
 def local(sky_map, pixel_mask, noise_factor, cycle_legendre, band_power, channel_cov, test_matrix):
@@ -320,10 +343,11 @@
     blocks = modes * mode_count // (tiles * LANES)
     everyone = ("high", "low", "mode")
     hbm, vmem, bf16, f32, shape = pl.ANY, pltpu.VMEM, jnp.bfloat16, jnp.float32, jax.ShapeDtypeStruct
-    twiddle, table = transform_tables(split, pixels * mode_count)
+    fold = 2 if modes % (2 * LANES) == 0 else 1
+    twiddle, table = transform_tables(split, pixels * mode_count, fold)
 
     message = call(
-        whiten_kernel,
+        functools.partial(whiten_kernel, fold),
         shape((groups, rows + legs, LANES), bf16),
         [
             vmem((cycles, chans, pixels), bf16),
@@ -333,15 +357,14 @@
             vmem((pixels, pixels), bf16),
             vmem((cycles * chans, pixels), bf16),
             vmem((groups, rows + legs, LANES), bf16),
-            pltpu.SemaphoreType.DMA((6 + split // 2,)),
+            pltpu.SemaphoreType.DMA((5 + split // 2,)),
         ],
         56,
-        [hbm] * 5,
+        [hbm] * 4,
         jnp.transpose(sky_map, (0, 2, 1)),
         pixel_mask,
         noise_factor[:, 0],
         jnp.transpose(cycle_legendre, (0, 2, 1)),
-        jnp.asarray(sorting(pixels, split)),
         out_space=hbm,
         cost=(2 * cycles * chans * pixels * (pixels + 4 * chans), 8 * MIB),
     )
@@ -351,8 +374,8 @@
         functools.partial(modes_kernel, width, offsets),
         shape((offsets, mode_count, 2 * width, modes), bf16),
         [
-            vmem((tiles, tiles * LANES, 2 * LANES), bf16),
-            vmem((pair * rows, tiles * LANES), bf16),
+            vmem((tiles, tiles * LANES // fold, 2 * LANES), bf16),
+            vmem((fold, pair * rows, tiles * LANES // fold), bf16),
             vmem((pair * cycles * offsets, mode_count * modes), f32),
             vmem((pair * rows, 2 * LANES), f32),
             vmem((pair * rows, 2 * LANES), f32),
@@ -367,12 +390,15 @@
         jnp.asarray(table),
         message,
         out_space=hbm,
-        cost=(4 * pair * rows * (tiles * LANES) ** 2, 8 * MIB),
+        cost=(4 * pair * rows * (tiles * LANES) ** 2 // fold, 8 * MIB),
     )
     alm = alm.reshape(devices, 2 * width, modes)
     alm = lax.all_to_all(alm, everyone, 0, 0, tiled=True)
     alm = alm.reshape(devices // groups, groups, 2 * width, modes)
 
+    right = test_matrix.reshape(modes // (fold * LANES), LANES, fold, 2, columns)
+    right = jnp.transpose(right, (3, 0, 2, 1, 4)).reshape(2, modes, columns)
+    band = jnp.swapaxes(band_power.reshape(-1, LANES, fold), 1, 2).reshape(1, modes)
     share = columns // (devices)
     fold = LANES // chans
     packed = share % (8 * fold) == 0
@@ -383,9 +409,9 @@
         24,
         [vmem] * 4,
         alm,
-        jnp.transpose(band_power),
+        band,
         channel_cov,
-        jnp.transpose(test_matrix[0], (1, 0, 2)),
+        right,
     )
     if not packed:
         part = part.reshape(devices, share, chans)

time: 71.7 us -> 69.9 us (0.975)
  Pallas kernels: 13.5 us -> 11.6 us
    reshape x0 -> x2, local copies, waits for them, and re-layouts: none -> 1.9 us  [the longest x1 1.73 us: local(): test_matrix.reshape(modes // (fold * LANES), LANES, fold, 2, columns)]
    pallas_call x4, Pallas kernels: 13.5 us -> 11.6 us  [call(): pl.pallas_call(kernel, out_shape=shape, in_specs=[pl.BlockSpec(memory_spa...]
    unnamed x9 -> x8, local copies, waits for them, and re-layouts: 1.68 us -> 0.03 us
  transfers between devices with their start and end apart: 1 -> 1, of which waited for: 1 -> 1; matrix products, arithmetic and copies ran while one was open for 2% -> 3% of each run, Pallas kernels for 0% -> 0%
where the time goes in v8:
time: 69.9 us; the launch traced here: 69.6 us
  blocking collectives  41.7 us (60%)
  Pallas kernels  11.6 us (17%)
  waiting for transfers between devices  11.1 us (16%)
  starting transfers between devices  2.97 us (4%)
  local copies, waits for them, and re-layouts  2.01 us (3%)
    all_to_all x1, blocking collectives, local(): message = lax.all_to_all(message, ('low', 'mode'), 0, 0, tiled=True)  31 us
    pallas_call x4, Pallas kernels, call(): pl.pallas_call(kernel, out_shape=shape, in_specs=[pl.BlockSpec(memory_spa...  11.6 us
    all_to_all x1, waiting for transfers between devices, local(): alm = lax.all_to_all(alm, everyone, 0, 0, tiled=True)  11.1 us
    all_to_all x1, blocking collectives, local(): part = lax.all_to_all(part, everyone, 0, 0, tiled=True)  10.7 us
    all_to_all x1, starting transfers between devices, local(): alm = lax.all_to_all(alm, everyone, 0, 0, tiled=True)  2.97 us
    reshape x1, local copies, waits for them, and re-layouts, local(): test_matrix.reshape(modes // (fold * LANES), LANES, fold, 2, columns)  1.73 us
  transfers between devices with their start and end apart: 1, of which 1 were waited for; matrix products, arithmetic and copies ran while one was open for 3% of the time, Pallas kernels for 0%

profile of v8, /device:TPU:0, one launch (start us, length us, event | category | flops | bytes accessed | tf_op | source)
XLA Modules:
  0.0 69.6 jit_solution(6931573772010153849)
XLA Ops:
  0.0 4.0 %shard_map.91 = bf16[16,448,128]{2,1,0:T(8,128)(2,1)} custom-call(bf16[8,64,1024]{2,1,0:T(8,128)(2,1)} %bitcast.17, s32[8,1024]{1,0:T(8,128)} %mask_hbm.1, f32[8,64,64]{2,1,0:T(8,128)} %bitcast.18, f32[8,4,768]{2,1,0:T(4,128)} %bitcast.19), custom_call_target="tpu_custom_call" | custom-call | flops 1342177280 | bytes 8388608 | tf_op jit(solution)/shard_map/pallas_call | solution.py:302
  4.0 0.0 copy-start
  4.0 0.0 copy-start.1
  4.1 31.0 %all_to_all.15.z_ref = bf16[16,448,128]{2,1,0:T(8,128)(2,1)S(1)} all-to-all(bf16[16,448,128]{2,1,0:T(8,128)(2,1)} %shard_map.91), channel_id=1, replica_groups=mesh['high'=2,'low'=2,'mode'=8] {'low','mode'}, dimensions={0} | all-to-all | bytes 3670016 | tf_op jit(solution)/shard_map/all_to_all | solution.py:371
  35.1 0.0 copy-done
  35.1 0.0 copy-done.1
  35.1 5.6 %shard_map.92 = bf16[4,8,8,768]{3,2,1,0:T(8,128)(2,1)} custom-call(f32[2,8,1024]{2,1,0:T(8,128)S(1)} %copy-done.1, bf16[8,512,256]{2,1,0:T(8,128)(2,1)S(1)} %copy-done, bf16[16,448,128]{2,1,0:T(8,128)(2,1)S(1)} %all_to_all.15.z_ref), custom_call_target="tpu_custom_call" | custom-call | flops 1073741824 | bytes 8388608 | tf_op jit(solution)/shard_map/pallas_call | solution.py:302
  40.7 0.0 copy-start.3
  40.7 3.0 %all-to-all-start.1 = ((bf16[32,8,768]{2,1,0:T(8,128)(2,1)}), bf16[32,8,768]{2,1,0:T(8,128)(2,1)S(1)}, u32[]{:S(2)}, u32[]{:S(2)}) async-start(bf16[32,8,768]{2,1,0:T(8,128)(2,1)} %bitcast.3), calls=%async_computation.1 | async-start | bytes 786432 | tf_op jit(solution)/shard_map/all_to_all | solution.py:396
  43.7 0.0 copy-start.2
  43.7 1.7 %copy.13 = bf16[3,128,2,2,512]{4,1,2,0,3:T(8,128)(2,1)S(1)} copy(bf16[3,128,2,2,512]{4,3,2,1,0:T(2,128)(2,1)} %bitcast.15) | data formatting | bytes 3145728 | tf_op jit(solution)/shard_map/reshape | solution.py:399
  45.4 0.0 copy-done.3
  45.5 0.2 reshape.20
  45.6 0.1 copy.12
  45.7 11.1 %all-to-all-done.1 = bf16[32,8,768]{2,1,0:T(8,128)(2,1)S(1)} async-done(((bf16[32,8,768]{2,1,0:T(8,128)(2,1)}), bf16[32,8,768]{2,1,0:T(8,128)(2,1)S(1)}, u32[]{:S(2)}, u32[]{:S(2)}) %all-to-all-start.1) | async-done | bytes 393248 | tf_op jit(solution)/shard_map/all_to_all | solution.py:396
  56.8 0.0 copy-done.2
  56.8 1.3 %shard_map.93 = f32[32,8,128]{2,1,0:T(8,128)S(1)} custom-call(bf16[2,16,8,768]{3,2,1,0:T(8,128)(2,1)S(1)} %bitcast.13, f32[1,768]{1,0:T(1,128)S(1)} %bitcast.14, f32[64,64]{1,0:T(8,128)S(1)} %copy-done.2, bf16[2,768,512]{2,1,0:T(8,128)(2,1)S(1)} %bitcast.12), custom_call_target="tpu_custom_call" | custom-call | tf_op jit(solution)/shard_map/pallas_call | solution.py:302
  58.2 10.7 %all_to_all.16.part_ref = f32[32,8,128]{2,1,0:T(8,128)S(1)} all-to-all(f32[32,8,128]{2,1,0:T(8,128)S(1)} %shard_map.93), channel_id=1, replica_groups=mesh['high'=2,'low'=2,'mode'=8] {'high','low','mode'}, dimensions={0} | all-to-all | bytes 262144 | tf_op jit(solution)/shard_map/all_to_all | solution.py:418
  68.9 0.7 %shard_map.94 = f32[16,64]{1,0:T(8,128)} custom-call(f32[32,8,128]{2,1,0:T(8,128)S(1)} %all_to_all.16.part_ref), custom_call_target="tpu_custom_call" | custom-call | tf_op jit(solution)/shard_map/pallas_call | solution.py:302
  (1 shorter events, 0.0 us)
Async XLA Ops:
  4.0 31.1 %copy-start = (bf16[8,512,256]{2,1,0:T(8,128)(2,1)S(1)}, bf16[8,512,256]{2,1,0:T(8,128)(2,1)}, u32[]{:S(2)}) copy-start(bf16[8,512,256]{2,1,0:T(8,128)(2,1)} %constant.5.clone.table_hbm) | copy-start | bytes 6291460
  4.0 31.0 %copy-start.1 = (f32[2,8,1024]{2,1,0:T(8,128)S(1)}, f32[2,8,1024]{2,1,0:T(8,128)}, u32[]{:S(2)}) copy-start(f32[2,8,1024]{2,1,0:T(8,128)} %constant.4.clone.twiddle_ref) | copy-start | bytes 196612
  40.7 4.7 %copy-start.3 = (f32[768,1]{0,1:T(1,128)S(1)}, f32[768,1]{0,1:T(1,128)}, u32[]{:S(2)}) copy-start(f32[768,1]{0,1:T(1,128)} %param.13) | copy-start | bytes 9220
  40.7 16.2 %all-to-all-start.1 = ((bf16[32,8,768]{2,1,0:T(8,128)(2,1)}), bf16[32,8,768]{2,1,0:T(8,128)(2,1)S(1)}, u32[]{:S(2)}, u32[]{:S(2)}) async-start(bf16[32,8,768]{2,1,0:T(8,128)(2,1)} %bitcast.3), calls=%async_computation.1 | async-start | bytes 786432 | tf_op jit(solution)/shard_map/all_to_all | solution.py:396
  43.7 13.2 %copy-start.2 = (f32[64,64]{1,0:T(8,128)S(1)}, f32[64,64]{1,0:T(8,128)}, u32[]{:S(2)}) copy-start(f32[64,64]{1,0:T(8,128)} %cov_ref.1) | copy-start | bytes 49156

commit v9 on v8

--- a/solution.py
+++ b/solution.py
@@ -131,8 +131,8 @@
         send.wait()
 
 
-def modes_kernel(width, offsets, twiddle_ref, table_hbm, z_ref, out_hbm, *refs):
-    table, left, leg, prod_a, prod_b, x_ref, out_ref, table_sems, out_sems = refs
+def modes_kernel(width, offsets, twiddle_ref, table, z_ref, out_hbm, *refs):
+    left, leg, prod_a, prod_b, x_ref, out_ref, out_sems = refs
     tiles = table.shape[0]
     split = twiddle_ref.shape[1]
     tall = x_ref.shape[3]
@@ -146,17 +146,12 @@
     count = cycles // parts * width
     high = cycles // parts * offsets
 
-    def copy(tile):
-        return pltpu.make_async_copy(table_hbm.at[tile], table.at[tile], table_sems.at[tile])
-
     def store(step, n):
         mode_tile = n // 2 * tiles + 2 * step + n % 2
         lanes = pl.ds(pl.multiple_of(mode_tile % per * LANES, LANES), LANES)
         where = (slice(None), mode_tile // per, slice(None), lanes)
         return pltpu.make_async_copy(out_ref.at[where], out_hbm.at[where], out_sems.at[step, n])
 
-    copy(0).start()
-    copy(1).start()
     fold = left.shape[0]
     for p in range(parts):
         for q in range(sources // fold):
@@ -171,13 +166,10 @@
                     more = z_ref[p * sources + sources // 2 + q, n * count : (n + 1) * count, :].astype(jnp.float32)
                     left[0, place : place + count, lanes] = (rows + more).astype(jnp.bfloat16)
                     left[1, place : place + count, lanes] = (rows - more).astype(jnp.bfloat16)
-    for tile in range(2, tiles):
-        copy(tile).start()
 
     def product(tile, prod, kind):
         prod[...] = jnp.dot(left[kind % fold], table[tile], preferred_element_type=jnp.float32)
 
-    copy(0).wait()
     product(0, prod_a, 0)
     for p in range(parts):
         for q in range(sources):
@@ -236,12 +228,6 @@
 
     @pl.loop(0, tiles // 2)
     def _(step):
-        copy(2 * step + 1).wait()
-
-        @pl.when(2 * step + 2 < tiles)
-        def _():
-            copy(2 * step + 2).wait()
-
         product(2 * step + 1, prod_b, 1)
         use(2 * step, prod_a)
         product(jnp.minimum(2 * step + 2, tiles - 2), prod_a, 0)
@@ -374,18 +360,16 @@
         functools.partial(modes_kernel, width, offsets),
         shape((offsets, mode_count, 2 * width, modes), bf16),
         [
-            vmem((tiles, tiles * LANES // fold, 2 * LANES), bf16),
             vmem((fold, pair * rows, tiles * LANES // fold), bf16),
             vmem((pair * cycles * offsets, mode_count * modes), f32),
             vmem((pair * rows, 2 * LANES), f32),
             vmem((pair * rows, 2 * LANES), f32),
             vmem((blocks, 2, pair * cycles // group, group * width, LANES), f32),
             vmem((offsets, mode_count, 2 * width, modes), bf16),
-            pltpu.SemaphoreType.DMA((tiles,)),
             pltpu.SemaphoreType.DMA((tiles // 2, 2 * blocks)),
         ],
-        40,
-        [vmem, hbm, vmem],
+        24,
+        [vmem] * 3,
         jnp.asarray(twiddle),
         jnp.asarray(table),
         message,

time: 69.9 us -> 69.5 us (level)
  no operation moved by 1% of the time
where the time goes in v9:
time: 69.5 us; the launch traced here: 69.2 us
  blocking collectives  41.7 us (60%)
  Pallas kernels  11.3 us (16%)
  waiting for transfers between devices  11.1 us (16%)
  starting transfers between devices  2.97 us (4%)
  local copies, waits for them, and re-layouts  2.01 us (3%)
    all_to_all x1, blocking collectives, local(): message = lax.all_to_all(message, ('low', 'mode'), 0, 0, tiled=True)  31 us
    pallas_call x4, Pallas kernels, call(): pl.pallas_call(kernel, out_shape=shape, in_specs=[pl.BlockSpec(memory_spa...  11.3 us
    all_to_all x1, waiting for transfers between devices, local(): alm = lax.all_to_all(alm, everyone, 0, 0, tiled=True)  11.1 us
    all_to_all x1, blocking collectives, local(): part = lax.all_to_all(part, everyone, 0, 0, tiled=True)  10.7 us
    all_to_all x1, starting transfers between devices, local(): alm = lax.all_to_all(alm, everyone, 0, 0, tiled=True)  2.97 us
    reshape x1, local copies, waits for them, and re-layouts, local(): test_matrix.reshape(modes // (fold * LANES), LANES, fold, 2, columns)  1.73 us
  transfers between devices with their start and end apart: 1, of which 1 were waited for; matrix products, arithmetic and copies ran while one was open for 3% of the time, Pallas kernels for 0%

profile of v9, /device:TPU:0, one launch (start us, length us, event | category | flops | bytes accessed | tf_op | source)
XLA Modules:
  0.0 69.2 jit_solution(12047322431970411934)
XLA Ops:
  0.0 4.0 %shard_map.91 = bf16[16,448,128]{2,1,0:T(8,128)(2,1)} custom-call(bf16[8,64,1024]{2,1,0:T(8,128)(2,1)} %bitcast.17, s32[8,1024]{1,0:T(8,128)} %mask_hbm.1, f32[8,64,64]{2,1,0:T(8,128)} %bitcast.18, f32[8,4,768]{2,1,0:T(4,128)} %bitcast.19), custom_call_target="tpu_custom_call" | custom-call | flops 1342177280 | bytes 8388608 | tf_op jit(solution)/shard_map/pallas_call | solution.py:288
  4.0 0.0 copy-start
  4.0 0.0 copy-start.1
  4.1 31.0 %all_to_all.15.z_ref = bf16[16,448,128]{2,1,0:T(8,128)(2,1)S(1)} all-to-all(bf16[16,448,128]{2,1,0:T(8,128)(2,1)} %shard_map.91), channel_id=1, replica_groups=mesh['high'=2,'low'=2,'mode'=8] {'low','mode'}, dimensions={0} | all-to-all | bytes 3670016 | tf_op jit(solution)/shard_map/all_to_all | solution.py:357
  35.1 0.0 copy-done
  35.1 0.0 copy-done.1
  35.1 5.2 %shard_map.92 = bf16[4,8,8,768]{3,2,1,0:T(8,128)(2,1)} custom-call(f32[2,8,1024]{2,1,0:T(8,128)S(1)} %copy-done.1, bf16[8,512,256]{2,1,0:T(8,128)(2,1)S(1)} %copy-done, bf16[16,448,128]{2,1,0:T(8,128)(2,1)S(1)} %all_to_all.15.z_ref), custom_call_target="tpu_custom_call" | custom-call | flops 1073741824 | bytes 8388608 | tf_op jit(solution)/shard_map/pallas_call | solution.py:288
  40.3 0.0 copy-start.3
  40.3 3.0 %all-to-all-start.1 = ((bf16[32,8,768]{2,1,0:T(8,128)(2,1)}), bf16[32,8,768]{2,1,0:T(8,128)(2,1)S(1)}, u32[]{:S(2)}, u32[]{:S(2)}) async-start(bf16[32,8,768]{2,1,0:T(8,128)(2,1)} %bitcast.3), calls=%async_computation.1 | async-start | bytes 786432 | tf_op jit(solution)/shard_map/all_to_all | solution.py:380
  43.3 0.0 copy-start.2
  43.3 1.7 %copy.13 = bf16[3,128,2,2,512]{4,1,2,0,3:T(8,128)(2,1)S(1)} copy(bf16[3,128,2,2,512]{4,3,2,1,0:T(2,128)(2,1)} %bitcast.15) | data formatting | bytes 3145728 | tf_op jit(solution)/shard_map/reshape | solution.py:383
  45.0 0.0 copy-done.3
  45.1 0.2 reshape.20
  45.3 0.1 copy.12
  45.3 11.1 %all-to-all-done.1 = bf16[32,8,768]{2,1,0:T(8,128)(2,1)S(1)} async-done(((bf16[32,8,768]{2,1,0:T(8,128)(2,1)}), bf16[32,8,768]{2,1,0:T(8,128)(2,1)S(1)}, u32[]{:S(2)}, u32[]{:S(2)}) %all-to-all-start.1) | async-done | bytes 393248 | tf_op jit(solution)/shard_map/all_to_all | solution.py:380
  56.5 0.0 copy-done.2
  56.5 1.3 %shard_map.93 = f32[32,8,128]{2,1,0:T(8,128)S(1)} custom-call(bf16[2,16,8,768]{3,2,1,0:T(8,128)(2,1)S(1)} %bitcast.13, f32[1,768]{1,0:T(1,128)S(1)} %bitcast.14, f32[64,64]{1,0:T(8,128)S(1)} %copy-done.2, bf16[2,768,512]{2,1,0:T(8,128)(2,1)S(1)} %bitcast.12), custom_call_target="tpu_custom_call" | custom-call | tf_op jit(solution)/shard_map/pallas_call | solution.py:288
  57.8 10.7 %all_to_all.16.part_ref = f32[32,8,128]{2,1,0:T(8,128)S(1)} all-to-all(f32[32,8,128]{2,1,0:T(8,128)S(1)} %shard_map.93), channel_id=1, replica_groups=mesh['high'=2,'low'=2,'mode'=8] {'high','low','mode'}, dimensions={0} | all-to-all | bytes 262144 | tf_op jit(solution)/shard_map/all_to_all | solution.py:402
  68.5 0.7 %shard_map.94 = f32[16,64]{1,0:T(8,128)} custom-call(f32[32,8,128]{2,1,0:T(8,128)S(1)} %all_to_all.16.part_ref), custom_call_target="tpu_custom_call" | custom-call | tf_op jit(solution)/shard_map/pallas_call | solution.py:288
  (1 shorter events, 0.0 us)
Async XLA Ops:
  4.0 31.1 %copy-start = (bf16[8,512,256]{2,1,0:T(8,128)(2,1)S(1)}, bf16[8,512,256]{2,1,0:T(8,128)(2,1)}, u32[]{:S(2)}) copy-start(bf16[8,512,256]{2,1,0:T(8,128)(2,1)} %constant.5.clone.table) | copy-start | bytes 6291460
  4.0 31.0 %copy-start.1 = (f32[2,8,1024]{2,1,0:T(8,128)S(1)}, f32[2,8,1024]{2,1,0:T(8,128)}, u32[]{:S(2)}) copy-start(f32[2,8,1024]{2,1,0:T(8,128)} %constant.4.clone.twiddle_ref) | copy-start | bytes 196612
  40.3 4.7 %copy-start.3 = (f32[768,1]{0,1:T(1,128)S(1)}, f32[768,1]{0,1:T(1,128)}, u32[]{:S(2)}) copy-start(f32[768,1]{0,1:T(1,128)} %param.13) | copy-start | bytes 9220
  40.3 16.1 %all-to-all-start.1 = ((bf16[32,8,768]{2,1,0:T(8,128)(2,1)}), bf16[32,8,768]{2,1,0:T(8,128)(2,1)S(1)}, u32[]{:S(2)}, u32[]{:S(2)}) async-start(bf16[32,8,768]{2,1,0:T(8,128)(2,1)} %bitcast.3), calls=%async_computation.1 | async-start | bytes 786432 | tf_op jit(solution)/shard_map/all_to_all | solution.py:380
  43.3 13.2 %copy-start.2 = (f32[64,64]{1,0:T(8,128)S(1)}, f32[64,64]{1,0:T(8,128)}, u32[]{:S(2)}) copy-start(f32[64,64]{1,0:T(8,128)} %cov_ref.1) | copy-start | bytes 49156

commit v10 on v9

--- a/solution.py
+++ b/solution.py
@@ -135,7 +135,7 @@
     left, leg, prod_a, prod_b, x_ref, out_ref, out_sems = refs
     tiles = table.shape[0]
     split = twiddle_ref.shape[1]
-    tall = x_ref.shape[3]
+    tall = x_ref.shape[2]
     group = tall // width
     modes = out_ref.shape[3]
     sources = out_ref.shape[1]
@@ -181,7 +181,7 @@
     def use(tile, prod):
         lanes = pl.ds(pl.multiple_of(tile * LANES, LANES), LANES)
         cosine, sine = twiddle_ref[0, :, lanes], twiddle_ref[1, :, lanes]
-        cycle_of = lax.broadcasted_iota(jnp.int32, (tall, LANES), 0) // width
+        row_in = lax.broadcasted_iota(jnp.int32, (tall, LANES), 0)
         for pack in range(cycles // group):
             values = []
             for s in range(split):
@@ -189,42 +189,28 @@
                 re = prod[place : place + tall, :LANES]
                 im = prod[place : place + tall, LANES:]
                 if s == 0:
-                    values.append((re, -im))
+                    values.append((re, im))
                 else:
                     c, d = cosine[s : s + 1, :], sine[s : s + 1, :]
-                    values.append((re * c - im * d, -(re * d) - im * c))
+                    values.append((re * c + im * d, im * c - re * d))
             parts = dft(values)
             for b in range(blocks):
-                x_ref[b, 0, pack] = parts[b][0]
-                x_ref[b, 1, pack] = parts[b][1]
+                for g in range(group):
+                    shifts = ((group - g) * width % tall, (group + 1 - g) * width % tall)
+                    rows = [pltpu.roll(v, m, 0) if m else v for v, m in zip(parts[b], shifts)]
+                    x_ref[b, pack * group + g] = jnp.where(row_in < width, rows[0], rows[1])
         for b in range(blocks):
             mode_tile = b * tiles + tile
             d, n = mode_tile // per, mode_tile % per
             mode = pl.ds(pl.multiple_of(mode_tile * LANES, LANES), LANES)
+            values = [x_ref[b, r] for r in range(cycles)]
             for k in range(offsets):
-                total = [None, None]
-                for pack in range(cycles // group):
-                    row = None
-                    for g in range(group):
-                        r = pack * group + g
-                        next_row = leg[r * offsets + k : r * offsets + k + 1, mode]
-                        if g == 0:
-                            row = jnp.broadcast_to(next_row, (tall, LANES))
-                        else:
-                            row = jnp.where(cycle_of < g, row, next_row)
-                    for t in range(2):
-                        term = row * x_ref[b, t, pack]
-                        total[t] = term if pack == 0 else total[t] + term
-                step = tall // 2
-                while step >= width:
-                    total = [value + pltpu.roll(value, step, 0) for value in total]
-                    step //= 2
-                if group == 1:
-                    both = jnp.concatenate(total, axis=0)
-                else:
-                    both = jnp.where(cycle_of < 1, total[0], total[1])[: 2 * width]
+                total = None
+                for r in range(cycles):
+                    term = leg[r * offsets + k : r * offsets + k + 1, mode] * values[r]
+                    total = term if r == 0 else total + term
                 place = pl.ds(pl.multiple_of(n * LANES, LANES), LANES)
-                out_ref[k, d, :, place] = both.astype(jnp.bfloat16)
+                out_ref[k, d, :, place] = total[: 2 * width].astype(jnp.bfloat16)
 
     @pl.loop(0, tiles // 2)
     def _(step):
@@ -308,7 +294,7 @@
     twiddle = np.stack([np.cos(angle), np.sin(angle)]).astype(np.float32)
     step = np.arange(half // fold)[:, None] * modes[None, :] % half
     angle = (step * (2.0 * math.pi / half)).reshape(half // fold, half // LANES, LANES)
-    table = np.transpose(np.concatenate([np.cos(angle), np.sin(angle)], axis=2), (1, 0, 2))
+    table = np.transpose(np.concatenate([np.cos(angle), -np.sin(angle)], axis=2), (1, 0, 2))
     return twiddle, table.astype(ml_dtypes.bfloat16)
 
 
@@ -364,7 +350,7 @@
             vmem((pair * cycles * offsets, mode_count * modes), f32),
             vmem((pair * rows, 2 * LANES), f32),
             vmem((pair * rows, 2 * LANES), f32),
-            vmem((blocks, 2, pair * cycles // group, group * width, LANES), f32),
+            vmem((blocks, pair * cycles, group * width, LANES), f32),
             vmem((offsets, mode_count, 2 * width, modes), bf16),
             pltpu.SemaphoreType.DMA((tiles // 2, 2 * blocks)),
         ],

time: 69.5 us -> 69.1 us (level)
  no operation moved by 1% of the time
where the time goes in v10:
time: 69.1 us; the launch traced here: 68.8 us
  blocking collectives  41.7 us (60%)
  waiting for transfers between devices  11.1 us (16%)
  Pallas kernels  10.9 us (16%)
  starting transfers between devices  2.97 us (4%)
  local copies, waits for them, and re-layouts  2.01 us (3%)
    all_to_all x1, blocking collectives, local(): message = lax.all_to_all(message, ('low', 'mode'), 0, 0, tiled=True)  31 us
    all_to_all x1, waiting for transfers between devices, local(): alm = lax.all_to_all(alm, everyone, 0, 0, tiled=True)  11.1 us
    pallas_call x4, Pallas kernels, call(): pl.pallas_call(kernel, out_shape=shape, in_specs=[pl.BlockSpec(memory_spa...  10.9 us
    all_to_all x1, blocking collectives, local(): part = lax.all_to_all(part, everyone, 0, 0, tiled=True)  10.7 us
    all_to_all x1, starting transfers between devices, local(): alm = lax.all_to_all(alm, everyone, 0, 0, tiled=True)  2.97 us
    reshape x1, local copies, waits for them, and re-layouts, local(): test_matrix.reshape(modes // (fold * LANES), LANES, fold, 2, columns)  1.73 us
  transfers between devices with their start and end apart: 1, of which 1 were waited for; matrix products, arithmetic and copies ran while one was open for 3% of the time, Pallas kernels for 0%

profile of v10, /device:TPU:0, one launch (start us, length us, event | category | flops | bytes accessed | tf_op | source)
XLA Modules:
  0.0 68.8 jit_solution(3982004109547785542)
XLA Ops:
  0.0 4.0 %shard_map.91 = bf16[16,448,128]{2,1,0:T(8,128)(2,1)} custom-call(bf16[8,64,1024]{2,1,0:T(8,128)(2,1)} %bitcast.17, s32[8,1024]{1,0:T(8,128)} %mask_hbm.1, f32[8,64,64]{2,1,0:T(8,128)} %bitcast.18, f32[8,4,768]{2,1,0:T(4,128)} %bitcast.19), custom_call_target="tpu_custom_call" | custom-call | flops 1342177280 | bytes 8388608 | tf_op jit(solution)/shard_map/pallas_call | solution.py:274
  4.0 0.0 copy-start
  4.0 0.0 copy-start.1
  4.1 31.0 %all_to_all.15.z_ref = bf16[16,448,128]{2,1,0:T(8,128)(2,1)S(1)} all-to-all(bf16[16,448,128]{2,1,0:T(8,128)(2,1)} %shard_map.91), channel_id=1, replica_groups=mesh['high'=2,'low'=2,'mode'=8] {'low','mode'}, dimensions={0} | all-to-all | bytes 3670016 | tf_op jit(solution)/shard_map/all_to_all | solution.py:343
  35.1 0.0 copy-done
  35.1 0.0 copy-done.1
  35.1 4.8 %shard_map.92 = bf16[4,8,8,768]{3,2,1,0:T(8,128)(2,1)} custom-call(f32[2,8,1024]{2,1,0:T(8,128)S(1)} %copy-done.1, bf16[8,512,256]{2,1,0:T(8,128)(2,1)S(1)} %copy-done, bf16[16,448,128]{2,1,0:T(8,128)(2,1)S(1)} %all_to_all.15.z_ref), custom_call_target="tpu_custom_call" | custom-call | flops 1073741824 | bytes 8388608 | tf_op jit(solution)/shard_map/pallas_call | solution.py:274
  39.9 0.0 copy-start.3
  39.9 3.0 %all-to-all-start.1 = ((bf16[32,8,768]{2,1,0:T(8,128)(2,1)}), bf16[32,8,768]{2,1,0:T(8,128)(2,1)S(1)}, u32[]{:S(2)}, u32[]{:S(2)}) async-start(bf16[32,8,768]{2,1,0:T(8,128)(2,1)} %bitcast.3), calls=%async_computation.1 | async-start | bytes 786432 | tf_op jit(solution)/shard_map/all_to_all | solution.py:366
  42.9 0.0 copy-start.2
  42.9 1.7 %copy.13 = bf16[3,128,2,2,512]{4,1,2,0,3:T(8,128)(2,1)S(1)} copy(bf16[3,128,2,2,512]{4,3,2,1,0:T(2,128)(2,1)} %bitcast.15) | data formatting | bytes 3145728 | tf_op jit(solution)/shard_map/reshape | solution.py:369
  44.7 0.0 copy-done.3
  44.7 0.2 reshape.20
  44.9 0.1 copy.12
  45.0 11.1 %all-to-all-done.1 = bf16[32,8,768]{2,1,0:T(8,128)(2,1)S(1)} async-done(((bf16[32,8,768]{2,1,0:T(8,128)(2,1)}), bf16[32,8,768]{2,1,0:T(8,128)(2,1)S(1)}, u32[]{:S(2)}, u32[]{:S(2)}) %all-to-all-start.1) | async-done | bytes 393248 | tf_op jit(solution)/shard_map/all_to_all | solution.py:366
  56.1 0.0 copy-done.2
  56.1 1.3 %shard_map.93 = f32[32,8,128]{2,1,0:T(8,128)S(1)} custom-call(bf16[2,16,8,768]{3,2,1,0:T(8,128)(2,1)S(1)} %bitcast.13, f32[1,768]{1,0:T(1,128)S(1)} %bitcast.14, f32[64,64]{1,0:T(8,128)S(1)} %copy-done.2, bf16[2,768,512]{2,1,0:T(8,128)(2,1)S(1)} %bitcast.12), custom_call_target="tpu_custom_call" | custom-call | tf_op jit(solution)/shard_map/pallas_call | solution.py:274
  57.4 10.7 %all_to_all.16.part_ref = f32[32,8,128]{2,1,0:T(8,128)S(1)} all-to-all(f32[32,8,128]{2,1,0:T(8,128)S(1)} %shard_map.93), channel_id=1, replica_groups=mesh['high'=2,'low'=2,'mode'=8] {'high','low','mode'}, dimensions={0} | all-to-all | bytes 262144 | tf_op jit(solution)/shard_map/all_to_all | solution.py:388
  68.1 0.7 %shard_map.94 = f32[16,64]{1,0:T(8,128)} custom-call(f32[32,8,128]{2,1,0:T(8,128)S(1)} %all_to_all.16.part_ref), custom_call_target="tpu_custom_call" | custom-call | tf_op jit(solution)/shard_map/pallas_call | solution.py:274
  (1 shorter events, 0.0 us)
Async XLA Ops:
  4.0 31.1 %copy-start = (bf16[8,512,256]{2,1,0:T(8,128)(2,1)S(1)}, bf16[8,512,256]{2,1,0:T(8,128)(2,1)}, u32[]{:S(2)}) copy-start(bf16[8,512,256]{2,1,0:T(8,128)(2,1)} %constant.5.clone.table) | copy-start | bytes 6291460
  4.0 31.0 %copy-start.1 = (f32[2,8,1024]{2,1,0:T(8,128)S(1)}, f32[2,8,1024]{2,1,0:T(8,128)}, u32[]{:S(2)}) copy-start(f32[2,8,1024]{2,1,0:T(8,128)} %constant.4.clone.twiddle_ref) | copy-start | bytes 196612
  39.9 4.7 %copy-start.3 = (f32[768,1]{0,1:T(1,128)S(1)}, f32[768,1]{0,1:T(1,128)}, u32[]{:S(2)}) copy-start(f32[768,1]{0,1:T(1,128)} %param.13) | copy-start | bytes 9220
  39.9 16.1 %all-to-all-start.1 = ((bf16[32,8,768]{2,1,0:T(8,128)(2,1)}), bf16[32,8,768]{2,1,0:T(8,128)(2,1)S(1)}, u32[]{:S(2)}, u32[]{:S(2)}) async-start(bf16[32,8,768]{2,1,0:T(8,128)(2,1)} %bitcast.3), calls=%async_computation.1 | async-start | bytes 786432 | tf_op jit(solution)/shard_map/all_to_all | solution.py:366
  42.9 13.2 %copy-start.2 = (f32[64,64]{1,0:T(8,128)S(1)}, f32[64,64]{1,0:T(8,128)}, u32[]{:S(2)}) copy-start(f32[64,64]{1,0:T(8,128)} %cov_ref.1) | copy-start | bytes 49156

commit v11 on v10

--- a/solution.py
+++ b/solution.py
@@ -240,20 +240,12 @@
             left_ref[t, g * width : (g + 1) * width, :] = part[t * width : (t + 1) * width]
     sketch = None
     for t in range(2):
-        term = lax.dot_general(
-            test_ref[t],
-            left_ref[t].astype(jnp.bfloat16),
-            (((0,), (1,)), ((), ())),
-            preferred_element_type=jnp.float32,
-        )
+        term = jnp.dot(left_ref[t].astype(jnp.bfloat16), test_ref[t], preferred_element_type=jnp.float32)
         sketch = term if t == 0 else sketch + term
-    mixed = lax.dot_general(
-        sketch,
-        cov_ref[...],
-        (((1,), (1,)), ((), ())),
-        precision=lax.Precision.HIGHEST,
-        preferred_element_type=jnp.float32,
+    mixed = jnp.dot(
+        cov_ref[...], sketch, precision=lax.Precision.HIGHEST, preferred_element_type=jnp.float32
     )
+    mixed = jnp.transpose(mixed)
     if out_ref.ndim == 2:
         out_ref[...] = mixed
     else:

time: 69.1 us -> 68.6 us (level)
  no operation moved by 1% of the time
where the time goes in v11:
time: 68.6 us; the launch traced here: 68.3 us
  blocking collectives  41.7 us (61%)
  waiting for transfers between devices  11.1 us (16%)
  Pallas kernels  10.4 us (15%)
  starting transfers between devices  2.97 us (4%)
  local copies, waits for them, and re-layouts  2.01 us (3%)
    all_to_all x1, blocking collectives, local(): message = lax.all_to_all(message, ('low', 'mode'), 0, 0, tiled=True)  31 us
    all_to_all x1, waiting for transfers between devices, local(): alm = lax.all_to_all(alm, everyone, 0, 0, tiled=True)  11.1 us
    all_to_all x1, blocking collectives, local(): part = lax.all_to_all(part, everyone, 0, 0, tiled=True)  10.7 us
    pallas_call x4, Pallas kernels, call(): pl.pallas_call(kernel, out_shape=shape, in_specs=[pl.BlockSpec(memory_spa...  10.4 us
    all_to_all x1, starting transfers between devices, local(): alm = lax.all_to_all(alm, everyone, 0, 0, tiled=True)  2.97 us
    reshape x1, local copies, waits for them, and re-layouts, local(): test_matrix.reshape(modes // (fold * LANES), LANES, fold, 2, columns)  1.73 us
  transfers between devices with their start and end apart: 1, of which 1 were waited for; matrix products, arithmetic and copies ran while one was open for 3% of the time, Pallas kernels for 0%

profile of v11, /device:TPU:0, one launch (start us, length us, event | category | flops | bytes accessed | tf_op | source)
XLA Modules:
  0.0 68.3 jit_solution(4814187461647291181)
XLA Ops:
  0.0 4.0 %shard_map.91 = bf16[16,448,128]{2,1,0:T(8,128)(2,1)} custom-call(bf16[8,64,1024]{2,1,0:T(8,128)(2,1)} %bitcast.17, s32[8,1024]{1,0:T(8,128)} %mask_hbm.1, f32[8,64,64]{2,1,0:T(8,128)} %bitcast.18, f32[8,4,768]{2,1,0:T(4,128)} %bitcast.19), custom_call_target="tpu_custom_call" | custom-call | flops 1342177280 | bytes 8388608 | tf_op jit(solution)/shard_map/pallas_call | solution.py:266
  4.0 0.0 copy-start
  4.0 0.0 copy-start.1
  4.1 31.0 %all_to_all.15.z_ref = bf16[16,448,128]{2,1,0:T(8,128)(2,1)S(1)} all-to-all(bf16[16,448,128]{2,1,0:T(8,128)(2,1)} %shard_map.91), channel_id=1, replica_groups=mesh['high'=2,'low'=2,'mode'=8] {'low','mode'}, dimensions={0} | all-to-all | bytes 3670016 | tf_op jit(solution)/shard_map/all_to_all | solution.py:335
  35.1 0.0 copy-done
  35.1 0.0 copy-done.1
  35.1 4.8 %shard_map.92 = bf16[4,8,8,768]{3,2,1,0:T(8,128)(2,1)} custom-call(f32[2,8,1024]{2,1,0:T(8,128)S(1)} %copy-done.1, bf16[8,512,256]{2,1,0:T(8,128)(2,1)S(1)} %copy-done, bf16[16,448,128]{2,1,0:T(8,128)(2,1)S(1)} %all_to_all.15.z_ref), custom_call_target="tpu_custom_call" | custom-call | flops 1073741824 | bytes 8388608 | tf_op jit(solution)/shard_map/pallas_call | solution.py:266
  39.9 0.0 copy-start.3
  39.9 3.0 %all-to-all-start.1 = ((bf16[32,8,768]{2,1,0:T(8,128)(2,1)}), bf16[32,8,768]{2,1,0:T(8,128)(2,1)S(1)}, u32[]{:S(2)}, u32[]{:S(2)}) async-start(bf16[32,8,768]{2,1,0:T(8,128)(2,1)} %bitcast.3), calls=%async_computation.1 | async-start | bytes 786432 | tf_op jit(solution)/shard_map/all_to_all | solution.py:358
  42.9 0.0 copy-start.2
  42.9 1.7 %copy.13 = bf16[3,128,2,2,512]{4,1,2,0,3:T(8,128)(2,1)S(1)} copy(bf16[3,128,2,2,512]{4,3,2,1,0:T(2,128)(2,1)} %bitcast.15) | data formatting | bytes 3145728 | tf_op jit(solution)/shard_map/reshape | solution.py:361
  44.7 0.0 copy-done.3
  44.7 0.2 reshape.20
  44.9 0.1 copy.12
  45.0 11.1 %all-to-all-done.1 = bf16[32,8,768]{2,1,0:T(8,128)(2,1)S(1)} async-done(((bf16[32,8,768]{2,1,0:T(8,128)(2,1)}), bf16[32,8,768]{2,1,0:T(8,128)(2,1)S(1)}, u32[]{:S(2)}, u32[]{:S(2)}) %all-to-all-start.1) | async-done | bytes 393248 | tf_op jit(solution)/shard_map/all_to_all | solution.py:358
  56.1 0.0 copy-done.2
  56.1 0.8 %shard_map.93 = f32[32,8,128]{2,1,0:T(8,128)S(1)} custom-call(bf16[2,16,8,768]{3,2,1,0:T(8,128)(2,1)S(1)} %bitcast.13, f32[1,768]{1,0:T(1,128)S(1)} %bitcast.14, f32[64,64]{1,0:T(8,128)S(1)} %copy-done.2, bf16[2,768,512]{2,1,0:T(8,128)(2,1)S(1)} %bitcast.12), custom_call_target="tpu_custom_call" | custom-call | tf_op jit(solution)/shard_map/pallas_call | solution.py:266
  56.9 10.7 %all_to_all.16.part_ref = f32[32,8,128]{2,1,0:T(8,128)S(1)} all-to-all(f32[32,8,128]{2,1,0:T(8,128)S(1)} %shard_map.93), channel_id=1, replica_groups=mesh['high'=2,'low'=2,'mode'=8] {'high','low','mode'}, dimensions={0} | all-to-all | bytes 262144 | tf_op jit(solution)/shard_map/all_to_all | solution.py:380
  67.6 0.7 %shard_map.94 = f32[16,64]{1,0:T(8,128)} custom-call(f32[32,8,128]{2,1,0:T(8,128)S(1)} %all_to_all.16.part_ref), custom_call_target="tpu_custom_call" | custom-call | tf_op jit(solution)/shard_map/pallas_call | solution.py:266
  (1 shorter events, 0.0 us)
Async XLA Ops:
  4.0 31.1 %copy-start = (bf16[8,512,256]{2,1,0:T(8,128)(2,1)S(1)}, bf16[8,512,256]{2,1,0:T(8,128)(2,1)}, u32[]{:S(2)}) copy-start(bf16[8,512,256]{2,1,0:T(8,128)(2,1)} %constant.5.clone.table) | copy-start | bytes 6291460
  4.0 31.0 %copy-start.1 = (f32[2,8,1024]{2,1,0:T(8,128)S(1)}, f32[2,8,1024]{2,1,0:T(8,128)}, u32[]{:S(2)}) copy-start(f32[2,8,1024]{2,1,0:T(8,128)} %constant.4.clone.twiddle_ref) | copy-start | bytes 196612
  39.9 4.7 %copy-start.3 = (f32[768,1]{0,1:T(1,128)S(1)}, f32[768,1]{0,1:T(1,128)}, u32[]{:S(2)}) copy-start(f32[768,1]{0,1:T(1,128)} %param.13) | copy-start | bytes 9220
  39.9 16.1 %all-to-all-start.1 = ((bf16[32,8,768]{2,1,0:T(8,128)(2,1)}), bf16[32,8,768]{2,1,0:T(8,128)(2,1)S(1)}, u32[]{:S(2)}, u32[]{:S(2)}) async-start(bf16[32,8,768]{2,1,0:T(8,128)(2,1)} %bitcast.3), calls=%async_computation.1 | async-start | bytes 786432 | tf_op jit(solution)/shard_map/all_to_all | solution.py:358
  42.9 13.2 %copy-start.2 = (f32[64,64]{1,0:T(8,128)S(1)}, f32[64,64]{1,0:T(8,128)}, u32[]{:S(2)}) copy-start(f32[64,64]{1,0:T(8,128)} %cov_ref.1) | copy-start | bytes 49156

commit v12 on v11

--- a/solution.py
+++ b/solution.py
@@ -47,14 +47,14 @@
 
 
 def whiten_kernel(fold, sky_hbm, mask_hbm, factor_hbm, leg_hbm, out_hbm, *refs):
-    sky, mask, factor, leg, sort, white, stage, sems = refs
+    sky, mask, factor, leg, sort, white, stage, leg_rows, sems = refs
     cycles, chans, pixels = sky.shape
     groups = stage.shape[0]
     width = chans // groups
     group = max(1, SUBLANES // width)
     tall = group * width
     split = pixels // LANES
-    sources, targets = (factor_hbm, sky_hbm, mask_hbm, leg_hbm), (factor, sky, mask, leg)
+    sources, targets = (factor_hbm, leg_hbm, sky_hbm, mask_hbm), (factor, leg, sky, mask)
     copies = [pltpu.make_async_copy(a, b, sems.at[n]) for n, (a, b) in enumerate(zip(sources, targets))]
     for copy in copies:
         copy.start()
@@ -78,20 +78,7 @@
         high = rows.astype(jnp.bfloat16)
         low = (rows - high.astype(jnp.float32)).astype(jnp.bfloat16)
         lefts.append(jnp.concatenate([high, low], axis=1))
-    for copy in copies[1:3]:
-        copy.wait()
-    cycle_of = lax.broadcasted_iota(jnp.int32, (tall, pixels), 0) // width
-    for pack in range(cycles // group):
-        data = jnp.concatenate([sky[pack * group + g] for g in range(group)] * 2, axis=0)
-        value = jnp.dot(lefts[pack], data, preferred_element_type=jnp.float32)
-        keep = jnp.broadcast_to(mask[pack * group : pack * group + 1, :], (tall, pixels))
-        for g in range(1, group):
-            keep = jnp.where(cycle_of < g, keep, mask[pack * group + g : pack * group + g + 1, :])
-        keep = keep.astype(jnp.float32)
-        for e in range(groups):
-            place = (e * (cycles // group) + pack) * tall
-            white[place : place + tall, :] = (value[e * tall : (e + 1) * tall] * keep).astype(jnp.bfloat16)
-    copies[3].wait()
+    copies[1].wait()
     count = cycles * width
     rows = jnp.concatenate([leg[r] for r in range(cycles)], axis=0).astype(jnp.bfloat16)
     high = rows.shape[0]
@@ -106,17 +93,28 @@
         ]
         rows = jnp.concatenate(rows, axis=1).astype(jnp.bfloat16)
     for n in range(rows.shape[1] // LANES):
+        leg_rows[n * high : (n + 1) * high, :] = rows[:, n * LANES : (n + 1) * LANES]
+    sends = []
+
+    def send(source, target):
+        sends.append(pltpu.make_async_copy(source, target, sems.at[4 + len(sends)]))
+        sends[-1].start()
+
+    for e in range(groups):
+        send(leg_rows, out_hbm.at[e, split * count :])
+    for copy in copies[2:]:
+        copy.wait()
+    cycle_of = lax.broadcasted_iota(jnp.int32, (tall, pixels), 0) // width
+    for pack in range(cycles // group):
+        data = jnp.concatenate([sky[pack * group + g] for g in range(group)] * 2, axis=0)
+        value = jnp.dot(lefts[pack], data, preferred_element_type=jnp.float32)
+        keep = jnp.broadcast_to(mask[pack * group : pack * group + 1, :], (tall, pixels))
+        for g in range(1, group):
+            keep = jnp.where(cycle_of < g, keep, mask[pack * group + g : pack * group + g + 1, :])
+        keep = keep.astype(jnp.float32)
         for e in range(groups):
-            place = split * count + n * high
-            stage[e, place : place + high, :] = rows[:, n * LANES : (n + 1) * LANES]
-    sends = []
-
-    def send(first, last):
-        where = (slice(None), slice(first, last))
-        sends.append(pltpu.make_async_copy(stage.at[where], out_hbm.at[where], sems.at[4 + len(sends)]))
-        sends[-1].start()
-
-    send(split * count, stage.shape[1])
+            place = (e * (cycles // group) + pack) * tall
+            white[place : place + tall, :] = (value[e * tall : (e + 1) * tall] * keep).astype(jnp.bfloat16)
     for pair in range(split // 2):
         wide = slice(pair * 2 * LANES, (pair + 1) * 2 * LANES)
         value = jnp.dot(white[...], sort[:, wide], preferred_element_type=jnp.float32).astype(jnp.bfloat16)
@@ -126,7 +124,8 @@
                 stage[e, s * count : (s + 1) * count, :] = value[
                     e * count : (e + 1) * count, side * LANES : (side + 1) * LANES
                 ]
-        send(pair * 2 * count, (pair + 1) * 2 * count)
+        where = (slice(None), slice(pair * 2 * count, (pair + 1) * 2 * count))
+        send(stage.at[where], out_hbm.at[where])
     for send in sends:
         send.wait()
 
@@ -320,8 +319,9 @@
             vmem((cycles, offsets, modes), f32),
             vmem((pixels, pixels), bf16),
             vmem((cycles * chans, pixels), bf16),
-            vmem((groups, rows + legs, LANES), bf16),
-            pltpu.SemaphoreType.DMA((5 + split // 2,)),
+            vmem((groups, rows, LANES), bf16),
+            vmem((legs, LANES), bf16),
+            pltpu.SemaphoreType.DMA((4 + groups + split // 2,)),
         ],
         56,
         [hbm] * 4,

time: 68.6 us -> 68.6 us (level)
  no operation moved by 1% of the time
where the time goes in v12:
time: 68.6 us; the launch traced here: 68.3 us
  blocking collectives  41.7 us (61%)
  waiting for transfers between devices  11.1 us (16%)
  Pallas kernels  10.4 us (15%)
  starting transfers between devices  2.97 us (4%)
  local copies, waits for them, and re-layouts  2.01 us (3%)
    all_to_all x1, blocking collectives, local(): message = lax.all_to_all(message, ('low', 'mode'), 0, 0, tiled=True)  31 us
    all_to_all x1, waiting for transfers between devices, local(): alm = lax.all_to_all(alm, everyone, 0, 0, tiled=True)  11.1 us
    all_to_all x1, blocking collectives, local(): part = lax.all_to_all(part, everyone, 0, 0, tiled=True)  10.7 us
    pallas_call x4, Pallas kernels, call(): pl.pallas_call(kernel, out_shape=shape, in_specs=[pl.BlockSpec(memory_spa...  10.4 us
    all_to_all x1, starting transfers between devices, local(): alm = lax.all_to_all(alm, everyone, 0, 0, tiled=True)  2.97 us
    reshape x1, local copies, waits for them, and re-layouts, local(): test_matrix.reshape(modes // (fold * LANES), LANES, fold, 2, columns)  1.73 us
  transfers between devices with their start and end apart: 1, of which 1 were waited for; matrix products, arithmetic and copies ran while one was open for 3% of the time, Pallas kernels for 0%

profile of v12, /device:TPU:0, one launch (start us, length us, event | category | flops | bytes accessed | tf_op | source)
XLA Modules:
  0.0 68.3 jit_solution(12371588381166468602)
XLA Ops:
  0.0 4.0 %shard_map.91 = bf16[16,448,128]{2,1,0:T(8,128)(2,1)} custom-call(bf16[8,64,1024]{2,1,0:T(8,128)(2,1)} %bitcast.17, s32[8,1024]{1,0:T(8,128)} %mask_hbm.1, f32[8,64,64]{2,1,0:T(8,128)} %bitcast.18, f32[8,4,768]{2,1,0:T(4,128)} %bitcast.19), custom_call_target="tpu_custom_call" | custom-call | flops 1342177280 | bytes 8388608 | tf_op jit(solution)/shard_map/pallas_call | solution.py:265
  4.0 0.0 copy-start
  4.0 0.0 copy-start.1
  4.1 31.0 %all_to_all.15.z_ref = bf16[16,448,128]{2,1,0:T(8,128)(2,1)S(1)} all-to-all(bf16[16,448,128]{2,1,0:T(8,128)(2,1)} %shard_map.91), channel_id=1, replica_groups=mesh['high'=2,'low'=2,'mode'=8] {'low','mode'}, dimensions={0} | all-to-all | bytes 3670016 | tf_op jit(solution)/shard_map/all_to_all | solution.py:335
  35.1 0.0 copy-done
  35.1 0.0 copy-done.1
  35.1 4.8 %shard_map.92 = bf16[4,8,8,768]{3,2,1,0:T(8,128)(2,1)} custom-call(f32[2,8,1024]{2,1,0:T(8,128)S(1)} %copy-done.1, bf16[8,512,256]{2,1,0:T(8,128)(2,1)S(1)} %copy-done, bf16[16,448,128]{2,1,0:T(8,128)(2,1)S(1)} %all_to_all.15.z_ref), custom_call_target="tpu_custom_call" | custom-call | flops 1073741824 | bytes 8388608 | tf_op jit(solution)/shard_map/pallas_call | solution.py:265
  39.9 0.0 copy-start.3
  39.9 3.0 %all-to-all-start.1 = ((bf16[32,8,768]{2,1,0:T(8,128)(2,1)}), bf16[32,8,768]{2,1,0:T(8,128)(2,1)S(1)}, u32[]{:S(2)}, u32[]{:S(2)}) async-start(bf16[32,8,768]{2,1,0:T(8,128)(2,1)} %bitcast.3), calls=%async_computation.1 | async-start | bytes 786432 | tf_op jit(solution)/shard_map/all_to_all | solution.py:358
  42.9 0.0 copy-start.2
  42.9 1.7 %copy.13 = bf16[3,128,2,2,512]{4,1,2,0,3:T(8,128)(2,1)S(1)} copy(bf16[3,128,2,2,512]{4,3,2,1,0:T(2,128)(2,1)} %bitcast.15) | data formatting | bytes 3145728 | tf_op jit(solution)/shard_map/reshape | solution.py:361
  44.7 0.0 copy-done.3
  44.7 0.2 reshape.20
  44.9 0.1 copy.12
  44.9 11.1 %all-to-all-done.1 = bf16[32,8,768]{2,1,0:T(8,128)(2,1)S(1)} async-done(((bf16[32,8,768]{2,1,0:T(8,128)(2,1)}), bf16[32,8,768]{2,1,0:T(8,128)(2,1)S(1)}, u32[]{:S(2)}, u32[]{:S(2)}) %all-to-all-start.1) | async-done | bytes 393248 | tf_op jit(solution)/shard_map/all_to_all | solution.py:358
  56.1 0.0 copy-done.2
  56.1 0.8 %shard_map.93 = f32[32,8,128]{2,1,0:T(8,128)S(1)} custom-call(bf16[2,16,8,768]{3,2,1,0:T(8,128)(2,1)S(1)} %bitcast.13, f32[1,768]{1,0:T(1,128)S(1)} %bitcast.14, f32[64,64]{1,0:T(8,128)S(1)} %copy-done.2, bf16[2,768,512]{2,1,0:T(8,128)(2,1)S(1)} %bitcast.12), custom_call_target="tpu_custom_call" | custom-call | tf_op jit(solution)/shard_map/pallas_call | solution.py:265
  56.9 10.7 %all_to_all.16.part_ref = f32[32,8,128]{2,1,0:T(8,128)S(1)} all-to-all(f32[32,8,128]{2,1,0:T(8,128)S(1)} %shard_map.93), channel_id=1, replica_groups=mesh['high'=2,'low'=2,'mode'=8] {'high','low','mode'}, dimensions={0} | all-to-all | bytes 262144 | tf_op jit(solution)/shard_map/all_to_all | solution.py:380
  67.6 0.7 %shard_map.94 = f32[16,64]{1,0:T(8,128)} custom-call(f32[32,8,128]{2,1,0:T(8,128)S(1)} %all_to_all.16.part_ref), custom_call_target="tpu_custom_call" | custom-call | tf_op jit(solution)/shard_map/pallas_call | solution.py:265
  (1 shorter events, 0.0 us)
Async XLA Ops:
  4.0 31.0 %copy-start = (bf16[8,512,256]{2,1,0:T(8,128)(2,1)S(1)}, bf16[8,512,256]{2,1,0:T(8,128)(2,1)}, u32[]{:S(2)}) copy-start(bf16[8,512,256]{2,1,0:T(8,128)(2,1)} %constant.5.clone.table) | copy-start | bytes 6291460
  4.0 31.0 %copy-start.1 = (f32[2,8,1024]{2,1,0:T(8,128)S(1)}, f32[2,8,1024]{2,1,0:T(8,128)}, u32[]{:S(2)}) copy-start(f32[2,8,1024]{2,1,0:T(8,128)} %constant.4.clone.twiddle_ref) | copy-start | bytes 196612
  39.9 4.7 %copy-start.3 = (f32[768,1]{0,1:T(1,128)S(1)}, f32[768,1]{0,1:T(1,128)}, u32[]{:S(2)}) copy-start(f32[768,1]{0,1:T(1,128)} %param.13) | copy-start | bytes 9220
  39.9 16.2 %all-to-all-start.1 = ((bf16[32,8,768]{2,1,0:T(8,128)(2,1)}), bf16[32,8,768]{2,1,0:T(8,128)(2,1)S(1)}, u32[]{:S(2)}, u32[]{:S(2)}) async-start(bf16[32,8,768]{2,1,0:T(8,128)(2,1)} %bitcast.3), calls=%async_computation.1 | async-start | bytes 786432 | tf_op jit(solution)/shard_map/all_to_all | solution.py:358
  42.9 13.2 %copy-start.2 = (f32[64,64]{1,0:T(8,128)S(1)}, f32[64,64]{1,0:T(8,128)}, u32[]{:S(2)}) copy-start(f32[64,64]{1,0:T(8,128)} %cov_ref.1) | copy-start | bytes 49156

commit v13 on v11

--- a/solution.py
+++ b/solution.py
@@ -212,14 +212,20 @@
                 place = pl.ds(pl.multiple_of(n * LANES, LANES), LANES)
                 out_ref[k, d, :, place] = total[: 2 * width].astype(jnp.bfloat16)
 
-    @pl.loop(0, tiles // 2)
-    def _(step):
+    def both(step, last):
         product(2 * step + 1, prod_b, 1)
         use(2 * step, prod_a)
-        product(jnp.minimum(2 * step + 2, tiles - 2), prod_a, 0)
+        if not last:
+            product(2 * step + 2, prod_a, 0)
         use(2 * step + 1, prod_b)
         for n in range(2 * blocks):
             store(step, n).start()
+
+    @pl.loop(0, tiles // 2 - 1)
+    def _(step):
+        both(step, False)
+
+    both(jnp.int32(tiles // 2 - 1), True)
 
     @pl.loop(0, tiles // 2)
     def _(step):

time: 68.6 us -> 68.5 us (level)
  no operation moved by 1% of the time
where the time goes in v13:
time: 68.5 us; the launch traced here: 68.2 us
  blocking collectives  41.7 us (61%)
  waiting for transfers between devices  11.1 us (16%)
  Pallas kernels  10.3 us (15%)
  starting transfers between devices  2.97 us (4%)
  local copies, waits for them, and re-layouts  2.01 us (3%)
    all_to_all x1, blocking collectives, local(): message = lax.all_to_all(message, ('low', 'mode'), 0, 0, tiled=True)  31 us
    all_to_all x1, waiting for transfers between devices, local(): alm = lax.all_to_all(alm, everyone, 0, 0, tiled=True)  11.1 us
    all_to_all x1, blocking collectives, local(): part = lax.all_to_all(part, everyone, 0, 0, tiled=True)  10.7 us
    pallas_call x4, Pallas kernels, call(): pl.pallas_call(kernel, out_shape=shape, in_specs=[pl.BlockSpec(memory_spa...  10.3 us
    all_to_all x1, starting transfers between devices, local(): alm = lax.all_to_all(alm, everyone, 0, 0, tiled=True)  2.97 us
    reshape x1, local copies, waits for them, and re-layouts, local(): test_matrix.reshape(modes // (fold * LANES), LANES, fold, 2, columns)  1.73 us
  transfers between devices with their start and end apart: 1, of which 1 were waited for; matrix products, arithmetic and copies ran while one was open for 3% of the time, Pallas kernels for 0%

profile of v13, /device:TPU:0, one launch (start us, length us, event | category | flops | bytes accessed | tf_op | source)
XLA Modules:
  0.0 68.2 jit_solution(11153004172823242138)
XLA Ops:
  0.0 4.0 %shard_map.91 = bf16[16,448,128]{2,1,0:T(8,128)(2,1)} custom-call(bf16[8,64,1024]{2,1,0:T(8,128)(2,1)} %bitcast.17, s32[8,1024]{1,0:T(8,128)} %mask_hbm.1, f32[8,64,64]{2,1,0:T(8,128)} %bitcast.18, f32[8,4,768]{2,1,0:T(4,128)} %bitcast.19), custom_call_target="tpu_custom_call" | custom-call | flops 1342177280 | bytes 8388608 | tf_op jit(solution)/shard_map/pallas_call | solution.py:272
  4.0 0.0 copy-start
  4.0 0.0 copy-start.1
  4.1 31.0 %all_to_all.15.z_ref = bf16[16,448,128]{2,1,0:T(8,128)(2,1)S(1)} all-to-all(bf16[16,448,128]{2,1,0:T(8,128)(2,1)} %shard_map.91), channel_id=1, replica_groups=mesh['high'=2,'low'=2,'mode'=8] {'low','mode'}, dimensions={0} | all-to-all | bytes 3670016 | tf_op jit(solution)/shard_map/all_to_all | solution.py:341
  35.1 0.0 copy-done
  35.1 0.0 copy-done.1
  35.1 4.8 %shard_map.92 = bf16[4,8,8,768]{3,2,1,0:T(8,128)(2,1)} custom-call(f32[2,8,1024]{2,1,0:T(8,128)S(1)} %copy-done.1, bf16[8,512,256]{2,1,0:T(8,128)(2,1)S(1)} %copy-done, bf16[16,448,128]{2,1,0:T(8,128)(2,1)S(1)} %all_to_all.15.z_ref), custom_call_target="tpu_custom_call" | custom-call | flops 1073741824 | bytes 8388608 | tf_op jit(solution)/shard_map/pallas_call | solution.py:272
  39.8 0.0 copy-start.3
  39.9 3.0 %all-to-all-start.1 = ((bf16[32,8,768]{2,1,0:T(8,128)(2,1)}), bf16[32,8,768]{2,1,0:T(8,128)(2,1)S(1)}, u32[]{:S(2)}, u32[]{:S(2)}) async-start(bf16[32,8,768]{2,1,0:T(8,128)(2,1)} %bitcast.3), calls=%async_computation.1 | async-start | bytes 786432 | tf_op jit(solution)/shard_map/all_to_all | solution.py:364
  42.8 0.0 copy-start.2
  42.8 1.7 %copy.13 = bf16[3,128,2,2,512]{4,1,2,0,3:T(8,128)(2,1)S(1)} copy(bf16[3,128,2,2,512]{4,3,2,1,0:T(2,128)(2,1)} %bitcast.15) | data formatting | bytes 3145728 | tf_op jit(solution)/shard_map/reshape | solution.py:367
  44.6 0.0 copy-done.3
  44.6 0.2 reshape.20
  44.8 0.1 copy.12
  44.9 11.1 %all-to-all-done.1 = bf16[32,8,768]{2,1,0:T(8,128)(2,1)S(1)} async-done(((bf16[32,8,768]{2,1,0:T(8,128)(2,1)}), bf16[32,8,768]{2,1,0:T(8,128)(2,1)S(1)}, u32[]{:S(2)}, u32[]{:S(2)}) %all-to-all-start.1) | async-done | bytes 393248 | tf_op jit(solution)/shard_map/all_to_all | solution.py:364
  56.0 0.0 copy-done.2
  56.0 0.8 %shard_map.93 = f32[32,8,128]{2,1,0:T(8,128)S(1)} custom-call(bf16[2,16,8,768]{3,2,1,0:T(8,128)(2,1)S(1)} %bitcast.13, f32[1,768]{1,0:T(1,128)S(1)} %bitcast.14, f32[64,64]{1,0:T(8,128)S(1)} %copy-done.2, bf16[2,768,512]{2,1,0:T(8,128)(2,1)S(1)} %bitcast.12), custom_call_target="tpu_custom_call" | custom-call | tf_op jit(solution)/shard_map/pallas_call | solution.py:272
  56.8 10.7 %all_to_all.16.part_ref = f32[32,8,128]{2,1,0:T(8,128)S(1)} all-to-all(f32[32,8,128]{2,1,0:T(8,128)S(1)} %shard_map.93), channel_id=1, replica_groups=mesh['high'=2,'low'=2,'mode'=8] {'high','low','mode'}, dimensions={0} | all-to-all | bytes 262144 | tf_op jit(solution)/shard_map/all_to_all | solution.py:386
  67.5 0.7 %shard_map.94 = f32[16,64]{1,0:T(8,128)} custom-call(f32[32,8,128]{2,1,0:T(8,128)S(1)} %all_to_all.16.part_ref), custom_call_target="tpu_custom_call" | custom-call | tf_op jit(solution)/shard_map/pallas_call | solution.py:272
  (1 shorter events, 0.0 us)
Async XLA Ops:
  4.0 31.1 %copy-start = (bf16[8,512,256]{2,1,0:T(8,128)(2,1)S(1)}, bf16[8,512,256]{2,1,0:T(8,128)(2,1)}, u32[]{:S(2)}) copy-start(bf16[8,512,256]{2,1,0:T(8,128)(2,1)} %constant.5.clone.table) | copy-start | bytes 6291460
  4.0 31.0 %copy-start.1 = (f32[2,8,1024]{2,1,0:T(8,128)S(1)}, f32[2,8,1024]{2,1,0:T(8,128)}, u32[]{:S(2)}) copy-start(f32[2,8,1024]{2,1,0:T(8,128)} %constant.4.clone.twiddle_ref) | copy-start | bytes 196612
  39.8 4.7 %copy-start.3 = (f32[768,1]{0,1:T(1,128)S(1)}, f32[768,1]{0,1:T(1,128)}, u32[]{:S(2)}) copy-start(f32[768,1]{0,1:T(1,128)} %param.13) | copy-start | bytes 9220
  39.9 16.1 %all-to-all-start.1 = ((bf16[32,8,768]{2,1,0:T(8,128)(2,1)}), bf16[32,8,768]{2,1,0:T(8,128)(2,1)S(1)}, u32[]{:S(2)}, u32[]{:S(2)}) async-start(bf16[32,8,768]{2,1,0:T(8,128)(2,1)} %bitcast.3), calls=%async_computation.1 | async-start | bytes 786432 | tf_op jit(solution)/shard_map/all_to_all | solution.py:364
  42.8 13.2 %copy-start.2 = (f32[64,64]{1,0:T(8,128)S(1)}, f32[64,64]{1,0:T(8,128)}, u32[]{:S(2)}) copy-start(f32[64,64]{1,0:T(8,128)} %cov_ref.1) | copy-start | bytes 49156
